TPU v7x, 32 devices: a whole 2x2x4 slice. The times are simulated.
32 devices in a mesh: ga: 4 (over z), ka: 8 (over y, x, core).
Axes of the slice: x: 2, y: 2, z: 4, core: 2. Of those that a mesh axis runs over, the one named last changes fastest.
Arguments:
- amplitudes: float32 [14400, 2048], P(None, ('ka', 'ga')), may hold values from -6 to 6
- integrals: float32 [2048, 15360], P('ga', 'ka'), may hold values from -0.125 to 0.125
Outputs:
- residual: float32 [14400, 15360], P('ga', 'ka')
All inputs are finite; a program needn't handle non-finite values.
Results may differ from a plain program's by a relative error of at most 0.00007.
Values sent between devices are 32-bit elements; how exact they have to be, the bound alone decides.
No kernel may reach another device: no remote copies, remote signals or barrier semaphores. Data moves between devices by JAX's collectives and lax.ppermute only.
A program may use at most 128 MiB of HBM per device.

v0:
```python
import functools

import jax
import jax.numpy as jnp
from jax import lax
from jax.experimental import pallas as pl
from jax.experimental.pallas import tpu as pltpu
from jax.sharding import PartitionSpec as P

ROWS = 400
WIDE = 512
VMEM_BYTES = 60 * 2**20


def params():
    return pltpu.CompilerParams(vmem_limit_bytes=VMEM_BYTES)


def moved(bytes_accessed, flops=0):
    return pl.CostEstimate(
        flops=flops, bytes_accessed=bytes_accessed, transcendentals=0
    )


def chunks_of(columns, line):
    if columns == 1920 and line == 4:
        return [
            (768, 256, 256, False),
            (0, 512, 512, True),
            (1536, 384, 384, False),
            (1024, 256, 256, False),
            (512, 256, 256, True),
            (1280, 256, 256, False),
        ]
    wide = [(n, WIDE, WIDE, False) for n in range(0, columns - WIDE + 1, WIDE)]
    start = len(wide) * WIDE
    return wide + ([(start, columns - start, WIDE, False)] if start < columns else [])


def cut_kernel(t_ref, out_ref):
    groups, _, rows = out_ref.shape
    for n in range(groups):
        out_ref[n] = t_ref[:, n * rows : (n + 1) * rows]


def cut(columns, groups, half):
    depth, pairs = columns.shape
    shape = (groups, depth // 2, pairs // groups)
    return pl.pallas_call(
        cut_kernel,
        grid=(1,),
        in_specs=[pl.BlockSpec((depth // 2, pairs), lambda i: (half, 0))],
        out_specs=pl.BlockSpec(shape, lambda i: (0, 0, 0)),
        out_shape=jax.ShapeDtypeStruct(shape, jnp.float32),
        compiler_params=params(),
        cost_estimate=moved(4 * depth * pairs),
    )(columns)


def turn_kernel(t_ref, out_ref):
    out_ref[...] = t_ref[...].T


def turn(columns):
    depth, rows = columns.shape
    width = 512
    return pl.pallas_call(
        turn_kernel,
        grid=(pl.cdiv(rows, width),),
        in_specs=[pl.BlockSpec((depth, width), lambda i: (0, i))],
        out_specs=pl.BlockSpec((width, depth), lambda i: (i, 0)),
        out_shape=jax.ShapeDtypeStruct((rows, depth), jnp.float32),
        compiler_params=params(),
        cost_estimate=moved(8 * depth * rows),
    )(columns)


def split(x):
    high = x.astype(jnp.bfloat16)
    return high, (x - high.astype(jnp.float32)).astype(jnp.bfloat16)


def holder(here, n):
    away = here ^ n
    if away < 2:
        return away
    if here in (0, 3):
        return 3 if away == 2 else 5
    return 4 if away == 2 else 2


def product_kernel(line, devices, gathered, place_ref, *refs):
    out_ref, w, w_high, w_low, even_high, even_low, odd_high, odd_low, arrived = refs[-9:]
    parts, sources = refs[: 2 * devices], refs[2 * devices :]
    depth, width = w.shape
    size = depth // line
    block = depth // devices
    half = block // 2
    now = pl.program_id(0)

    @pl.when(now == 0)
    def _():
        if gathered:
            whole = pltpu.make_async_copy(sources[0], w, arrived.at[0])
            whole.start()
            whole.wait()
        else:

            def copy(source, n):
                return pltpu.make_async_copy(
                    sources[source], w.at[pl.ds(n * size, size)], arrived.at[n]
                )

            for here in range(line):

                @pl.when(place_ref[1] == here)
                def _():
                    for n in range(line):
                        copy(holder(here, n), n).start()

            for n in range(line):
                copy(0, n).wait()
        piece = half // line
        for n in range(devices):
            start = pl.multiple_of((place_ref[0] ^ n) * block, block)
            for k in range(2):
                rows = [
                    w[pl.ds(start + (2 * m + k) * piece, piece), :] for m in range(line)
                ]
                to = pl.ds((2 * n + k) * half, half)
                w_high[to, :], w_low[to, :] = split(jnp.concatenate(rows, axis=0))

    def step(next_high, next_low, t_high, t_low):
        for n, part in enumerate(parts):
            to = slice(n * half, (n + 1) * half)
            next_high[:, to], next_low[:, to] = split(part[...])
        dot = functools.partial(jnp.dot, preferred_element_type=jnp.float32)
        total = dot(t_low[...], w_high[...])
        total += dot(t_high[...], w_low[...])
        total += dot(t_high[...], w_high[...])
        out_ref[:, :width] = 0.5 * total

    @pl.when(now % 2 == 0)
    def _():
        step(even_high, even_low, odd_high, odd_low)

    @pl.when(now % 2 == 1)
    def _():
        step(odd_high, odd_low, even_high, even_low)


def product(line, place, parts, sources, out, chunk, shape):
    start, width, block, by_line = chunk
    rows, size = parts[0].shape
    depth = size * len(parts)
    tiles = pl.cdiv(rows, ROWS)
    part_spec = pl.BlockSpec((ROWS, size), lambda i, p: (jnp.minimum(i, tiles - 1), 0))
    anywhere = pl.BlockSpec(memory_space=pl.ANY)
    operands = [place, *parts, *sources]
    aliases = {}
    if out is not None:
        aliases = {len(operands): 0}
        operands.append(out)
    others = len(operands) - 1 - len(parts)
    t_half = pltpu.VMEM((ROWS, depth), jnp.bfloat16)
    w_half = pltpu.VMEM((depth, width), jnp.bfloat16)
    return pl.pallas_call(
        functools.partial(product_kernel, line, len(parts) // 2, not by_line),
        grid_spec=pltpu.PrefetchScalarGridSpec(
            num_scalar_prefetch=1,
            grid=(tiles + 1,),
            in_specs=[part_spec] * len(parts) + [anywhere] * others,
            out_specs=pl.BlockSpec(
                (ROWS, block), lambda i, p: (jnp.maximum(i - 1, 0), start // block)
            ),
            scratch_shapes=[
                pltpu.VMEM((depth, width), jnp.float32),
                w_half,
                w_half,
                t_half,
                t_half,
                t_half,
                t_half,
                pltpu.SemaphoreType.DMA((line,)),
            ],
        ),
        out_shape=jax.ShapeDtypeStruct(shape, jnp.float32),
        input_output_aliases=aliases,
        compiler_params=params(),
        cost_estimate=moved(
            4 * (rows * depth + depth * width + rows * width),
            6 * rows * depth * width,
        ),
    )(*operands)


def tie(*values):
    return lax.optimization_barrier(values)


def per_device(line, devices, amplitudes, integrals):
    columns = integrals.shape[1]
    rows = amplitudes.shape[0] // line
    chunks = chunks_of(columns, line)
    outer, inner = [(1, 0), (2, 3)], [(1, 2), (2, 1)]
    both = outer + [(0, 1), (3, 2)]

    def piece(chunk, source):
        return lax.slice_in_dim(source, chunk[0], chunk[0] + chunk[1], axis=1)

    def send(x, pairs):
        return lax.ppermute(x, "ga", pairs)

    def swap(x, mask):
        return lax.ppermute(x, "ka", [(d, d ^ mask) for d in range(devices)])

    near, far = [chunk for chunk in chunks if chunk[3]] or (None, None)
    sources = {}

    turned = []
    for half in range(2):
        blocks = cut(amplitudes.T, line, half)
        blocks = lax.all_to_all(blocks, "ga", split_axis=0, concat_axis=0, tiled=True)
        turned.append(blocks.reshape(-1, rows))
    if near:
        own = piece(near, integrals)
        turned[1], first = tie(turned[1], send(own, both))
    turned[1], integrals = tie(turned[1], integrals)
    if near:
        second = send(piece(near, integrals), inner)

    for chunk in chunks:
        if not chunk[3]:
            sources[chunk] = [lax.all_gather(piece(chunk, integrals), "ga", axis=0, tiled=True)]

    masks = [1 << bit for bit in range(1, devices.bit_length() - 1)]
    held = [{0: turn(half)} for half in turned]
    orders = (masks[::-1], masks)
    across = [{}, {}]
    for level in range(1, len(masks) + 1):
        if level == 2:
            across[0] = {n: swap(block, 1) for n, block in held[0].items()}
            across[1] = {0: swap(held[1][0], 1)}
        if level == 2 and near:
            held, across, first, second = tie(held, across, first, second)
            third, fourth = send(second, outer), send(first, inner)
        elif level > 1:
            held, across = tie(held, across)
        added = [{}, {}]
        for n in range(2, devices, 2):
            if n.bit_count() == level:
                for blocks, new, order in zip(held, added, orders):
                    last = [mask for mask in order if n & mask][-1]
                    new[n] = swap(blocks[n ^ last], last)
        held = [blocks | new for blocks, new in zip(held, added)]
    for blocks, others in zip(held, across):
        for n in sorted(blocks.keys() - others.keys()):
            others[n] = swap(blocks[n], 1)
    parts = [
        (across if n % 2 else held)[half][n - n % 2]
        for n in range(devices)
        for half in range(2)
    ]

    place = jnp.stack([lax.axis_index("ka"), lax.axis_index("ga")])
    if near:
        place, third, fourth = tie(place, third, fourth)
        sources[near] = [own, first, second, third, fourth, send(fourth, outer)]

    out = None
    for n, chunk in enumerate(chunks):
        if near and n == 1:
            out, mine = tie(out, piece(far, integrals))
            first, second = send(mine, both), send(mine, inner)
        elif near and n == 2:
            out, first, second = tie(out, first, second)
            third, fourth = send(second, outer), send(first, inner)
        elif near and n == 3:
            out, third, fourth = tie(out, third, fourth)
            sources[far] = [mine, first, second, third, fourth, send(fourth, outer)]
        out = product(line, place, parts, sources[chunk], out, chunk, (rows, columns))
    return out


def solution(mesh):
    placed = (P(None, ("ka", "ga")), P("ga", "ka"))
    return jax.shard_map(
        functools.partial(per_device, mesh.shape["ga"], mesh.shape["ka"]),
        mesh=mesh,
        in_specs=placed,
        out_specs=P("ga", "ka"),
        check_vma=False,
    )
```

profile of v0, /device:TPU:16, one launch (start us, length us, event | category | flops | bytes accessed | tf_op | source)
XLA Modules:
  0.0 614.6 jit_solution(13428561583179578338)
XLA Ops:
  6.5 3.2 shard_map.30
  9.7 5.2 all-to-all-start.1
  17.8 52.2 %collective-permute-done.2.refs_17_ = f32[512,512]{1,0:T(8,128)} collective-permute-done((f32[512,512]{1,0:T(8,128)S(1)}, f32[512,512]{1,0:T(8,128)}, u32[]{:S(2)}, u32[]{:S(2)}) %collective-permute-start.2) | collective-permute-done | bytes 1048608 | tf_op jit(solution)/shard_map/ppermute | solution.py:212
  69.9 3.4 fusion
  73.4 3.4 shard_map.28
  76.7 4.9 all-to-all-start
  83.8 5.8 shard_map.31.refs_1_
  91.1 64.0 %all-to-all-done = f32[4,32,3600]{2,1,0:T(8,128)} async-done(((f32[4,32,3600]{2,1,0:T(8,128)}), f32[4,32,3600]{2,1,0:T(8,128)}, u32[]{:S(2)}, u32[]{:S(2)}) %all-to-all-start) | async-done | bytes 1843232 | tf_op jit(solution)/shard_map/all_to_all | solution.py:223
  155.1 5.8 shard_map.29.refs_0_
  168.4 69.7 %collective-permute-done.9.refs_18_ = f32[512,512]{1,0:T(8,128)S(1)} collective-permute-done((f32[512,512]{1,0:T(8,128)S(1)}, f32[512,512]{1,0:T(8,128)S(1)}, u32[]{:S(2)}, u32[]{:S(2)}) %collective-permute-start.9) | collective-permute-done | bytes 1048608 | tf_op jit(solution)/shard_map/ppermute | solution.py:212
  239.2 3.8 collective-permute-done.4.refs_9_
  243.7 3.3 collective-permute-done.5.refs_2_
  253.5 38.9 %collective-permute-done.15.refs_13_ = f32[3600,128]{1,0:T(8,128)} collective-permute-done((f32[3600,128]{1,0:T(8,128)S(1)}, f32[3600,128]{1,0:T(8,128)}, u32[]{:S(2)}, u32[]{:S(2)}) %collective-permute-start.15) | collective-permute-done | bytes 1843232 | tf_op jit(solution)/shard_map/ppermute | solution.py:215
  293.3 15.6 %collective-permute-done.10.refs_19_ = f32[512,512]{1,0:T(8,128)S(1)} collective-permute-done((f32[512,512]{1,0:T(8,128)S(1)}, f32[512,512]{1,0:T(8,128)S(1)}, u32[]{:S(2)}, u32[]{:S(2)}) %collective-permute-start.10) | collective-permute-done | bytes 1048608 | tf_op jit(solution)/shard_map/ppermute | solution.py:212
  309.9 3.1 collective-permute-start.11
  313.7 53.8 %collective-permute-done.11.refs_20_ = f32[512,512]{1,0:T(8,128)} collective-permute-done((f32[512,512]{1,0:T(8,128)}, f32[512,512]{1,0:T(8,128)}, u32[]{:S(2)}, u32[]{:S(2)}) %collective-permute-start.11) | collective-permute-done | bytes 1048608 | tf_op jit(solution)/shard_map/ppermute | solution.py:212
  369.8 33.4 %shard_map.32.refs_22_ = f32[3600,1920]{1,0:T(8,128)} custom-call(s32[2]{0:T(128)} %pad_add_fusion.place_ref, f32[3600,128]{1,0:T(8,128)} %shard_map.29.refs_0_, f32[3600,128]{1,0:T(8,128)} %shard_map.31.refs_1_, f32[3600,128]{1,0:T(8,128)} %copy-done.5, f32[3600,128]{1,0:T(8,128)} %copy-done.4, f32[3600,128]{1,0:T(8,128)} %copy-done.2, ...), custom_call_target="tpu_custom_call" | custom-call | flops 11324620800 | bytes 35274752 | tf_op jit(solution)/shard_map/pallas_call | solution.py:167
  403.3 3.0 collective-permute-start.20
  406.4 47.3 %shard_map.33.refs_17_ = f32[3600,1920]{1,0:T(8,128)} custom-call(s32[2]{0:T(128)} %pad_add_fusion.place_ref, f32[3600,128]{1,0:T(8,128)} %shard_map.29.refs_0_, f32[3600,128]{1,0:T(8,128)} %shard_map.31.refs_1_, f32[3600,128]{1,0:T(8,128)} %copy-done.5, f32[3600,128]{1,0:T(8,128)} %copy-done.4, ...), custom_call_target="tpu_custom_call", output_to_operand_aliasing={{}: (23, {})} | custom-call | flops 22649241600 | bytes 41058304 | tf_op jit(solution)/shard_map/pallas_call | solution.py:167
  455.5 2.8 collective-permute-start.22
  458.3 46.8 %shard_map.34.refs_17_ = f32[3600,1920]{1,0:T(8,128)} custom-call(s32[2]{0:T(128)} %pad_add_fusion.place_ref, f32[3600,128]{1,0:T(8,128)} %shard_map.29.refs_0_, f32[3600,128]{1,0:T(8,128)} %shard_map.31.refs_1_, f32[3600,128]{1,0:T(8,128)} %copy-done.5, f32[3600,128]{1,0:T(8,128)} %copy-done.4, ...), custom_call_target="tpu_custom_call", output_to_operand_aliasing={{}: (18, {})} | custom-call | flops 16986931200 | bytes 38166528 | tf_op jit(solution)/shard_map/pallas_call | solution.py:167
  506.8 33.4 %shard_map.35.refs_22_ = f32[3600,1920]{1,0:T(8,128)} custom-call(s32[2]{0:T(128)} %pad_add_fusion.place_ref, f32[3600,128]{1,0:T(8,128)} %shard_map.29.refs_0_, f32[3600,128]{1,0:T(8,128)} %shard_map.31.refs_1_, f32[3600,128]{1,0:T(8,128)} %copy-done.5, f32[3600,128]{1,0:T(8,128)} %copy-done.4, ...), custom_call_target="tpu_custom_call", output_to_operand_aliasing={{}: (18, {})} | custom-call | flops 11324620800 | bytes 35274752 | tf_op jit(solution)/shard_map/pallas_call | solution.py:167
  541.1 33.3 %shard_map.36.refs_17_ = f32[3600,1920]{1,0:T(8,128)} custom-call(s32[2]{0:T(128)} %pad_add_fusion.place_ref, f32[3600,128]{1,0:T(8,128)} %shard_map.29.refs_0_, f32[3600,128]{1,0:T(8,128)} %shard_map.31.refs_1_, f32[3600,128]{1,0:T(8,128)} %copy-done.5, f32[3600,128]{1,0:T(8,128)} %copy-done.4, ...), custom_call_target="tpu_custom_call", output_to_operand_aliasing={{}: (23, {})} | custom-call | flops 11324620800 | bytes 35274752 | tf_op jit(solution)/shard_map/pallas_call | solution.py:167
  574.4 33.7 %shard_map.37 = f32[3600,1920]{1,0:T(8,128)} custom-call(s32[2]{0:T(128)} %pad_add_fusion.place_ref, f32[3600,128]{1,0:T(8,128)} %shard_map.29.refs_0_, f32[3600,128]{1,0:T(8,128)} %shard_map.31.refs_1_, f32[3600,128]{1,0:T(8,128)} %copy-done.5, f32[3600,128]{1,0:T(8,128)} %copy-done.4, f32[3600,128]{1,0:T(8,128)} %copy-done.2, ...), custom_call_target="tpu_custom_call", output_to_operand_aliasing={{}: (18, {})} | custom-call | flops 11324620800 | bytes 35274752 | tf_op jit(solution)/shard_map/pallas_call | solution.py:167
  (91 shorter events, 31.2 us)
Async XLA Ops:
  9.7 60.2 %all-to-all-start.1 = ((f32[4,32,3600]{2,1,0:T(8,128)}), f32[4,32,3600]{2,1,0:T(8,128)S(1)}, u32[]{:S(2)}, u32[]{:S(2)}) async-start(f32[4,32,3600]{2,1,0:T(8,128)} %shard_map.30), calls=%async_computation.1 | async-start | bytes 3801088 | tf_op jit(solution)/shard_map/all_to_all | solution.py:223
  14.9 354.8 %all-gather.7.cloned.1.call-start = ((), (), s32[]{:S(2)}) async-start(), calls=%async_computation.3 | async-start | bytes 2621440 | tf_op jit(solution)/shard_map/all_gather | solution.py:234
  16.2 53.7 %collective-permute-start.2 = (f32[512,512]{1,0:T(8,128)S(1)}, f32[512,512]{1,0:T(8,128)}, u32[]{:S(2)}, u32[]{:S(2)}) collective-permute-start(f32[512,512]{1,0:T(8,128)S(1)} %slice.21.refs_16_), channel_id=1, source_target_pairs={{8,0},{16,24},{0,8},{24,16},{9,1},{17,25},{1,9},{25,17},{10,2},{18... | collective-permute-start | bytes 3145736 | tf_op jit(solution)/shard_map/ppermute | solution.py:212
  76.7 78.4 %all-to-all-start = ((f32[4,32,3600]{2,1,0:T(8,128)}), f32[4,32,3600]{2,1,0:T(8,128)}, u32[]{:S(2)}, u32[]{:S(2)}) async-start(f32[4,32,3600]{2,1,0:T(8,128)} %shard_map.28), calls=%async_computation | async-start | bytes 3801088 | tf_op jit(solution)/shard_map/all_to_all | solution.py:223
  81.6 376.7 %all-gather.9.cloned.1.call-start = ((), (), s32[]{:S(2)}) async-start(), calls=%async_computation.4 | async-start | bytes 3932160 | tf_op jit(solution)/shard_map/all_gather | solution.py:234
  83.7 423.0 %all-gather.11.cloned.1.call-start = ((), (), s32[]{:S(2)}) async-start(), calls=%async_computation.5 | async-start | bytes 2621440 | tf_op jit(solution)/shard_map/all_gather | solution.py:234
  89.6 148.5 %collective-permute-start.3 = (f32[3600,128]{1,0:T(8,128)}, f32[3600,128]{1,0:T(8,128)S(1)}, u32[]{:S(2)}, u32[]{:S(2)}) collective-permute-start(f32[3600,128]{1,0:T(8,128)} %shard_map.31.refs_1_), channel_id=1, source_target_pairs={{0,2},{1,3},{2,0},{3,1},{4,6},{5,7},{6,4},{7,5},{8,10},{9,11},{10,... | collective-permute-start | bytes 5529608 | tf_op jit(solution)/shard_map/ppermute | solution.py:215
  161.0 77.7 %collective-permute-start = (f32[3600,128]{1,0:T(8,128)}, f32[3600,128]{1,0:T(8,128)S(1)}, u32[]{:S(2)}, u32[]{:S(2)}) collective-permute-start(f32[3600,128]{1,0:T(8,128)} %shard_map.29.refs_0_), channel_id=1, source_target_pairs={{0,2},{1,3},{2,0},{3,1},{4,6},{5,7},{6,4},{7,5},{8,10},{9,11},{10,... | collective-permute-start | bytes 5529608 | tf_op jit(solution)/shard_map/ppermute | solution.py:215
  162.4 76.3 %collective-permute-start.1 = (f32[3600,128]{1,0:T(8,128)}, f32[3600,128]{1,0:T(8,128)}, u32[]{:S(2)}, u32[]{:S(2)}) collective-permute-start(f32[3600,128]{1,0:T(8,128)} %shard_map.29.refs_0_), channel_id=1, source_target_pairs={{0,4},{1,5},{2,6},{3,7},{4,0},{5,1},{6,2},{7,3},{8,12},{9,13},{10,... | collective-permute-start | bytes 5529608 | tf_op jit(solution)/shard_map/ppermute | solution.py:215
  165.3 72.8 %collective-permute-start.9 = (f32[512,512]{1,0:T(8,128)S(1)}, f32[512,512]{1,0:T(8,128)S(1)}, u32[]{:S(2)}, u32[]{:S(2)}) collective-permute-start(f32[512,512]{1,0:T(8,128)S(1)} %slice.22), channel_id=1, source_target_pairs={{8,16},{16,8},{9,17},{17,9},{10,18},{18,10},{11,19},{19,11},{12,20... | collective-permute-start | bytes 3145736 | tf_op jit(solution)/shard_map/ppermute | solution.py:212
  167.8 75.2 %collective-permute-start.4 = (f32[3600,128]{1,0:T(8,128)S(1)}, f32[3600,128]{1,0:T(8,128)S(1)}, u32[]{:S(2)}, u32[]{:S(2)}) collective-permute-start(f32[3600,128]{1,0:T(8,128)S(1)} %copy-done), channel_id=1, source_target_pairs={{0,4},{1,5},{2,6},{3,7},{4,0},{5,1},{6,2},{7,3},{8,12},{9,13},{10,... | collective-permute-start | bytes 5529608 | tf_op jit(solution)/shard_map/ppermute | solution.py:215
  250.1 42.3 %collective-permute-start.15 = (f32[3600,128]{1,0:T(8,128)S(1)}, f32[3600,128]{1,0:T(8,128)}, u32[]{:S(2)}, u32[]{:S(2)}) collective-permute-start(f32[3600,128]{1,0:T(8,128)S(1)} %collective-permute-done.3.refs_5_), channel_id=1, source_target_pairs={{0,4},{1,5},{2,6},{3,7},{4,0},{5,1},{6,2},{7,3},{8,12},{9,13},{10,... | collective-permute-start | bytes 5529608 | tf_op jit(solution)/shard_map/ppermute | solution.py:215
  251.0 42.3 %collective-permute-start.14 = (f32[3600,128]{1,0:T(8,128)}, f32[3600,128]{1,0:T(8,128)}, u32[]{:S(2)}, u32[]{:S(2)}) collective-permute-start(f32[3600,128]{1,0:T(8,128)} %collective-permute-done.1.refs_8_), channel_id=1, source_target_pairs={{0,2},{1,3},{2,0},{3,1},{4,6},{5,7},{6,4},{7,5},{8,10},{9,11},{10,... | collective-permute-start | bytes 5529608 | tf_op jit(solution)/shard_map/ppermute | solution.py:215
  251.5 322.9 %all-gather.5.cloned.1.call-start = ((), (), s32[]{:S(2)}) async-start(), calls=%async_computation.2 | async-start | bytes 2621440 | tf_op jit(solution)/shard_map/all_gather | solution.py:234
  251.6 57.3 %collective-permute-start.10 = (f32[512,512]{1,0:T(8,128)S(1)}, f32[512,512]{1,0:T(8,128)S(1)}, u32[]{:S(2)}, u32[]{:S(2)}) collective-permute-start(f32[512,512]{1,0:T(8,128)S(1)} %collective-permute-done.9.refs_18_), channel_id=1, source_target_pairs={{8,0},{16,24},{9,1},{17,25},{10,2},{18,26},{11,3},{19,27},{12,4},{... | collective-permute-start | bytes 3145736 | tf_op jit(solution)/shard_map/ppermute | solution.py:212
  252.9 116.8 %collective-permute-start.12 = (f32[3600,128]{1,0:T(8,128)S(1)}, f32[3600,128]{1,0:T(8,128)}, u32[]{:S(2)}, u32[]{:S(2)}) collective-permute-start(f32[3600,128]{1,0:T(8,128)S(1)} %collective-permute-done.3.refs_5_), channel_id=1, source_target_pairs={{0,1},{1,0},{2,3},{3,2},{4,5},{5,4},{6,7},{7,6},{8,9},{9,8},{10,11... | collective-permute-start | bytes 5529608 | tf_op jit(solution)/shard_map/ppermute | solution.py:215
  253.0 116.7 %collective-permute-start.13 = (f32[3600,128]{1,0:T(8,128)}, f32[3600,128]{1,0:T(8,128)}, u32[]{:S(2)}, u32[]{:S(2)}) collective-permute-start(f32[3600,128]{1,0:T(8,128)} %copy-done.3), channel_id=1, source_target_pairs={{0,1},{1,0},{2,3},{3,2},{4,5},{5,4},{6,7},{7,6},{8,9},{9,8},{10,11... | collective-permute-start | bytes 5529608 | tf_op jit(solution)/shard_map/ppermute | solution.py:215
  292.4 77.3 %collective-permute-start.17 = (f32[3600,128]{1,0:T(8,128)}, f32[3600,128]{1,0:T(8,128)}, u32[]{:S(2)}, u32[]{:S(2)}) collective-permute-start(f32[3600,128]{1,0:T(8,128)} %collective-permute-done.15.refs_13_), channel_id=1, source_target_pairs={{0,1},{1,0},{2,3},{3,2},{4,5},{5,4},{6,7},{7,6},{8,9},{9,8},{10,11... | collective-permute-start | bytes 5529608 | tf_op jit(solution)/shard_map/ppermute | solution.py:215
  293.3 76.5 %collective-permute-start.16 = (f32[3600,128]{1,0:T(8,128)}, f32[3600,128]{1,0:T(8,128)}, u32[]{:S(2)}, u32[]{:S(2)}) collective-permute-start(f32[3600,128]{1,0:T(8,128)} %collective-permute-done.14.refs_12_), channel_id=1, source_target_pairs={{0,1},{1,0},{2,3},{3,2},{4,5},{5,4},{6,7},{7,6},{8,9},{9,8},{10,11... | collective-permute-start | bytes 5529608 | tf_op jit(solution)/shard_map/ppermute | solution.py:215
  309.9 57.5 %collective-permute-start.11 = (f32[512,512]{1,0:T(8,128)}, f32[512,512]{1,0:T(8,128)}, u32[]{:S(2)}, u32[]{:S(2)}) collective-permute-start(f32[512,512]{1,0:T(8,128)} %collective-permute-done.2.refs_17_), channel_id=1, source_target_pairs={{8,16},{16,8},{9,17},{17,9},{10,18},{18,10},{11,19},{19,11},{12,20... | collective-permute-start | bytes 3145736 | tf_op jit(solution)/shard_map/ppermute | solution.py:212
  403.2 50.5 %collective-permute-start.19 = (f32[512,256]{1,0:T(8,128)S(1)}, f32[512,256]{1,0:T(8,128)S(1)}, u32[]{:S(2)}, u32[]{:S(2)}) collective-permute-start(f32[512,256]{1,0:T(8,128)S(1)} %get-tuple-element.49.refs_16_), channel_id=1, source_target_pairs={{8,0},{16,24},{0,8},{24,16},{9,1},{17,25},{1,9},{25,17},{10,2},{18... | collective-permute-start | bytes 1572872 | tf_op jit(solution)/shard_map/ppermute | solution.py:212
  403.3 50.4 %collective-permute-start.20 = (f32[512,256]{1,0:T(8,128)S(1)}, f32[512,256]{1,0:T(8,128)S(1)}, u32[]{:S(2)}, u32[]{:S(2)}) collective-permute-start(f32[512,256]{1,0:T(8,128)S(1)} %get-tuple-element.49.refs_16_), channel_id=1, source_target_pairs={{8,16},{16,8},{9,17},{17,9},{10,18},{18,10},{11,19},{19,11},{12,20... | collective-permute-start | bytes 1572872 | tf_op jit(solution)/shard_map/ppermute | solution.py:212
  453.7 51.4 %collective-permute-start.21 = (f32[512,256]{1,0:T(8,128)S(1)}, f32[512,256]{1,0:T(8,128)S(1)}, u32[]{:S(2)}, u32[]{:S(2)}) collective-permute-start(f32[512,256]{1,0:T(8,128)S(1)} %collective-permute-done.20.refs_18_), channel_id=1, source_target_pairs={{8,0},{16,24},{9,1},{17,25},{10,2},{18,26},{11,3},{19,27},{12,4},{... | collective-permute-start | bytes 1572872 | tf_op jit(solution)/shard_map/ppermute | solution.py:212
  455.5 49.7 %collective-permute-start.22 = (f32[512,256]{1,0:T(8,128)S(1)}, f32[512,256]{1,0:T(8,128)S(1)}, u32[]{:S(2)}, u32[]{:S(2)}) collective-permute-start(f32[512,256]{1,0:T(8,128)S(1)} %collective-permute-done.19.refs_17_), channel_id=1, source_target_pairs={{8,16},{16,8},{9,17},{17,9},{10,18},{18,10},{11,19},{19,11},{12,20... | collective-permute-start | bytes 1572872 | tf_op jit(solution)/shard_map/ppermute | solution.py:212
  (24 other events, 1011.9 us)
Sparse Core Ops, SparseCore 0:
  73.5 79.1 all-gather.6
  154.3 84.9 all-gather.8
  251.6 57.7 all-gather.10
  313.8 54.4 all-gather.4
where the time goes:
time: 616 us; the launch traced here: 615 us
  waiting for transfers between devices  306 us (50%)
  Pallas kernels  246 us (40%)
  starting transfers between devices  38.2 us (6%)
  between operations  13.5 us (2%)
  local copies, waits for them, and re-layouts  10.1 us (2%)
    pallas_call x6, Pallas kernels, product(): pl.pallas_call(functools.partial(product_kernel, line, len(parts) // 2, n...  228 us
    ppermute x10, waiting for transfers between devices, send(): return lax.ppermute(x, 'ga', pairs)  191 us
    all_to_all x2, waiting for transfers between devices, per_device(): lax.all_to_all(blocks, 'ga', split_axis=0, concat_axis=0, tiled=True)  64 us
    ppermute x14, waiting for transfers between devices, swap(): return lax.ppermute(x, 'ka', [(d, d ^ mask) for d in range(devices)])  50.6 us
    ppermute x10, starting transfers between devices, send(): return lax.ppermute(x, 'ga', pairs)  19.9 us
  transfers between devices with their start and end apart: 30, of which 12 were waited for; matrix products, arithmetic and copies ran while one was open for 1% of the time, Pallas kernels for 34%

commit v1 on v0

v1 whole, which is shorter than its diff:
```python
import functools

import jax
import jax.numpy as jnp
from jax import lax
from jax.experimental import pallas as pl
from jax.experimental.pallas import tpu as pltpu
from jax.sharding import PartitionSpec as P

ROWS = 240
WIDE = 512
VMEM_BYTES = 60 * 2**20


def params():
    return pltpu.CompilerParams(vmem_limit_bytes=VMEM_BYTES)


def moved(bytes_accessed, flops=0):
    return pl.CostEstimate(
        flops=flops, bytes_accessed=bytes_accessed, transcendentals=0
    )


def chunks_of(columns):
    if columns == 1920:
        order = [(0, 1024), (1280, 640), (1024, 256)]
        return [(start, width, width) for start, width in order]
    wide = [(n, WIDE, WIDE) for n in range(0, columns - WIDE + 1, WIDE)]
    start = len(wide) * WIDE
    return wide + ([(start, columns - start, WIDE)] if start < columns else [])


def cut_kernel(t_ref, out_ref):
    groups, _, rows = out_ref.shape
    for n in range(groups):
        out_ref[n] = t_ref[:, n * rows : (n + 1) * rows]


def cut(columns, groups, half):
    depth, pairs = columns.shape
    shape = (groups, depth // 2, pairs // groups)
    return pl.pallas_call(
        cut_kernel,
        grid=(1,),
        in_specs=[pl.BlockSpec((depth // 2, pairs), lambda i: (half, 0))],
        out_specs=pl.BlockSpec(shape, lambda i: (0, 0, 0)),
        out_shape=jax.ShapeDtypeStruct(shape, jnp.float32),
        compiler_params=params(),
        cost_estimate=moved(4 * depth * pairs),
    )(columns)


def turn_kernel(t_ref, out_ref):
    out_ref[...] = t_ref[...].T


def turn(columns):
    depth, rows = columns.shape
    width = 512
    return pl.pallas_call(
        turn_kernel,
        grid=(pl.cdiv(rows, width),),
        in_specs=[pl.BlockSpec((depth, width), lambda i: (0, i))],
        out_specs=pl.BlockSpec((width, depth), lambda i: (i, 0)),
        out_shape=jax.ShapeDtypeStruct((rows, depth), jnp.float32),
        compiler_params=params(),
        cost_estimate=moved(8 * depth * rows),
    )(columns)


def split(x):
    high = x.astype(jnp.bfloat16)
    return high, (x - high.astype(jnp.float32)).astype(jnp.bfloat16)


def product_kernel(line, devices, place_ref, *refs):
    parts, w_hbm = refs[: 2 * devices], refs[2 * devices]
    out_ref, w, w_high, w_low, t_high, t_low, arrived = refs[-7:]
    depth, width = w.shape
    block = depth // devices
    half = block // 2

    @pl.when(pl.program_id(0) == 0)
    def _():
        whole = pltpu.make_async_copy(w_hbm, w, arrived)
        whole.start()
        whole.wait()
        piece = half // line
        for n in range(devices):
            start = pl.multiple_of((place_ref[0] ^ n) * block, block)
            for k in range(2):
                rows = [
                    w[pl.ds(start + (2 * m + k) * piece, piece), :] for m in range(line)
                ]
                to = pl.ds((2 * n + k) * half, half)
                w_high[to, :], w_low[to, :] = split(jnp.concatenate(rows, axis=0))

    for n, part in enumerate(parts):
        to = slice(n * half, (n + 1) * half)
        t_high[:, to], t_low[:, to] = split(part[...])
    dot = functools.partial(jnp.dot, preferred_element_type=jnp.float32)
    total = dot(t_low[...], w_high[...])
    total += dot(t_high[...], w_low[...])
    total += dot(t_high[...], w_high[...])
    out_ref[:, :width] = 0.5 * total


def product(line, place, parts, w, out, chunk, full):
    start, width, block = chunk
    rows, size = parts[0].shape
    depth = size * len(parts)
    part_spec = pl.BlockSpec((ROWS, size), lambda i, p: (i, 0))
    anywhere = pl.BlockSpec(memory_space=pl.ANY)
    operands = [place, *parts, w]
    aliases = {}
    if out is not None:
        aliases = {len(operands): 0}
        operands.append(out)
    others = len(operands) - 1 - len(parts)
    t_half = pltpu.VMEM((ROWS, depth), jnp.bfloat16)
    w_half = pltpu.VMEM((depth, width), jnp.bfloat16)
    return pl.pallas_call(
        functools.partial(product_kernel, line, len(parts) // 2),
        grid_spec=pltpu.PrefetchScalarGridSpec(
            num_scalar_prefetch=1,
            grid=(pl.cdiv(rows, ROWS),),
            in_specs=[part_spec] * len(parts) + [anywhere] * others,
            out_specs=pl.BlockSpec((ROWS, block), lambda i, p: (i, start // block)),
            scratch_shapes=[
                pltpu.VMEM((depth, width), jnp.float32),
                w_half,
                w_half,
                t_half,
                t_half,
                pltpu.SemaphoreType.DMA(()),
            ],
        ),
        out_shape=jax.ShapeDtypeStruct((rows, full), jnp.float32),
        input_output_aliases=aliases,
        compiler_params=params(),
        cost_estimate=moved(
            4 * (rows * depth + depth * width + rows * width),
            6 * rows * depth * width,
        ),
    )(*operands)


def tie(*values):
    return lax.optimization_barrier(values)


def per_device(line, devices, amplitudes, integrals):
    columns = integrals.shape[1]
    rows = amplitudes.shape[0] // line
    chunks = chunks_of(columns)

    def swap(x, mask):
        return lax.ppermute(x, "ka", [(d, d ^ mask) for d in range(devices)])

    pieces = [
        lax.slice_in_dim(integrals, start, start + width, axis=1)
        for start, width, _ in chunks
    ]
    pieces[0], amplitudes = tie(pieces[0], amplitudes)
    gathered = [lax.all_gather(x, "ga", axis=0, tiled=True) for x in pieces]

    held = []
    for half in range(2):
        blocks = cut(amplitudes.T, line, half)
        if half:
            blocks, first = tie(blocks, first)
            held.append({0: turn(first)})
        blocks = lax.all_to_all(blocks, "ga", split_axis=0, concat_axis=0, tiled=True)
        first = blocks.reshape(-1, rows)
    held.append({0: turn(first)})

    masks = [1 << bit for bit in range(1, devices.bit_length() - 1)]
    orders = (masks[::-1], masks)
    across = [{}, {}]
    for level in range(1, len(masks) + 1):
        if level == 2:
            across[0] = {n: swap(block, 1) for n, block in held[0].items()}
            across[1] = {0: swap(held[1][0], 1)}
        if level > 1:
            held, across = tie(held, across)
        added = [{}, {}]
        for n in range(2, devices, 2):
            if n.bit_count() == level:
                for blocks, new, order in zip(held, added, orders):
                    last = [mask for mask in order if n & mask][-1]
                    new[n] = swap(blocks[n ^ last], last)
        held = [blocks | new for blocks, new in zip(held, added)]
    for blocks, others in zip(held, across):
        for n in sorted(blocks.keys() - others.keys()):
            others[n] = swap(blocks[n], 1)
    parts = [
        (across if n % 2 else held)[half][n - n % 2]
        for n in range(devices)
        for half in range(2)
    ]

    place = lax.axis_index("ka").astype(jnp.int32).reshape(1)
    out = None
    for chunk, w in zip(chunks, gathered):
        out = product(line, place, parts, w, out, chunk, columns)
    return out


def solution(mesh):
    placed = (P(None, ("ka", "ga")), P("ga", "ka"))
    return jax.shard_map(
        functools.partial(per_device, mesh.shape["ga"], mesh.shape["ka"]),
        mesh=mesh,
        in_specs=placed,
        out_specs=P("ga", "ka"),
        check_vma=False,
    )
```

time: 616 us -> 433 us (0.70)
  Pallas kernels: 246 us -> 143 us
  waiting for transfers between devices: 306 us -> 241 us
  starting transfers between devices: 38.2 us -> 20.2 us
    ppermute x10 -> x0, waiting for transfers between devices: 191 us -> none  [send(): return lax.ppermute(x, 'ga', pairs)]
    pallas_call x6 -> x3, Pallas kernels: 228 us -> 124 us  [product(): pl.pallas_call(functools.partial(product_kernel, line, len(parts) // 2),...]
    all_to_all x2, waiting for transfers between devices: 64 us -> 132 us  [per_device(): lax.all_to_all(blocks, 'ga', split_axis=0, concat_axis=0, tiled=True)]
    ppermute x14, waiting for transfers between devices: 50.6 us -> 109 us  [swap(): return lax.ppermute(x, 'ka', [(d, d ^ mask) for d in range(devices)])]
    ppermute x10 -> x0, starting transfers between devices: 19.9 us -> none  [send(): return lax.ppermute(x, 'ga', pairs)]
  transfers between devices with their start and end apart: 30 -> 19, of which waited for: 12 -> 10; matrix products, arithmetic and copies ran while one was open for 1% -> 1% of each run, Pallas kernels for 34% -> 28%
where the time goes in v1:
time: 433 us; the launch traced here: 428 us
  waiting for transfers between devices  241 us (56%)
  Pallas kernels  143 us (33%)
  starting transfers between devices  20.2 us (5%)
  between operations  13.2 us (3%)
  local copies, waits for them, and re-layouts  10.2 us (2%)
    all_to_all x2, waiting for transfers between devices, per_device(): lax.all_to_all(blocks, 'ga', split_axis=0, concat_axis=0, tiled=True)  132 us
    pallas_call x3, Pallas kernels, product(): pl.pallas_call(functools.partial(product_kernel, line, len(parts) // 2),...  124 us
    ppermute x14, waiting for transfers between devices, swap(): return lax.ppermute(x, 'ka', [(d, d ^ mask) for d in range(devices)])  109 us
    all_to_all x2, starting transfers between devices, per_device(): lax.all_to_all(blocks, 'ga', split_axis=0, concat_axis=0, tiled=True)  12.1 us
    pallas_call x2, Pallas kernels, turn(): pl.pallas_call(turn_kernel, grid=(pl.cdiv(rows, width),), in_specs=[pl.Bl...  11.7 us
  transfers between devices with their start and end apart: 19, of which 10 were waited for; matrix products, arithmetic and copies ran while one was open for 1% of the time, Pallas kernels for 28%

profile of v1, /device:TPU:16, one launch (start us, length us, event | category | flops | bytes accessed | tf_op | source)
XLA Modules:
  0.0 427.6 jit_solution(3536176114529191648)
XLA Ops:
  6.5 3.2 slice.9
  9.7 3.2 shard_map.29
  13.0 5.2 %all-to-all-start = ((f32[4,32,3600]{2,1,0:T(8,128)}), f32[4,32,3600]{2,1,0:T(8,128)S(1)}, u32[]{:S(2)}, u32[]{:S(2)}) async-start(f32[4,32,3600]{2,1,0:T(8,128)} %shard_map.29), calls=%async_computation | async-start | bytes 3801088 | tf_op jit(solution)/shard_map/all_to_all | solution.py:174
  18.2 3.4 shard_map.28
  21.6 91.5 %all-to-all-done = f32[4,32,3600]{2,1,0:T(8,128)S(1)} async-done(((f32[4,32,3600]{2,1,0:T(8,128)}), f32[4,32,3600]{2,1,0:T(8,128)S(1)}, u32[]{:S(2)}, u32[]{:S(2)}) %all-to-all-start) | async-done | bytes 1843232 | tf_op jit(solution)/shard_map/all_to_all | solution.py:174
  114.4 6.9 %all-to-all-start.1 = ((f32[4,32,3600]{2,1,0:T(8,128)}), f32[4,32,3600]{2,1,0:T(8,128)S(1)}, u32[]{:S(2)}, u32[]{:S(2)}) async-start(f32[4,32,3600]{2,1,0:T(8,128)} %shard_map.28), calls=%async_computation.1 | async-start | bytes 3801088 | tf_op jit(solution)/shard_map/all_to_all | solution.py:174
  121.2 2.6 slice.11
  123.8 5.8 %shard_map.30.refs_0_ = f32[3600,128]{1,0:T(8,128)} custom-call(f32[128,3600]{1,0:T(8,128)} %bitcast.7), custom_call_target="tpu_custom_call" | custom-call | bytes 3686400 | tf_op jit(solution)/shard_map/pallas_call | solution.py:61
  129.7 1.5 collective-permute-start
  131.2 1.5 collective-permute-start.1
  132.7 30.5 %collective-permute-done.refs_4_ = f32[3600,128]{1,0:T(8,128)} collective-permute-done((f32[3600,128]{1,0:T(8,128)}, f32[3600,128]{1,0:T(8,128)}, u32[]{:S(2)}, u32[]{:S(2)}) %collective-permute-start) | collective-permute-done | bytes 1843232 | tf_op jit(solution)/shard_map/ppermute | solution.py:159
  164.4 40.6 %all-to-all-done.1 = f32[4,32,3600]{2,1,0:T(8,128)S(1)} async-done(((f32[4,32,3600]{2,1,0:T(8,128)}), f32[4,32,3600]{2,1,0:T(8,128)S(1)}, u32[]{:S(2)}, u32[]{:S(2)}) %all-to-all-start.1) | async-done | bytes 1843232 | tf_op jit(solution)/shard_map/all_to_all | solution.py:174
  206.3 5.8 %shard_map.31.refs_1_ = f32[3600,128]{1,0:T(8,128)} custom-call(f32[128,3600]{1,0:T(8,128)} %bitcast.6), custom_call_target="tpu_custom_call" | custom-call | bytes 3686400 | tf_op jit(solution)/shard_map/pallas_call | solution.py:61
  212.1 1.5 collective-permute-start.2
  213.6 1.5 collective-permute-start.3
  215.1 36.3 %collective-permute-done.2.refs_5_ = f32[3600,128]{1,0:T(8,128)S(1)} collective-permute-done((f32[3600,128]{1,0:T(8,128)}, f32[3600,128]{1,0:T(8,128)S(1)}, u32[]{:S(2)}, u32[]{:S(2)}) %collective-permute-start.2) | collective-permute-done | bytes 1843232 | tf_op jit(solution)/shard_map/ppermute | solution.py:159
  251.4 2.4 collective-permute-done.3.refs_9_
  253.8 1.5 collective-permute-start.11
  255.9 34.1 %collective-permute-done.10.refs_12_ = f32[3600,128]{1,0:T(8,128)} collective-permute-done((f32[3600,128]{1,0:T(8,128)}, f32[3600,128]{1,0:T(8,128)}, u32[]{:S(2)}, u32[]{:S(2)}) %collective-permute-start.10) | collective-permute-done | bytes 1843232 | tf_op jit(solution)/shard_map/ppermute | solution.py:159
  291.2 1.9 slice.10
  294.1 2.6 collective-permute-done.13.refs_15_
  296.7 56.8 %shard_map.32.refs_17_ = f32[3600,1920]{1,0:T(8,128)} custom-call(s32[1]{0:T(128)} %bitcast.place_ref, f32[3600,128]{1,0:T(8,128)} %shard_map.30.refs_0_, f32[3600,128]{1,0:T(8,128)} %shard_map.31.refs_1_, f32[3600,128]{1,0:T(8,128)} %collective-permute-done.4.refs_2_, f32[3600,128]{1,0:T(8,128)} %copy-done.3, f32[3600,128]{1,0:T(8,128)} %collective-permute-done.refs_4_, ...), custom_call_target="tpu_custom_call" | custom-call | flops 45298483200 | bytes 52625408 | tf_op jit(solution)/shard_map/pallas_call | solution.py:123
  353.6 44.1 %shard_map.33.refs_17_ = f32[3600,1920]{1,0:T(8,128)} custom-call(s32[1]{0:T(128)} %bitcast.place_ref, f32[3600,128]{1,0:T(8,128)} %shard_map.30.refs_0_, f32[3600,128]{1,0:T(8,128)} %shard_map.31.refs_1_, f32[3600,128]{1,0:T(8,128)} %collective-permute-done.4.refs_2_, f32[3600,128]{1,0:T(8,128)} %copy-done.3, ...), custom_call_target="tpu_custom_call", output_to_operand_aliasing={{}: (18, {})} | custom-call | flops 28311552000 | bytes 43950080 | tf_op jit(solution)/shard_map/pallas_call | solution.py:123
  397.7 23.3 %shard_map.34 = f32[3600,1920]{1,0:T(8,128)} custom-call(s32[1]{0:T(128)} %bitcast.place_ref, f32[3600,128]{1,0:T(8,128)} %shard_map.30.refs_0_, f32[3600,128]{1,0:T(8,128)} %shard_map.31.refs_1_, f32[3600,128]{1,0:T(8,128)} %collective-permute-done.4.refs_2_, f32[3600,128]{1,0:T(8,128)} %copy-done.3, ...), custom_call_target="tpu_custom_call", output_to_operand_aliasing={{}: (18, {})} | custom-call | flops 11324620800 | bytes 35274752 | tf_op jit(solution)/shard_map/pallas_call | solution.py:123
  (35 shorter events, 6.7 us)
Async XLA Ops:
  6.5 290.2 %all-gather.8.cloned.1.call-start = ((), (), s32[]{:S(2)}) async-start(), calls=%async_computation.4 | async-start | bytes 10485760 | tf_op jit(solution)/shard_map/all_gather | solution.py:166
  13.0 100.2 %all-to-all-start = ((f32[4,32,3600]{2,1,0:T(8,128)}), f32[4,32,3600]{2,1,0:T(8,128)S(1)}, u32[]{:S(2)}, u32[]{:S(2)}) async-start(f32[4,32,3600]{2,1,0:T(8,128)} %shard_map.29), calls=%async_computation | async-start | bytes 3801088 | tf_op jit(solution)/shard_map/all_to_all | solution.py:174
  113.1 1.2 copy-start.1
  114.4 90.6 %all-to-all-start.1 = ((f32[4,32,3600]{2,1,0:T(8,128)}), f32[4,32,3600]{2,1,0:T(8,128)S(1)}, u32[]{:S(2)}, u32[]{:S(2)}) async-start(f32[4,32,3600]{2,1,0:T(8,128)} %shard_map.28), calls=%async_computation.1 | async-start | bytes 3801088 | tf_op jit(solution)/shard_map/all_to_all | solution.py:174
  121.2 232.4 %all-gather.6.cloned.1.call-start = ((), (), s32[]{:S(2)}) async-start(), calls=%async_computation.3 | async-start | bytes 6553600 | tf_op jit(solution)/shard_map/all_gather | solution.py:166
  123.8 273.9 %all-gather.4.cloned.1.call-start = ((), (), s32[]{:S(2)}) async-start(), calls=%async_computation.2 | async-start | bytes 2621440 | tf_op jit(solution)/shard_map/all_gather | solution.py:166
  129.7 33.5 %collective-permute-start = (f32[3600,128]{1,0:T(8,128)}, f32[3600,128]{1,0:T(8,128)}, u32[]{:S(2)}, u32[]{:S(2)}) collective-permute-start(f32[3600,128]{1,0:T(8,128)} %shard_map.30.refs_0_), channel_id=1, source_target_pairs={{0,2},{1,3},{2,0},{3,1},{4,6},{5,7},{6,4},{7,5},{8,10},{9,11},{10,... | collective-permute-start | bytes 5529608 | tf_op jit(solution)/shard_map/ppermute | solution.py:159
  131.2 33.2 %collective-permute-start.1 = (f32[3600,128]{1,0:T(8,128)}, f32[3600,128]{1,0:T(8,128)}, u32[]{:S(2)}, u32[]{:S(2)}) collective-permute-start(f32[3600,128]{1,0:T(8,128)} %shard_map.30.refs_0_), channel_id=1, source_target_pairs={{0,4},{1,5},{2,6},{3,7},{4,0},{5,1},{6,2},{7,3},{8,12},{9,13},{10,... | collective-permute-start | bytes 5529608 | tf_op jit(solution)/shard_map/ppermute | solution.py:159
  132.7 82.4 %collective-permute-start.4 = (f32[3600,128]{1,0:T(8,128)}, f32[3600,128]{1,0:T(8,128)}, u32[]{:S(2)}, u32[]{:S(2)}) collective-permute-start(f32[3600,128]{1,0:T(8,128)} %shard_map.30.refs_0_), channel_id=1, source_target_pairs={{0,1},{1,0},{2,3},{3,2},{4,5},{5,4},{6,7},{7,6},{8,9},{9,8},{10,11... | collective-permute-start | bytes 5529608 | tf_op jit(solution)/shard_map/ppermute | solution.py:159
  163.2 52.0 %collective-permute-start.5 = (f32[3600,128]{1,0:T(8,128)}, f32[3600,128]{1,0:T(8,128)}, u32[]{:S(2)}, u32[]{:S(2)}) collective-permute-start(f32[3600,128]{1,0:T(8,128)} %collective-permute-done.refs_4_), channel_id=1, source_target_pairs={{0,1},{1,0},{2,3},{3,2},{4,5},{5,4},{6,7},{7,6},{8,9},{9,8},{10,11... | collective-permute-start | bytes 5529608 | tf_op jit(solution)/shard_map/ppermute | solution.py:159
  164.4 50.8 %collective-permute-start.6 = (f32[3600,128]{1,0:T(8,128)}, f32[3600,128]{1,0:T(8,128)}, u32[]{:S(2)}, u32[]{:S(2)}) collective-permute-start(f32[3600,128]{1,0:T(8,128)} %collective-permute-done.1.refs_8_), channel_id=1, source_target_pairs={{0,1},{1,0},{2,3},{3,2},{4,5},{5,4},{6,7},{7,6},{8,9},{9,8},{10,11... | collective-permute-start | bytes 5529608 | tf_op jit(solution)/shard_map/ppermute | solution.py:159
  204.9 1.4 copy-start
  212.1 39.3 %collective-permute-start.2 = (f32[3600,128]{1,0:T(8,128)}, f32[3600,128]{1,0:T(8,128)S(1)}, u32[]{:S(2)}, u32[]{:S(2)}) collective-permute-start(f32[3600,128]{1,0:T(8,128)} %shard_map.31.refs_1_), channel_id=1, source_target_pairs={{0,2},{1,3},{2,0},{3,1},{4,6},{5,7},{6,4},{7,5},{8,10},{9,11},{10,... | collective-permute-start | bytes 5529608 | tf_op jit(solution)/shard_map/ppermute | solution.py:159
  213.6 40.2 %collective-permute-start.3 = (f32[3600,128]{1,0:T(8,128)}, f32[3600,128]{1,0:T(8,128)}, u32[]{:S(2)}, u32[]{:S(2)}) collective-permute-start(f32[3600,128]{1,0:T(8,128)} %shard_map.31.refs_1_), channel_id=1, source_target_pairs={{0,4},{1,5},{2,6},{3,7},{4,0},{5,1},{6,2},{7,3},{8,12},{9,13},{10,... | collective-permute-start | bytes 5529608 | tf_op jit(solution)/shard_map/ppermute | solution.py:159
  215.1 38.7 %collective-permute-start.7 = (f32[3600,128]{1,0:T(8,128)}, f32[3600,128]{1,0:T(8,128)S(1)}, u32[]{:S(2)}, u32[]{:S(2)}) collective-permute-start(f32[3600,128]{1,0:T(8,128)} %shard_map.31.refs_1_), channel_id=1, source_target_pairs={{0,1},{1,0},{2,3},{3,2},{4,5},{5,4},{6,7},{7,6},{8,9},{9,8},{10,11... | collective-permute-start | bytes 5529608 | tf_op jit(solution)/shard_map/ppermute | solution.py:159
  251.4 45.3 %copy-start.2 = (f32[3600,128]{1,0:T(8,128)}, f32[3600,128]{1,0:T(8,128)S(1)}, u32[]{:S(2)}) copy-start(f32[3600,128]{1,0:T(8,128)S(1)} %collective-permute-done.2.refs_5_) | copy-start | bytes 5529604
  253.8 37.4 %copy-start.3 = (f32[3600,128]{1,0:T(8,128)}, f32[3600,128]{1,0:T(8,128)S(1)}, u32[]{:S(2)}) copy-start(f32[3600,128]{1,0:T(8,128)S(1)} %collective-permute-done.7.refs_3_) | copy-start | bytes 5529604
  253.8 36.2 %collective-permute-start.10 = (f32[3600,128]{1,0:T(8,128)}, f32[3600,128]{1,0:T(8,128)}, u32[]{:S(2)}, u32[]{:S(2)}) collective-permute-start(f32[3600,128]{1,0:T(8,128)} %collective-permute-done.1.refs_8_), channel_id=1, source_target_pairs={{0,2},{1,3},{2,0},{3,1},{4,6},{5,7},{6,4},{7,5},{8,10},{9,11},{10,... | collective-permute-start | bytes 5529608 | tf_op jit(solution)/shard_map/ppermute | solution.py:159
  253.8 37.3 %collective-permute-start.11 = (f32[3600,128]{1,0:T(8,128)S(1)}, f32[3600,128]{1,0:T(8,128)}, u32[]{:S(2)}, u32[]{:S(2)}) collective-permute-start(f32[3600,128]{1,0:T(8,128)S(1)} %collective-permute-done.2.refs_5_), channel_id=1, source_target_pairs={{0,4},{1,5},{2,6},{3,7},{4,0},{5,1},{6,2},{7,3},{8,12},{9,13},{10,... | collective-permute-start | bytes 5529608 | tf_op jit(solution)/shard_map/ppermute | solution.py:159
  255.4 37.7 %collective-permute-start.8 = (f32[3600,128]{1,0:T(8,128)S(1)}, f32[3600,128]{1,0:T(8,128)}, u32[]{:S(2)}, u32[]{:S(2)}) collective-permute-start(f32[3600,128]{1,0:T(8,128)S(1)} %collective-permute-done.2.refs_5_), channel_id=1, source_target_pairs={{0,1},{1,0},{2,3},{3,2},{4,5},{5,4},{6,7},{7,6},{8,9},{9,8},{10,11... | collective-permute-start | bytes 5529608 | tf_op jit(solution)/shard_map/ppermute | solution.py:159
  255.4 37.7 %collective-permute-start.9 = (f32[3600,128]{1,0:T(8,128)}, f32[3600,128]{1,0:T(8,128)}, u32[]{:S(2)}, u32[]{:S(2)}) collective-permute-start(f32[3600,128]{1,0:T(8,128)} %collective-permute-done.3.refs_9_), channel_id=1, source_target_pairs={{0,1},{1,0},{2,3},{3,2},{4,5},{5,4},{6,7},{7,6},{8,9},{9,8},{10,11... | collective-permute-start | bytes 5529608 | tf_op jit(solution)/shard_map/ppermute | solution.py:159
  290.0 4.1 collective-permute-start.12
  291.2 5.6 %collective-permute-start.13 = (f32[3600,128]{1,0:T(8,128)}, f32[3600,128]{1,0:T(8,128)}, u32[]{:S(2)}, u32[]{:S(2)}) collective-permute-start(f32[3600,128]{1,0:T(8,128)} %collective-permute-done.11.refs_13_), channel_id=1, source_target_pairs={{0,1},{1,0},{2,3},{3,2},{4,5},{5,4},{6,7},{7,6},{8,9},{9,8},{10,11... | collective-permute-start | bytes 5529608 | tf_op jit(solution)/shard_map/ppermute | solution.py:159
Sparse Core Ops, SparseCore 0:
  9.8 224.6 all-gather.7
  236.1 98.6 all-gather.5
  336.4 44.5 all-gather.3

commit v2 on v1

--- a/solution.py
+++ b/solution.py
@@ -74,9 +74,13 @@
     return high, (x - high.astype(jnp.float32)).astype(jnp.bfloat16)
 
 
-def product_kernel(line, devices, place_ref, *refs):
-    parts, w_hbm = refs[: 2 * devices], refs[2 * devices]
-    out_ref, w, w_high, w_low, t_high, t_low, arrived = refs[-7:]
+def product_kernel(line, devices, given, place_ref, *refs):
+    parts, w_hbm = refs[:given], refs[given]
+    if given == 2:
+        t_high, t_low = parts
+        out_ref, w, w_high, w_low, arrived = refs[-5:]
+    else:
+        out_ref, t_high, t_low, w, w_high, w_low, arrived = refs[-7:]
     depth, width = w.shape
     block = depth // devices
     half = block // 2
@@ -96,9 +100,10 @@
                 to = pl.ds((2 * n + k) * half, half)
                 w_high[to, :], w_low[to, :] = split(jnp.concatenate(rows, axis=0))
 
-    for n, part in enumerate(parts):
-        to = slice(n * half, (n + 1) * half)
-        t_high[:, to], t_low[:, to] = split(part[...])
+    if given > 2:
+        for n, part in enumerate(parts):
+            to = slice(n * half, (n + 1) * half)
+            t_high[:, to], t_low[:, to] = split(part[...])
     dot = functools.partial(jnp.dot, preferred_element_type=jnp.float32)
     total = dot(t_low[...], w_high[...])
     total += dot(t_high[...], w_low[...])
@@ -106,37 +111,38 @@
     out_ref[:, :width] = 0.5 * total
 
 
-def product(line, place, parts, w, out, chunk, full):
+def product(line, devices, place, parts, w, out, chunk, full):
     start, width, block = chunk
     rows, size = parts[0].shape
-    depth = size * len(parts)
+    given = len(parts)
+    depth = w.shape[0]
+    t_spec = pl.BlockSpec((ROWS, depth), lambda i, p: (i, 0))
     part_spec = pl.BlockSpec((ROWS, size), lambda i, p: (i, 0))
+    out_spec = pl.BlockSpec((ROWS, block), lambda i, p: (i, start // block))
+    out_shape = jax.ShapeDtypeStruct((rows, full), jnp.float32)
+    t_shape = jax.ShapeDtypeStruct((rows, depth), jnp.bfloat16)
     anywhere = pl.BlockSpec(memory_space=pl.ANY)
     operands = [place, *parts, w]
     aliases = {}
     if out is not None:
         aliases = {len(operands): 0}
         operands.append(out)
-    others = len(operands) - 1 - len(parts)
-    t_half = pltpu.VMEM((ROWS, depth), jnp.bfloat16)
     w_half = pltpu.VMEM((depth, width), jnp.bfloat16)
     return pl.pallas_call(
-        functools.partial(product_kernel, line, len(parts) // 2),
+        functools.partial(product_kernel, line, devices, given),
         grid_spec=pltpu.PrefetchScalarGridSpec(
             num_scalar_prefetch=1,
             grid=(pl.cdiv(rows, ROWS),),
-            in_specs=[part_spec] * len(parts) + [anywhere] * others,
-            out_specs=pl.BlockSpec((ROWS, block), lambda i, p: (i, start // block)),
+            in_specs=[part_spec] * given + [anywhere] * (len(operands) - 1 - given),
+            out_specs=[out_spec] + [t_spec] * (2 if given > 2 else 0),
             scratch_shapes=[
                 pltpu.VMEM((depth, width), jnp.float32),
                 w_half,
                 w_half,
-                t_half,
-                t_half,
                 pltpu.SemaphoreType.DMA(()),
             ],
         ),
-        out_shape=jax.ShapeDtypeStruct((rows, full), jnp.float32),
+        out_shape=[out_shape] + [t_shape] * (2 if given > 2 else 0),
         input_output_aliases=aliases,
         compiler_params=params(),
         cost_estimate=moved(
@@ -158,22 +164,21 @@
     def swap(x, mask):
         return lax.ppermute(x, "ka", [(d, d ^ mask) for d in range(devices)])
 
+    held = []
+    for half in range(2):
+        blocks = cut(amplitudes.T, line, half)
+        if half:
+            blocks, first, integrals = tie(blocks, first, integrals)
+            held.append({0: turn(first)})
+        blocks = lax.all_to_all(blocks, "ga", split_axis=0, concat_axis=0, tiled=True)
+        first = blocks.reshape(-1, rows)
+    held.append({0: turn(first)})
+
     pieces = [
         lax.slice_in_dim(integrals, start, start + width, axis=1)
         for start, width, _ in chunks
     ]
-    pieces[0], amplitudes = tie(pieces[0], amplitudes)
     gathered = [lax.all_gather(x, "ga", axis=0, tiled=True) for x in pieces]
-
-    held = []
-    for half in range(2):
-        blocks = cut(amplitudes.T, line, half)
-        if half:
-            blocks, first = tie(blocks, first)
-            held.append({0: turn(first)})
-        blocks = lax.all_to_all(blocks, "ga", split_axis=0, concat_axis=0, tiled=True)
-        first = blocks.reshape(-1, rows)
-    held.append({0: turn(first)})
 
     masks = [1 << bit for bit in range(1, devices.bit_length() - 1)]
     orders = (masks[::-1], masks)
@@ -203,7 +208,8 @@
     place = lax.axis_index("ka").astype(jnp.int32).reshape(1)
     out = None
     for chunk, w in zip(chunks, gathered):
-        out = product(line, place, parts, w, out, chunk, columns)
+        out, *halves = product(line, devices, place, parts, w, out, chunk, columns)
+        parts = halves or parts
     return out
 
 

time: 433 us -> 422 us (0.975)
  waiting for transfers between devices: 241 us -> 234 us
    all_to_all x2, waiting for transfers between devices: 132 us -> 80.9 us  [per_device(): lax.all_to_all(blocks, 'ga', split_axis=0, concat_axis=0, tiled=True)]
    all_gather x3, waiting for transfers between devices: 0.04 us -> 40.3 us  [per_device(): gathered = [lax.all_gather(x, 'ga', axis=0, tiled=True) for x in pieces]]
  transfers between devices with their start and end apart: 19 -> 19, of which waited for: 10 -> 12; matrix products, arithmetic and copies ran while one was open for 1% -> 1% of each run, Pallas kernels for 28% -> 28%
where the time goes in v2:
time: 422 us; the launch traced here: 418 us
  waiting for transfers between devices  234 us (55%)
  Pallas kernels  142 us (34%)
  starting transfers between devices  20.2 us (5%)
  between operations  13.2 us (3%)
  local copies, waits for them, and re-layouts  9.54 us (2%)
    pallas_call x3, Pallas kernels, product(): pl.pallas_call(functools.partial(product_kernel, line, devices, given), g...  123 us
    ppermute x14, waiting for transfers between devices, swap(): return lax.ppermute(x, 'ka', [(d, d ^ mask) for d in range(devices)])  112 us
    all_to_all x2, waiting for transfers between devices, per_device(): lax.all_to_all(blocks, 'ga', split_axis=0, concat_axis=0, tiled=True)  80.9 us
    all_gather x3, waiting for transfers between devices, per_device(): gathered = [lax.all_gather(x, 'ga', axis=0, tiled=True) for x in pieces]  40.3 us
    all_to_all x2, starting transfers between devices, per_device(): lax.all_to_all(blocks, 'ga', split_axis=0, concat_axis=0, tiled=True)  12.1 us
    pallas_call x2, Pallas kernels, turn(): pl.pallas_call(turn_kernel, grid=(pl.cdiv(rows, width),), in_specs=[pl.Bl...  11.9 us
  transfers between devices with their start and end apart: 19, of which 12 were waited for; matrix products, arithmetic and copies ran while one was open for 1% of the time, Pallas kernels for 28%

profile of v2, /device:TPU:16, one launch (start us, length us, event | category | flops | bytes accessed | tf_op | source)
XLA Modules:
  0.0 418.0 jit_solution(6505515110852764198)
XLA Ops:
  6.5 3.2 shard_map.29
  9.7 5.2 %all-to-all-start = ((f32[4,32,3600]{2,1,0:T(8,128)}), f32[4,32,3600]{2,1,0:T(8,128)S(1)}, u32[]{:S(2)}, u32[]{:S(2)}) async-start(f32[4,32,3600]{2,1,0:T(8,128)} %shard_map.29), calls=%async_computation | async-start | bytes 3801088 | tf_op jit(solution)/shard_map/all_to_all | solution.py:173
  14.9 3.2 shard_map.28
  18.1 37.5 %all-to-all-done = f32[4,32,3600]{2,1,0:T(8,128)S(1)} async-done(((f32[4,32,3600]{2,1,0:T(8,128)}), f32[4,32,3600]{2,1,0:T(8,128)S(1)}, u32[]{:S(2)}, u32[]{:S(2)}) %all-to-all-start) | async-done | bytes 1843232 | tf_op jit(solution)/shard_map/all_to_all | solution.py:173
  55.6 3.8 slice.9
  59.5 6.8 %all-to-all-start.1 = ((f32[4,32,3600]{2,1,0:T(8,128)}), f32[4,32,3600]{2,1,0:T(8,128)S(1)}, u32[]{:S(2)}, u32[]{:S(2)}) async-start(f32[4,32,3600]{2,1,0:T(8,128)} %shard_map.28), calls=%async_computation.1 | async-start | bytes 3801088 | tf_op jit(solution)/shard_map/all_to_all | solution.py:173
  66.4 2.5 slice.11
  69.0 6.0 %shard_map.30.refs_0_ = f32[3600,128]{1,0:T(8,128)} custom-call(f32[128,3600]{1,0:T(8,128)} %bitcast.7), custom_call_target="tpu_custom_call" | custom-call | bytes 3686400 | tf_op jit(solution)/shard_map/pallas_call | solution.py:61
  76.5 1.5 collective-permute-start.1
  78.0 38.2 %collective-permute-done.refs_4_ = f32[3600,128]{1,0:T(8,128)} collective-permute-done((f32[3600,128]{1,0:T(8,128)}, f32[3600,128]{1,0:T(8,128)}, u32[]{:S(2)}, u32[]{:S(2)}) %collective-permute-start) | collective-permute-done | bytes 1843232 | tf_op jit(solution)/shard_map/ppermute | solution.py:165
  117.4 43.4 %all-to-all-done.1 = f32[4,32,3600]{2,1,0:T(8,128)S(1)} async-done(((f32[4,32,3600]{2,1,0:T(8,128)}), f32[4,32,3600]{2,1,0:T(8,128)S(1)}, u32[]{:S(2)}, u32[]{:S(2)}) %all-to-all-start.1) | async-done | bytes 1843232 | tf_op jit(solution)/shard_map/all_to_all | solution.py:173
  162.1 5.8 %shard_map.31.refs_1_ = f32[3600,128]{1,0:T(8,128)} custom-call(f32[128,3600]{1,0:T(8,128)} %bitcast.6), custom_call_target="tpu_custom_call" | custom-call | bytes 3686400 | tf_op jit(solution)/shard_map/pallas_call | solution.py:61
  169.4 1.5 collective-permute-start.3
  171.0 36.3 %collective-permute-done.2.refs_5_ = f32[3600,128]{1,0:T(8,128)S(1)} collective-permute-done((f32[3600,128]{1,0:T(8,128)}, f32[3600,128]{1,0:T(8,128)S(1)}, u32[]{:S(2)}, u32[]{:S(2)}) %collective-permute-start.2) | collective-permute-done | bytes 1843232 | tf_op jit(solution)/shard_map/ppermute | solution.py:165
  207.2 2.4 collective-permute-done.3.refs_9_
  209.7 1.5 collective-permute-start.11
  211.7 29.4 %collective-permute-done.10.refs_12_ = f32[3600,128]{1,0:T(8,128)} collective-permute-done((f32[3600,128]{1,0:T(8,128)}, f32[3600,128]{1,0:T(8,128)}, u32[]{:S(2)}, u32[]{:S(2)}) %collective-permute-start.10) | collective-permute-done | bytes 1843232 | tf_op jit(solution)/shard_map/ppermute | solution.py:165
  242.3 1.9 slice.10
  245.2 2.6 collective-permute-done.13.refs_15_
  247.9 57.0 %shard_map.32 = (f32[3600,1920]{1,0:T(8,128)}, bf16[3600,2048]{1,0:T(8,128)(2,1)}, bf16[3600,2048]{1,0:T(8,128)(2,1)}) custom-call(s32[1]{0:T(128)} %bitcast.place_ref, f32[3600,128]{1,0:T(8,128)} %shard_map.30.refs_0_, f32[3600,128]{1,0:T(8,128)} %shard_map.31.refs_1_, f32[3600,128]{1,0:T(8,128)} %collective-permute-done.4.refs_2_, f32[3600,128]{1,0:T(8,128)} %copy-done.3, ...), custom_call_target="tpu_custom_call" | custom-call | flops 45298483200 | bytes 52625408 | tf_op jit(solution)/shard_map/pallas_call | solution.py:131
  304.9 37.1 %all-gather.8.cloned.1.call-done.refs_2_ = f32[2048,640]{1,0:T(8,128)} async-done(((f32[512,640]{1,0:T(8,128)}), f32[2048,640]{1,0:T(8,128)}) %all-gather.8.cloned.1.call-update) | async-done | bytes 5242896 | tf_op jit(solution)/shard_map/all_gather | solution.py:181
  342.0 43.0 %shard_map.33.refs_3_ = f32[3600,1920]{1,0:T(8,128)} custom-call(s32[1]{0:T(128)} %bitcast.place_ref, bf16[3600,2048]{1,0:T(8,128)(2,1)} %get-tuple-element.34.refs_0_, bf16[3600,2048]{1,0:T(8,128)(2,1)} %get-tuple-element.35.refs_1_, f32[2048,640]{1,0:T(8,128)} %all-gather.8.cloned.1.call-done.refs_2_, ...), custom_call_target="tpu_custom_call", output_to_operand_aliasing={{}: (4, {})} | custom-call | flops 28311552000 | bytes 43950080 | tf_op jit(solution)/shard_map/pallas_call | solution.py:131
  385.1 3.1 all-gather.6.cloned.1.call-done.refs_2_
  388.2 23.2 %shard_map.34 = f32[3600,1920]{1,0:T(8,128)} custom-call(s32[1]{0:T(128)} %bitcast.place_ref, bf16[3600,2048]{1,0:T(8,128)(2,1)} %get-tuple-element.34.refs_0_, bf16[3600,2048]{1,0:T(8,128)(2,1)} %get-tuple-element.35.refs_1_, f32[2048,256]{1,0:T(8,128)} %all-gather.6.cloned.1.call-done.refs_2_, ...), custom_call_target="tpu_custom_call", output_to_operand_aliasing={{}: (4, {})} | custom-call | flops 11324620800 | bytes 35274752 | tf_op jit(solution)/shard_map/pallas_call | solution.py:131
  (35 shorter events, 8.4 us)
Async XLA Ops:
  9.7 45.9 %all-to-all-start = ((f32[4,32,3600]{2,1,0:T(8,128)}), f32[4,32,3600]{2,1,0:T(8,128)S(1)}, u32[]{:S(2)}, u32[]{:S(2)}) async-start(f32[4,32,3600]{2,1,0:T(8,128)} %shard_map.29), calls=%async_computation | async-start | bytes 3801088 | tf_op jit(solution)/shard_map/all_to_all | solution.py:173
  14.9 232.9 %all-gather.4.cloned.1.call-start = ((), (), s32[]{:S(2)}) async-start(), calls=%async_computation.2 | async-start | bytes 10485760 | tf_op jit(solution)/shard_map/all_gather | solution.py:181
  55.6 3.8 copy-start.1
  59.5 101.3 %all-to-all-start.1 = ((f32[4,32,3600]{2,1,0:T(8,128)}), f32[4,32,3600]{2,1,0:T(8,128)S(1)}, u32[]{:S(2)}, u32[]{:S(2)}) async-start(f32[4,32,3600]{2,1,0:T(8,128)} %shard_map.28), calls=%async_computation.1 | async-start | bytes 3801088 | tf_op jit(solution)/shard_map/all_to_all | solution.py:173
  66.4 275.7 %all-gather.8.cloned.1.call-start = ((), (), s32[]{:S(2)}) async-start(), calls=%async_computation.4 | async-start | bytes 6553600 | tf_op jit(solution)/shard_map/all_gather | solution.py:181
  68.9 319.3 %all-gather.6.cloned.1.call-start = ((), (), s32[]{:S(2)}) async-start(), calls=%async_computation.3 | async-start | bytes 2621440 | tf_op jit(solution)/shard_map/all_gather | solution.py:181
  75.0 41.2 %collective-permute-start = (f32[3600,128]{1,0:T(8,128)}, f32[3600,128]{1,0:T(8,128)}, u32[]{:S(2)}, u32[]{:S(2)}) collective-permute-start(f32[3600,128]{1,0:T(8,128)} %shard_map.30.refs_0_), channel_id=1, source_target_pairs={{0,2},{1,3},{2,0},{3,1},{4,6},{5,7},{6,4},{7,5},{8,10},{9,11},{10,... | collective-permute-start | bytes 5529608 | tf_op jit(solution)/shard_map/ppermute | solution.py:165
  76.5 40.9 %collective-permute-start.1 = (f32[3600,128]{1,0:T(8,128)}, f32[3600,128]{1,0:T(8,128)}, u32[]{:S(2)}, u32[]{:S(2)}) collective-permute-start(f32[3600,128]{1,0:T(8,128)} %shard_map.30.refs_0_), channel_id=1, source_target_pairs={{0,4},{1,5},{2,6},{3,7},{4,0},{5,1},{6,2},{7,3},{8,12},{9,13},{10,... | collective-permute-start | bytes 5529608 | tf_op jit(solution)/shard_map/ppermute | solution.py:165
  78.0 93.0 %collective-permute-start.4 = (f32[3600,128]{1,0:T(8,128)}, f32[3600,128]{1,0:T(8,128)}, u32[]{:S(2)}, u32[]{:S(2)}) collective-permute-start(f32[3600,128]{1,0:T(8,128)} %shard_map.30.refs_0_), channel_id=1, source_target_pairs={{0,1},{1,0},{2,3},{3,2},{4,5},{5,4},{6,7},{7,6},{8,9},{9,8},{10,11... | collective-permute-start | bytes 5529608 | tf_op jit(solution)/shard_map/ppermute | solution.py:165
  116.2 54.7 %collective-permute-start.5 = (f32[3600,128]{1,0:T(8,128)}, f32[3600,128]{1,0:T(8,128)}, u32[]{:S(2)}, u32[]{:S(2)}) collective-permute-start(f32[3600,128]{1,0:T(8,128)} %collective-permute-done.refs_4_), channel_id=1, source_target_pairs={{0,1},{1,0},{2,3},{3,2},{4,5},{5,4},{6,7},{7,6},{8,9},{9,8},{10,11... | collective-permute-start | bytes 5529608 | tf_op jit(solution)/shard_map/ppermute | solution.py:165
  117.4 53.5 %collective-permute-start.6 = (f32[3600,128]{1,0:T(8,128)}, f32[3600,128]{1,0:T(8,128)}, u32[]{:S(2)}, u32[]{:S(2)}) collective-permute-start(f32[3600,128]{1,0:T(8,128)} %collective-permute-done.1.refs_8_), channel_id=1, source_target_pairs={{0,1},{1,0},{2,3},{3,2},{4,5},{5,4},{6,7},{7,6},{8,9},{9,8},{10,11... | collective-permute-start | bytes 5529608 | tf_op jit(solution)/shard_map/ppermute | solution.py:165
  160.8 1.3 copy-start
  167.9 39.3 %collective-permute-start.2 = (f32[3600,128]{1,0:T(8,128)}, f32[3600,128]{1,0:T(8,128)S(1)}, u32[]{:S(2)}, u32[]{:S(2)}) collective-permute-start(f32[3600,128]{1,0:T(8,128)} %shard_map.31.refs_1_), channel_id=1, source_target_pairs={{0,2},{1,3},{2,0},{3,1},{4,6},{5,7},{6,4},{7,5},{8,10},{9,11},{10,... | collective-permute-start | bytes 5529608 | tf_op jit(solution)/shard_map/ppermute | solution.py:165
  169.4 40.2 %collective-permute-start.3 = (f32[3600,128]{1,0:T(8,128)}, f32[3600,128]{1,0:T(8,128)}, u32[]{:S(2)}, u32[]{:S(2)}) collective-permute-start(f32[3600,128]{1,0:T(8,128)} %shard_map.31.refs_1_), channel_id=1, source_target_pairs={{0,4},{1,5},{2,6},{3,7},{4,0},{5,1},{6,2},{7,3},{8,12},{9,13},{10,... | collective-permute-start | bytes 5529608 | tf_op jit(solution)/shard_map/ppermute | solution.py:165
  170.9 38.7 %collective-permute-start.7 = (f32[3600,128]{1,0:T(8,128)}, f32[3600,128]{1,0:T(8,128)S(1)}, u32[]{:S(2)}, u32[]{:S(2)}) collective-permute-start(f32[3600,128]{1,0:T(8,128)} %shard_map.31.refs_1_), channel_id=1, source_target_pairs={{0,1},{1,0},{2,3},{3,2},{4,5},{5,4},{6,7},{7,6},{8,9},{9,8},{10,11... | collective-permute-start | bytes 5529608 | tf_op jit(solution)/shard_map/ppermute | solution.py:165
  207.2 40.6 %copy-start.2 = (f32[3600,128]{1,0:T(8,128)}, f32[3600,128]{1,0:T(8,128)S(1)}, u32[]{:S(2)}) copy-start(f32[3600,128]{1,0:T(8,128)S(1)} %collective-permute-done.2.refs_5_) | copy-start | bytes 5529604
  209.6 32.7 %copy-start.3 = (f32[3600,128]{1,0:T(8,128)}, f32[3600,128]{1,0:T(8,128)S(1)}, u32[]{:S(2)}) copy-start(f32[3600,128]{1,0:T(8,128)S(1)} %collective-permute-done.7.refs_3_) | copy-start | bytes 5529604
  209.6 31.5 %collective-permute-start.10 = (f32[3600,128]{1,0:T(8,128)}, f32[3600,128]{1,0:T(8,128)}, u32[]{:S(2)}, u32[]{:S(2)}) collective-permute-start(f32[3600,128]{1,0:T(8,128)} %collective-permute-done.1.refs_8_), channel_id=1, source_target_pairs={{0,2},{1,3},{2,0},{3,1},{4,6},{5,7},{6,4},{7,5},{8,10},{9,11},{10,... | collective-permute-start | bytes 5529608 | tf_op jit(solution)/shard_map/ppermute | solution.py:165
  209.7 32.6 %collective-permute-start.11 = (f32[3600,128]{1,0:T(8,128)S(1)}, f32[3600,128]{1,0:T(8,128)}, u32[]{:S(2)}, u32[]{:S(2)}) collective-permute-start(f32[3600,128]{1,0:T(8,128)S(1)} %collective-permute-done.2.refs_5_), channel_id=1, source_target_pairs={{0,4},{1,5},{2,6},{3,7},{4,0},{5,1},{6,2},{7,3},{8,12},{9,13},{10,... | collective-permute-start | bytes 5529608 | tf_op jit(solution)/shard_map/ppermute | solution.py:165
  211.2 33.0 %collective-permute-start.8 = (f32[3600,128]{1,0:T(8,128)S(1)}, f32[3600,128]{1,0:T(8,128)}, u32[]{:S(2)}, u32[]{:S(2)}) collective-permute-start(f32[3600,128]{1,0:T(8,128)S(1)} %collective-permute-done.2.refs_5_), channel_id=1, source_target_pairs={{0,1},{1,0},{2,3},{3,2},{4,5},{5,4},{6,7},{7,6},{8,9},{9,8},{10,11... | collective-permute-start | bytes 5529608 | tf_op jit(solution)/shard_map/ppermute | solution.py:165
  211.2 33.0 %collective-permute-start.9 = (f32[3600,128]{1,0:T(8,128)}, f32[3600,128]{1,0:T(8,128)}, u32[]{:S(2)}, u32[]{:S(2)}) collective-permute-start(f32[3600,128]{1,0:T(8,128)} %collective-permute-done.3.refs_9_), channel_id=1, source_target_pairs={{0,1},{1,0},{2,3},{3,2},{4,5},{5,4},{6,7},{7,6},{8,9},{9,8},{10,11... | collective-permute-start | bytes 5529608 | tf_op jit(solution)/shard_map/ppermute | solution.py:165
  241.1 4.1 collective-permute-start.12
  242.3 5.6 %collective-permute-start.13 = (f32[3600,128]{1,0:T(8,128)}, f32[3600,128]{1,0:T(8,128)}, u32[]{:S(2)}, u32[]{:S(2)}) collective-permute-start(f32[3600,128]{1,0:T(8,128)} %collective-permute-done.11.refs_13_), channel_id=1, source_target_pairs={{0,1},{1,0},{2,3},{3,2},{4,5},{5,4},{6,7},{7,6},{8,9},{9,8},{10,11... | collective-permute-start | bytes 5529608 | tf_op jit(solution)/shard_map/ppermute | solution.py:165
Sparse Core Ops, SparseCore 0:
  59.6 182.0 all-gather.3
  243.3 98.7 all-gather.7
  343.6 44.5 all-gather.5

commit v3 on v1

v3 whole, which is shorter than its diff:
```python
import functools

import jax
import jax.numpy as jnp
from jax import lax
from jax.experimental import pallas as pl
from jax.experimental.pallas import tpu as pltpu
from jax.sharding import PartitionSpec as P

ROWS = 240
WIDE = 512
VMEM_BYTES = 60 * 2**20


def params():
    return pltpu.CompilerParams(vmem_limit_bytes=VMEM_BYTES)


def moved(bytes_accessed, flops=0):
    return pl.CostEstimate(
        flops=flops, bytes_accessed=bytes_accessed, transcendentals=0
    )


def chunks_of(columns):
    if columns == 1920:
        order = [(0, 1024), (1280, 640), (1024, 256)]
        return [(start, width, width) for start, width in order]
    wide = [(n, WIDE, WIDE) for n in range(0, columns - WIDE + 1, WIDE)]
    start = len(wide) * WIDE
    return wide + ([(start, columns - start, WIDE)] if start < columns else [])


def cut_kernel(t_ref, out_ref):
    groups, _, rows = out_ref.shape
    for n in range(groups):
        out_ref[n] = t_ref[:, n * rows : (n + 1) * rows]


def cut(columns, groups, half):
    depth, pairs = columns.shape
    shape = (groups, depth // 2, pairs // groups)
    return pl.pallas_call(
        cut_kernel,
        grid=(1,),
        in_specs=[pl.BlockSpec((depth // 2, pairs), lambda i: (half, 0))],
        out_specs=pl.BlockSpec(shape, lambda i: (0, 0, 0)),
        out_shape=jax.ShapeDtypeStruct(shape, jnp.float32),
        compiler_params=params(),
        cost_estimate=moved(4 * depth * pairs),
    )(columns)


def turn_kernel(t_ref, out_ref):
    out_ref[...] = t_ref[...].T


def turn(columns):
    depth, rows = columns.shape
    width = 512
    return pl.pallas_call(
        turn_kernel,
        grid=(pl.cdiv(rows, width),),
        in_specs=[pl.BlockSpec((depth, width), lambda i: (0, i))],
        out_specs=pl.BlockSpec((width, depth), lambda i: (i, 0)),
        out_shape=jax.ShapeDtypeStruct((rows, depth), jnp.float32),
        compiler_params=params(),
        cost_estimate=moved(8 * depth * rows),
    )(columns)


def split(x):
    high = x.astype(jnp.bfloat16)
    return high, (x - high.astype(jnp.float32)).astype(jnp.bfloat16)


def product_kernel(devices, place_ref, *refs):
    parts, w_hbm = refs[: 2 * devices], refs[2 * devices]
    out_ref, t_ref, w, w_high, w_low, t_high, t_low, arrived = refs[-8:]
    depth, width = w.shape
    block = depth // devices

    @pl.when(pl.program_id(0) == 0)
    def _():
        whole = pltpu.make_async_copy(w_hbm, w, arrived)
        whole.start()
        whole.wait()
        for n in range(devices):
            rows = slice(n * block, (n + 1) * block)
            w_high[rows, :], w_low[rows, :] = split(w[rows, :])

    for n in range(devices):
        value = jnp.concatenate([parts[2 * n][...], parts[2 * n + 1][...]], axis=1)
        to = pl.ds(pl.multiple_of((place_ref[0] ^ n) * block, block), block)
        t_ref[:, to] = value
        t_high[:, to], t_low[:, to] = split(value)
    dot = functools.partial(jnp.dot, preferred_element_type=jnp.float32)
    total = dot(t_low[...], w_high[...])
    total += dot(t_high[...], w_low[...])
    total += dot(t_high[...], w_high[...])
    out_ref[:, :width] = 0.5 * total


def product(place, parts, w, chunk, full):
    start, width, block = chunk
    rows, size = parts[0].shape
    depth = w.shape[0]
    t_half = pltpu.VMEM((ROWS, depth), jnp.bfloat16)
    w_half = pltpu.VMEM((depth, width), jnp.bfloat16)
    return pl.pallas_call(
        functools.partial(product_kernel, len(parts) // 2),
        grid_spec=pltpu.PrefetchScalarGridSpec(
            num_scalar_prefetch=1,
            grid=(pl.cdiv(rows, ROWS),),
            in_specs=[pl.BlockSpec((ROWS, size), lambda i, p: (i, 0))] * len(parts)
            + [pl.BlockSpec(memory_space=pl.ANY)],
            out_specs=[
                pl.BlockSpec((ROWS, block), lambda i, p: (i, start // block)),
                pl.BlockSpec((ROWS, depth), lambda i, p: (i, 0)),
            ],
            scratch_shapes=[
                pltpu.VMEM((depth, width), jnp.float32),
                w_half,
                w_half,
                t_half,
                t_half,
                pltpu.SemaphoreType.DMA(()),
            ],
        ),
        out_shape=[
            jax.ShapeDtypeStruct((rows, full), jnp.float32),
            jax.ShapeDtypeStruct((rows, depth), jnp.float32),
        ],
        compiler_params=params(),
        cost_estimate=moved(
            4 * (2 * rows * depth + depth * width + rows * width),
            6 * rows * depth * width,
        ),
    )(place, *parts, w)


def tie(*values):
    return lax.optimization_barrier(values)


def per_device(line, devices, amplitudes, integrals):
    columns = integrals.shape[1]
    rows = amplitudes.shape[0] // line
    chunks = chunks_of(columns)

    def swap(x, mask):
        return lax.ppermute(x, "ka", [(d, d ^ mask) for d in range(devices)])

    def gather(n, source):
        start, width, _ = chunks[n]
        x = lax.slice_in_dim(source, start, start + width, axis=1)
        x = x.reshape(devices // line, line, 2, -1, width).swapaxes(1, 2)
        return lax.all_gather(x.reshape(-1, width), "ga", axis=0, tiled=True)

    source, amplitudes = tie(integrals, amplitudes)
    gathered = [gather(0, source)]

    held = []
    for half in range(2):
        blocks = cut(amplitudes.T, line, half)
        if half:
            blocks, first, source = tie(blocks, first, integrals)
            gathered.append(gather(1, source))
            held.append({0: turn(first)})
        blocks = lax.all_to_all(blocks, "ga", split_axis=0, concat_axis=0, tiled=True)
        first = blocks.reshape(-1, rows)
    held.append({0: turn(first)})

    masks = [1 << bit for bit in range(1, devices.bit_length() - 1)]
    orders = (masks[::-1], masks)
    across = [{}, {}]
    for half, order in enumerate(orders):
        blocks = held[half]
        if half:
            across[1] = {0: swap(blocks[0], 1)}
        for level in range(1, len(masks) + 1):
            if half and level == 2:
                held, across, source = tie(held, across, integrals)
                gathered += [gather(n, source) for n in range(2, len(chunks))]
                blocks = held[1]
            if half and level == 2 == len(masks):
                some = rows // 16 * 8
                by_first = swap(blocks[masks[0]][:some], masks[1])
                by_second = swap(blocks[masks[1]][some:], masks[0])
                blocks[masks[0] | masks[1]] = jnp.concatenate([by_first, by_second])
                continue
            for n in range(2, devices, 2):
                if n.bit_count() == level:
                    last = [mask for mask in order if n & mask][-1]
                    blocks[n] = swap(blocks[n ^ last], last)
        for n in sorted(blocks.keys() - across[half].keys()):
            across[half][n] = swap(blocks[n], 1)
    parts = [
        (across if n % 2 else held)[half][n - n % 2]
        for n in range(devices)
        for half in range(2)
    ]

    place = lax.axis_index("ka").astype(jnp.int32)
    out, whole = product(place.reshape(1), parts, gathered[0], chunks[0], columns)
    for (start, _, _), w in zip(chunks[1:], gathered[1:]):
        ladder = jnp.dot(
            whole,
            w,
            precision=lax.Precision.HIGH,
            preferred_element_type=jnp.float32,
        )
        out = lax.dynamic_update_slice_in_dim(out, 0.5 * ladder, start, axis=1)
    return out


def solution(mesh):
    placed = (P(None, ("ka", "ga")), P("ga", "ka"))
    return jax.shard_map(
        functools.partial(per_device, mesh.shape["ga"], mesh.shape["ka"]),
        mesh=mesh,
        in_specs=placed,
        out_specs=P("ga", "ka"),
        check_vma=False,
    )
```

time: 433 us -> 429 us (level)
  matrix products: 0 us -> 61.1 us
  Pallas kernels: 143 us -> 84.9 us
  waiting for transfers between devices: 241 us -> 228 us
    dot_general x0 -> x2, matrix products: none -> 61.1 us  [per_device(): jnp.dot(whole, w, precision=lax.Precision.HIGH, preferred_element_type=jn...]
    pallas_call x3 -> x1, Pallas kernels: 124 us -> 66.6 us  [product(): pl.pallas_call(functools.partial(product_kernel, len(parts) // 2), grid_s...]
    ppermute x14 -> x15, waiting for transfers between devices: 109 us -> 96.3 us  [swap(): return lax.ppermute(x, 'ka', [(d, d ^ mask) for d in range(devices)])]
    ppermute x14 -> x15, starting transfers between devices: 8.14 us -> 10.5 us  [swap(): return lax.ppermute(x, 'ka', [(d, d ^ mask) for d in range(devices)])]
  transfers between devices with their start and end apart: 19 -> 20, of which waited for: 10 -> 9; matrix products, arithmetic and copies ran while one was open for 1% -> 11% of each run, Pallas kernels for 28% -> 20%
where the time goes in v3:
time: 429 us; the launch traced here: 423 us
  waiting for transfers between devices  228 us (53%)
  Pallas kernels  84.9 us (20%)
  matrix products  61.1 us (14%)
  starting transfers between devices  22.7 us (5%)
  local copies, waits for them, and re-layouts  13.5 us (3%)
  between operations  13.2 us (3%)
    all_to_all x2, waiting for transfers between devices, per_device(): lax.all_to_all(blocks, 'ga', split_axis=0, concat_axis=0, tiled=True)  131 us
    ppermute x15, waiting for transfers between devices, swap(): return lax.ppermute(x, 'ka', [(d, d ^ mask) for d in range(devices)])  96.3 us
    pallas_call x1, Pallas kernels, product(): pl.pallas_call(functools.partial(product_kernel, len(parts) // 2), grid_s...  66.6 us
    dot_general x2, matrix products, per_device(): jnp.dot(whole, w, precision=lax.Precision.HIGH, preferred_element_type=jn...  61.1 us
    all_to_all x2, starting transfers between devices, per_device(): lax.all_to_all(blocks, 'ga', split_axis=0, concat_axis=0, tiled=True)  12.1 us
    pallas_call x2, Pallas kernels, turn(): pl.pallas_call(turn_kernel, grid=(pl.cdiv(rows, width),), in_specs=[pl.Bl...  11.7 us
    ppermute x15, starting transfers between devices, swap(): return lax.ppermute(x, 'ka', [(d, d ^ mask) for d in range(devices)])  10.5 us
  transfers between devices with their start and end apart: 20, of which 9 were waited for; matrix products, arithmetic and copies ran while one was open for 11% of the time, Pallas kernels for 20%

profile of v3, /device:TPU:16, one launch (start us, length us, event | category | flops | bytes accessed | tf_op | source)
XLA Modules:
  0.0 423.3 jit_solution(4118979910693209593)
XLA Ops:
  6.5 1.6 slice-done
  9.6 3.2 shard_map.29
  12.8 5.2 %all-to-all-start = ((f32[4,32,3600]{2,1,0:T(8,128)}), f32[4,32,3600]{2,1,0:T(8,128)S(1)}, u32[]{:S(2)}, u32[]{:S(2)}) async-start(f32[4,32,3600]{2,1,0:T(8,128)} %shard_map.29), calls=%async_computation | async-start | bytes 3801088 | tf_op jit(solution)/shard_map/all_to_all | solution.py:170
  18.0 3.4 shard_map.28
  21.5 91.5 %all-to-all-done = f32[4,32,3600]{2,1,0:T(8,128)S(1)} async-done(((f32[4,32,3600]{2,1,0:T(8,128)}), f32[4,32,3600]{2,1,0:T(8,128)S(1)}, u32[]{:S(2)}, u32[]{:S(2)}) %all-to-all-start) | async-done | bytes 1843232 | tf_op jit(solution)/shard_map/all_to_all | solution.py:170
  114.2 5.8 %shard_map.30.refs_0_ = f32[3600,128]{1,0:T(8,128)} custom-call(f32[128,3600]{1,0:T(8,128)} %bitcast.27), custom_call_target="tpu_custom_call" | custom-call | bytes 3686400 | tf_op jit(solution)/shard_map/pallas_call | solution.py:61
  120.0 1.5 collective-permute-start.1
  121.5 6.9 %all-to-all-start.1 = ((f32[4,32,3600]{2,1,0:T(8,128)}), f32[4,32,3600]{2,1,0:T(8,128)S(1)}, u32[]{:S(2)}, u32[]{:S(2)}) async-start(f32[4,32,3600]{2,1,0:T(8,128)} %shard_map.28), calls=%async_computation.1 | async-start | bytes 3801088 | tf_op jit(solution)/shard_map/all_to_all | solution.py:170
  131.1 1.6 collective-permute-start
  132.6 21.1 %collective-permute-done.1.refs_8_ = f32[3600,128]{1,0:T(8,128)} collective-permute-done((f32[3600,128]{1,0:T(8,128)}, f32[3600,128]{1,0:T(8,128)}, u32[]{:S(2)}, u32[]{:S(2)}) %collective-permute-start.1) | collective-permute-done | bytes 1843232 | tf_op jit(solution)/shard_map/ppermute | solution.py:152
  153.7 1.5 collective-permute-start.2
  155.2 19.4 %collective-permute-done.refs_4_ = f32[3600,128]{1,0:T(8,128)} collective-permute-done((f32[3600,128]{1,0:T(8,128)}, f32[3600,128]{1,0:T(8,128)}, u32[]{:S(2)}, u32[]{:S(2)}) %collective-permute-start) | collective-permute-done | bytes 1843232 | tf_op jit(solution)/shard_map/ppermute | solution.py:152
  174.6 40.0 %all-to-all-done.1 = f32[4,32,3600]{2,1,0:T(8,128)S(1)} async-done(((f32[4,32,3600]{2,1,0:T(8,128)}), f32[4,32,3600]{2,1,0:T(8,128)S(1)}, u32[]{:S(2)}, u32[]{:S(2)}) %all-to-all-start.1) | async-done | bytes 1843232 | tf_op jit(solution)/shard_map/all_to_all | solution.py:170
  215.9 5.8 %shard_map.31.refs_1_ = f32[3600,128]{1,0:T(8,128)} custom-call(f32[128,3600]{1,0:T(8,128)} %bitcast.26), custom_call_target="tpu_custom_call" | custom-call | bytes 3686400 | tf_op jit(solution)/shard_map/pallas_call | solution.py:61
  221.7 1.5 collective-permute-start.3
  224.5 35.0 %collective-permute-done.3.refs_5_ = f32[3600,128]{1,0:T(8,128)S(1)} collective-permute-done((f32[3600,128]{1,0:T(8,128)}, f32[3600,128]{1,0:T(8,128)S(1)}, u32[]{:S(2)}, u32[]{:S(2)}) %collective-permute-start.3) | collective-permute-done | bytes 1843232 | tf_op jit(solution)/shard_map/ppermute | solution.py:152
  259.6 2.0 collective-permute-done.4.refs_9_
  262.8 1.8 collective-permute-start.12
  267.2 13.9 %collective-permute-done.12 = f32[1800,128]{1,0:T(8,128)S(1)} collective-permute-done((f32[1800,128]{1,0:T(8,128)S(1)}, f32[1800,128]{1,0:T(8,128)S(1)}, u32[]{:S(2)}, u32[]{:S(2)}) %collective-permute-start.12) | collective-permute-done | bytes 921632 | tf_op jit(solution)/shard_map/ppermute | solution.py:152
  282.1 1.7 collective-permute-done.13
  285.7 3.2 collective-permute-done.14.refs_15_
  288.9 66.6 %shard_map.32 = (f32[3600,1920]{1,0:T(8,128)}, f32[3600,2048]{1,0:T(8,128)}) custom-call(s32[1]{0:T(128)} %bitcast.place_ref, f32[3600,128]{1,0:T(8,128)} %shard_map.30.refs_0_, f32[3600,128]{1,0:T(8,128)} %shard_map.31.refs_1_, f32[3600,128]{1,0:T(8,128)} %collective-permute-done.5.refs_2_, f32[3600,128]{1,0:T(8,128)} %copy-done.3, ...), custom_call_target="tpu_custom_call" | custom-call | flops 45298483200 | bytes 82116608 | tf_op jit(solution)/shard_map/pallas_call | solution.py:110
  355.6 41.9 %multiply_dynamic-update-slice_fusion = f32[3600,1920]{1,0:T(8,128)} fusion(f32[3600,1920]{1,0:T(8,128)} %get-tuple-element.41, f32[3600,2048]{1,0:T(8,128)} %get-tuple-element.42, f32[2048,640]{1,0:T(8,128)} %all-gather.6.cloned.1.call-done), kind=kOutput, calls=%fused_computation | convolution fusion | flops 28313856000 | bytes 43950080 | tf_op jit(solution)/shard_map/dot_general | solution.py:207
  397.5 19.3 %fusion = f32[3600,1920]{1,0:T(8,128)} fusion(f32[3600,1920]{1,0:T(8,128)} %multiply_dynamic-update-slice_fusion, f32[3600,2048]{1,0:T(8,128)} %get-tuple-element.42, f32[2048,256]{1,0:T(8,128)} %all-gather.8.cloned.1.call-done), kind=kOutput, calls=%fused_computation.2 | convolution fusion | flops 11325542400 | bytes 35274752 | tf_op jit(solution)/shard_map/dot_general | solution.py:207
  (47 shorter events, 14.8 us)
Async XLA Ops:
  6.5 1.6 slice-start
  6.5 282.4 %all-gather.4.cloned.1.call-start = ((), (), s32[]{:S(2)}) async-start(), calls=%async_computation.2 | async-start | bytes 10485760 | tf_op jit(solution)/shard_map/all_gather | solution.py:158
  12.8 100.1 %all-to-all-start = ((f32[4,32,3600]{2,1,0:T(8,128)}), f32[4,32,3600]{2,1,0:T(8,128)S(1)}, u32[]{:S(2)}, u32[]{:S(2)}) async-start(f32[4,32,3600]{2,1,0:T(8,128)} %shard_map.29), calls=%async_computation | async-start | bytes 3801088 | tf_op jit(solution)/shard_map/all_to_all | solution.py:170
  120.0 33.7 %collective-permute-start.1 = (f32[3600,128]{1,0:T(8,128)}, f32[3600,128]{1,0:T(8,128)}, u32[]{:S(2)}, u32[]{:S(2)}) collective-permute-start(f32[3600,128]{1,0:T(8,128)} %shard_map.30.refs_0_), channel_id=1, source_target_pairs={{0,4},{1,5},{2,6},{3,7},{4,0},{5,1},{6,2},{7,3},{8,12},{9,13},{10,... | collective-permute-start | bytes 5529608 | tf_op jit(solution)/shard_map/ppermute | solution.py:152
  121.5 93.1 %all-to-all-start.1 = ((f32[4,32,3600]{2,1,0:T(8,128)}), f32[4,32,3600]{2,1,0:T(8,128)S(1)}, u32[]{:S(2)}, u32[]{:S(2)}) async-start(f32[4,32,3600]{2,1,0:T(8,128)} %shard_map.28), calls=%async_computation.1 | async-start | bytes 3801088 | tf_op jit(solution)/shard_map/all_to_all | solution.py:170
  128.4 1.3 slice-start.1
  128.4 227.2 %all-gather.6.cloned.1.call-start = ((), (), s32[]{:S(2)}) async-start(), calls=%async_computation.3 | async-start | bytes 6553600 | tf_op jit(solution)/shard_map/all_gather | solution.py:158
  131.0 266.5 %all-gather.8.cloned.1.call-start = ((), (), s32[]{:S(2)}) async-start(), calls=%async_computation.4 | async-start | bytes 2621440 | tf_op jit(solution)/shard_map/all_gather | solution.py:158
  131.1 43.5 %collective-permute-start = (f32[3600,128]{1,0:T(8,128)}, f32[3600,128]{1,0:T(8,128)}, u32[]{:S(2)}, u32[]{:S(2)}) collective-permute-start(f32[3600,128]{1,0:T(8,128)} %shard_map.30.refs_0_), channel_id=1, source_target_pairs={{0,2},{1,3},{2,0},{3,1},{4,6},{5,7},{6,4},{7,5},{8,10},{9,11},{10,... | collective-permute-start | bytes 5529608 | tf_op jit(solution)/shard_map/ppermute | solution.py:152
  132.6 90.5 %collective-permute-start.5 = (f32[3600,128]{1,0:T(8,128)}, f32[3600,128]{1,0:T(8,128)}, u32[]{:S(2)}, u32[]{:S(2)}) collective-permute-start(f32[3600,128]{1,0:T(8,128)} %shard_map.30.refs_0_), channel_id=1, source_target_pairs={{0,1},{1,0},{2,3},{3,2},{4,5},{5,4},{6,7},{7,6},{8,9},{9,8},{10,11... | collective-permute-start | bytes 5529608 | tf_op jit(solution)/shard_map/ppermute | solution.py:152
  153.7 70.3 %collective-permute-start.2 = (f32[3600,128]{1,0:T(8,128)}, f32[3600,128]{1,0:T(8,128)}, u32[]{:S(2)}, u32[]{:S(2)}) collective-permute-start(f32[3600,128]{1,0:T(8,128)} %collective-permute-done.1.refs_8_), channel_id=1, source_target_pairs={{0,2},{1,3},{2,0},{3,1},{4,6},{5,7},{6,4},{7,5},{8,10},{9,11},{10,... | collective-permute-start | bytes 5529608 | tf_op jit(solution)/shard_map/ppermute | solution.py:152
  155.2 68.8 %collective-permute-start.7 = (f32[3600,128]{1,0:T(8,128)}, f32[3600,128]{1,0:T(8,128)}, u32[]{:S(2)}, u32[]{:S(2)}) collective-permute-start(f32[3600,128]{1,0:T(8,128)} %collective-permute-done.1.refs_8_), channel_id=1, source_target_pairs={{0,1},{1,0},{2,3},{3,2},{4,5},{5,4},{6,7},{7,6},{8,9},{9,8},{10,11... | collective-permute-start | bytes 5529608 | tf_op jit(solution)/shard_map/ppermute | solution.py:152
  174.6 50.0 %collective-permute-start.6 = (f32[3600,128]{1,0:T(8,128)}, f32[3600,128]{1,0:T(8,128)}, u32[]{:S(2)}, u32[]{:S(2)}) collective-permute-start(f32[3600,128]{1,0:T(8,128)} %collective-permute-done.refs_4_), channel_id=1, source_target_pairs={{0,1},{1,0},{2,3},{3,2},{4,5},{5,4},{6,7},{7,6},{8,9},{9,8},{10,11... | collective-permute-start | bytes 5529608 | tf_op jit(solution)/shard_map/ppermute | solution.py:152
  221.7 37.9 %collective-permute-start.3 = (f32[3600,128]{1,0:T(8,128)}, f32[3600,128]{1,0:T(8,128)S(1)}, u32[]{:S(2)}, u32[]{:S(2)}) collective-permute-start(f32[3600,128]{1,0:T(8,128)} %shard_map.31.refs_1_), channel_id=1, source_target_pairs={{0,2},{1,3},{2,0},{3,1},{4,6},{5,7},{6,4},{7,5},{8,10},{9,11},{10,... | collective-permute-start | bytes 5529608 | tf_op jit(solution)/shard_map/ppermute | solution.py:152
  223.2 38.4 %collective-permute-start.4 = (f32[3600,128]{1,0:T(8,128)}, f32[3600,128]{1,0:T(8,128)}, u32[]{:S(2)}, u32[]{:S(2)}) collective-permute-start(f32[3600,128]{1,0:T(8,128)} %shard_map.31.refs_1_), channel_id=1, source_target_pairs={{0,4},{1,5},{2,6},{3,7},{4,0},{5,1},{6,2},{7,3},{8,12},{9,13},{10,... | collective-permute-start | bytes 5529608 | tf_op jit(solution)/shard_map/ppermute | solution.py:152
  224.0 37.5 %collective-permute-start.9 = (f32[3600,128]{1,0:T(8,128)}, f32[3600,128]{1,0:T(8,128)S(1)}, u32[]{:S(2)}, u32[]{:S(2)}) collective-permute-start(f32[3600,128]{1,0:T(8,128)} %shard_map.31.refs_1_), channel_id=1, source_target_pairs={{0,1},{1,0},{2,3},{3,2},{4,5},{5,4},{6,7},{7,6},{8,9},{9,8},{10,11... | collective-permute-start | bytes 5529608 | tf_op jit(solution)/shard_map/ppermute | solution.py:152
  224.0 38.7 %collective-permute-start.8 = (f32[3600,128]{1,0:T(8,128)}, f32[3600,128]{1,0:T(8,128)}, u32[]{:S(2)}, u32[]{:S(2)}) collective-permute-start(f32[3600,128]{1,0:T(8,128)} %collective-permute-done.2.refs_12_), channel_id=1, source_target_pairs={{0,1},{1,0},{2,3},{3,2},{4,5},{5,4},{6,7},{7,6},{8,9},{9,8},{10,11... | collective-permute-start | bytes 5529608 | tf_op jit(solution)/shard_map/ppermute | solution.py:152
  259.6 22.6 %copy-start.2 = (f32[3600,128]{1,0:T(8,128)}, f32[3600,128]{1,0:T(8,128)S(1)}, u32[]{:S(2)}) copy-start(f32[3600,128]{1,0:T(8,128)S(1)} %collective-permute-done.3.refs_5_) | copy-start | bytes 5529604
  262.8 18.3 %collective-permute-start.12 = (f32[1800,128]{1,0:T(8,128)S(1)}, f32[1800,128]{1,0:T(8,128)S(1)}, u32[]{:S(2)}, u32[]{:S(2)}) collective-permute-start(f32[1800,128]{1,0:T(8,128)S(1)} %slice.15), channel_id=1, source_target_pairs={{0,4},{1,5},{2,6},{3,7},{4,0},{5,1},{6,2},{7,3},{8,12},{9,13},{10,... | collective-permute-start | bytes 2764808 | tf_op jit(solution)/shard_map/ppermute | solution.py:152
  265.8 19.0 %slice-start.2 = ((f32[512,1920]{1,0:T(8,128)}), f32[512,256]{1,0:T(8,128)S(1)}, s32[]{:S(2)}) async-start(f32[512,1920]{1,0:T(8,128)} %param.3), calls=%async_computation.7 | async-start | bytes 1048576 | tf_op jit(solution)/shard_map/slice | solution.py:156
  265.9 17.9 %collective-permute-start.13 = (f32[1800,128]{1,0:T(8,128)S(1)}, f32[1800,128]{1,0:T(8,128)S(1)}, u32[]{:S(2)}, u32[]{:S(2)}) collective-permute-start(f32[1800,128]{1,0:T(8,128)S(1)} %slice.16), channel_id=1, source_target_pairs={{0,2},{1,3},{2,0},{3,1},{4,6},{5,7},{6,4},{7,5},{8,10},{9,11},{10,... | collective-permute-start | bytes 2764808 | tf_op jit(solution)/shard_map/ppermute | solution.py:152
  266.7 19.0 %collective-permute-start.10 = (f32[3600,128]{1,0:T(8,128)S(1)}, f32[3600,128]{1,0:T(8,128)}, u32[]{:S(2)}, u32[]{:S(2)}) collective-permute-start(f32[3600,128]{1,0:T(8,128)S(1)} %collective-permute-done.3.refs_5_), channel_id=1, source_target_pairs={{0,1},{1,0},{2,3},{3,2},{4,5},{5,4},{6,7},{7,6},{8,9},{9,8},{10,11... | collective-permute-start | bytes 5529608 | tf_op jit(solution)/shard_map/ppermute | solution.py:152
  266.7 19.0 %collective-permute-start.11 = (f32[3600,128]{1,0:T(8,128)}, f32[3600,128]{1,0:T(8,128)}, u32[]{:S(2)}, u32[]{:S(2)}) collective-permute-start(f32[3600,128]{1,0:T(8,128)} %collective-permute-done.4.refs_9_), channel_id=1, source_target_pairs={{0,1},{1,0},{2,3},{3,2},{4,5},{5,4},{6,7},{7,6},{8,9},{9,8},{10,11... | collective-permute-start | bytes 5529608 | tf_op jit(solution)/shard_map/ppermute | solution.py:152
  284.8 4.1 collective-permute-start.14
  (3 other events, 3.7 us)
Sparse Core Ops, SparseCore 0:
  9.7 224.6 all-gather.3
  236.0 98.6 all-gather.5
  336.2 44.5 all-gather.7

commit v4 on v3

--- a/solution.py
+++ b/solution.py
@@ -76,7 +76,7 @@
 
 def product_kernel(devices, place_ref, *refs):
     parts, w_hbm = refs[: 2 * devices], refs[2 * devices]
-    out_ref, t_ref, w, w_high, w_low, t_high, t_low, arrived = refs[-8:]
+    out_ref, t_high, t_low, w, w_high, w_low, arrived = refs[-7:]
     depth, width = w.shape
     block = depth // devices
 
@@ -92,7 +92,6 @@
     for n in range(devices):
         value = jnp.concatenate([parts[2 * n][...], parts[2 * n + 1][...]], axis=1)
         to = pl.ds(pl.multiple_of((place_ref[0] ^ n) * block, block), block)
-        t_ref[:, to] = value
         t_high[:, to], t_low[:, to] = split(value)
     dot = functools.partial(jnp.dot, preferred_element_type=jnp.float32)
     total = dot(t_low[...], w_high[...])
@@ -105,7 +104,6 @@
     start, width, block = chunk
     rows, size = parts[0].shape
     depth = w.shape[0]
-    t_half = pltpu.VMEM((ROWS, depth), jnp.bfloat16)
     w_half = pltpu.VMEM((depth, width), jnp.bfloat16)
     return pl.pallas_call(
         functools.partial(product_kernel, len(parts) // 2),
@@ -117,19 +115,19 @@
             out_specs=[
                 pl.BlockSpec((ROWS, block), lambda i, p: (i, start // block)),
                 pl.BlockSpec((ROWS, depth), lambda i, p: (i, 0)),
+                pl.BlockSpec((ROWS, depth), lambda i, p: (i, 0)),
             ],
             scratch_shapes=[
                 pltpu.VMEM((depth, width), jnp.float32),
                 w_half,
                 w_half,
-                t_half,
-                t_half,
                 pltpu.SemaphoreType.DMA(()),
             ],
         ),
         out_shape=[
             jax.ShapeDtypeStruct((rows, full), jnp.float32),
-            jax.ShapeDtypeStruct((rows, depth), jnp.float32),
+            jax.ShapeDtypeStruct((rows, depth), jnp.bfloat16),
+            jax.ShapeDtypeStruct((rows, depth), jnp.bfloat16),
         ],
         compiler_params=params(),
         cost_estimate=moved(
@@ -202,14 +200,15 @@
     ]
 
     place = lax.axis_index("ka").astype(jnp.int32)
-    out, whole = product(place.reshape(1), parts, gathered[0], chunks[0], columns)
-    for (start, _, _), w in zip(chunks[1:], gathered[1:]):
-        ladder = jnp.dot(
-            whole,
-            w,
-            precision=lax.Precision.HIGH,
-            preferred_element_type=jnp.float32,
-        )
+    out, *t = product(place.reshape(1), parts, gathered[0], chunks[0], columns)
+    dot = functools.partial(jnp.dot, preferred_element_type=jnp.float32)
+    for (start, width, _), w in zip(chunks[1:], gathered[1:]):
+        out, (t_high, t_low), w = tie(out, t, w)
+        high = lax.reduce_precision(w, exponent_bits=8, mantissa_bits=7)
+        w_low = (w - high).astype(jnp.bfloat16)
+        w_high = high.astype(jnp.bfloat16)
+        both = dot(t_high, jnp.concatenate([w_low, w_high], axis=1))
+        ladder = dot(t_low, w_high) + both[:, :width] + both[:, width:]
         out = lax.dynamic_update_slice_in_dim(out, 0.5 * ladder, start, axis=1)
     return out
 

time: 429 us -> 431 us (level)
  other arithmetic: 0 us -> 5.38 us
    convert_element_type x0 -> x2, other arithmetic: none -> 5.38 us  [per_device(): w_low = (w - high).astype(jnp.bfloat16)]
    dot_general x2 -> x4, matrix products: 61.1 us -> 61.4 us  [the longest x2 35 us: per_device(): both = dot(t_high, jnp.concatenate([w_low, w_high], axis=1))]
  transfers between devices with their start and end apart: 20 -> 20, of which waited for: 9 -> 9; matrix products, arithmetic and copies ran while one was open for 11% -> 12% of each run, Pallas kernels for 20% -> 19%
where the time goes in v4:
time: 431 us; the launch traced here: 426 us
  waiting for transfers between devices  229 us (53%)
  Pallas kernels  82 us (19%)
  matrix products  61.4 us (14%)
  starting transfers between devices  22.7 us (5%)
  between operations  13.3 us (3%)
  local copies, waits for them, and re-layouts  12.4 us (3%)
  other arithmetic  5.38 us (1%)
    all_to_all x2, waiting for transfers between devices, per_device(): lax.all_to_all(blocks, 'ga', split_axis=0, concat_axis=0, tiled=True)  133 us
    ppermute x15, waiting for transfers between devices, swap(): return lax.ppermute(x, 'ka', [(d, d ^ mask) for d in range(devices)])  96.2 us
    pallas_call x1, Pallas kernels, product(): pl.pallas_call(functools.partial(product_kernel, len(parts) // 2), grid_s...  63.6 us
    dot_general x2, matrix products, per_device(): both = dot(t_high, jnp.concatenate([w_low, w_high], axis=1))  35 us
    dot_general x2, matrix products, per_device(): ladder = dot(t_low, w_high) + both[:, :width] + both[:, width:]  26.4 us
    all_to_all x2, starting transfers between devices, per_device(): lax.all_to_all(blocks, 'ga', split_axis=0, concat_axis=0, tiled=True)  12.1 us
    pallas_call x2, Pallas kernels, turn(): pl.pallas_call(turn_kernel, grid=(pl.cdiv(rows, width),), in_specs=[pl.Bl...  11.6 us
    ppermute x15, starting transfers between devices, swap(): return lax.ppermute(x, 'ka', [(d, d ^ mask) for d in range(devices)])  10.5 us
  transfers between devices with their start and end apart: 20, of which 9 were waited for; matrix products, arithmetic and copies ran while one was open for 12% of the time, Pallas kernels for 19%

profile of v4, /device:TPU:16, one launch (start us, length us, event | category | flops | bytes accessed | tf_op | source)
XLA Modules:
  0.0 426.1 jit_solution(14632929507530604286)
XLA Ops:
  6.5 1.6 slice-done
  9.6 3.2 shard_map.29
  12.8 5.2 %all-to-all-start = ((f32[4,32,3600]{2,1,0:T(8,128)}), f32[4,32,3600]{2,1,0:T(8,128)S(1)}, u32[]{:S(2)}, u32[]{:S(2)}) async-start(f32[4,32,3600]{2,1,0:T(8,128)} %shard_map.29), calls=%async_computation | async-start | bytes 3801088 | tf_op jit(solution)/shard_map/all_to_all | solution.py:168
  18.0 3.5 shard_map.28
  21.6 91.4 %all-to-all-done = f32[4,32,3600]{2,1,0:T(8,128)S(1)} async-done(((f32[4,32,3600]{2,1,0:T(8,128)}), f32[4,32,3600]{2,1,0:T(8,128)S(1)}, u32[]{:S(2)}, u32[]{:S(2)}) %all-to-all-start) | async-done | bytes 1843232 | tf_op jit(solution)/shard_map/all_to_all | solution.py:168
  114.2 5.8 %shard_map.30.refs_0_ = f32[3600,128]{1,0:T(8,128)} custom-call(f32[128,3600]{1,0:T(8,128)} %bitcast.29), custom_call_target="tpu_custom_call" | custom-call | bytes 3686400 | tf_op jit(solution)/shard_map/pallas_call | solution.py:61
  121.6 6.9 %all-to-all-start.1 = ((f32[4,32,3600]{2,1,0:T(8,128)}), f32[4,32,3600]{2,1,0:T(8,128)S(1)}, u32[]{:S(2)}, u32[]{:S(2)}) async-start(f32[4,32,3600]{2,1,0:T(8,128)} %shard_map.28), calls=%async_computation.1 | async-start | bytes 3801088 | tf_op jit(solution)/shard_map/all_to_all | solution.py:168
  131.3 22.4 %collective-permute-done.1.refs_8_ = f32[3600,128]{1,0:T(8,128)} collective-permute-done((f32[3600,128]{1,0:T(8,128)}, f32[3600,128]{1,0:T(8,128)}, u32[]{:S(2)}, u32[]{:S(2)}) %collective-permute-start.1) | collective-permute-done | bytes 1843232 | tf_op jit(solution)/shard_map/ppermute | solution.py:150
  155.2 18.0 %collective-permute-done.refs_4_ = f32[3600,128]{1,0:T(8,128)} collective-permute-done((f32[3600,128]{1,0:T(8,128)}, f32[3600,128]{1,0:T(8,128)}, u32[]{:S(2)}, u32[]{:S(2)}) %collective-permute-start) | collective-permute-done | bytes 1843232 | tf_op jit(solution)/shard_map/ppermute | solution.py:150
  173.3 41.4 %all-to-all-done.1 = f32[4,32,3600]{2,1,0:T(8,128)S(1)} async-done(((f32[4,32,3600]{2,1,0:T(8,128)}), f32[4,32,3600]{2,1,0:T(8,128)S(1)}, u32[]{:S(2)}, u32[]{:S(2)}) %all-to-all-start.1) | async-done | bytes 1843232 | tf_op jit(solution)/shard_map/all_to_all | solution.py:168
  216.0 5.8 %shard_map.31.refs_1_ = f32[3600,128]{1,0:T(8,128)} custom-call(f32[128,3600]{1,0:T(8,128)} %bitcast.28), custom_call_target="tpu_custom_call" | custom-call | bytes 3686400 | tf_op jit(solution)/shard_map/pallas_call | solution.py:61
  224.7 35.0 %collective-permute-done.3.refs_5_ = f32[3600,128]{1,0:T(8,128)S(1)} collective-permute-done((f32[3600,128]{1,0:T(8,128)}, f32[3600,128]{1,0:T(8,128)S(1)}, u32[]{:S(2)}, u32[]{:S(2)}) %collective-permute-start.3) | collective-permute-done | bytes 1843232 | tf_op jit(solution)/shard_map/ppermute | solution.py:150
  259.7 2.0 collective-permute-done.4.refs_9_
  263.0 1.8 collective-permute-start.12
  267.3 13.9 %collective-permute-done.12 = f32[1800,128]{1,0:T(8,128)S(1)} collective-permute-done((f32[1800,128]{1,0:T(8,128)S(1)}, f32[1800,128]{1,0:T(8,128)S(1)}, u32[]{:S(2)}, u32[]{:S(2)}) %collective-permute-start.12) | collective-permute-done | bytes 921632 | tf_op jit(solution)/shard_map/ppermute | solution.py:150
  282.3 1.7 collective-permute-done.13
  285.9 3.2 collective-permute-done.14.refs_15_
  289.1 63.6 %shard_map.32 = (f32[3600,1920]{1,0:T(8,128)}, bf16[3600,2048]{1,0:T(8,128)(2,1)}, bf16[3600,2048]{1,0:T(8,128)(2,1)}) custom-call(s32[1]{0:T(128)} %bitcast.place_ref, f32[3600,128]{1,0:T(8,128)} %shard_map.30.refs_0_, f32[3600,128]{1,0:T(8,128)} %shard_map.31.refs_1_, f32[3600,128]{1,0:T(8,128)} %collective-permute-done.5.refs_2_, f32[3600,128]{1,0:T(8,128)} %copy-done.3, ...), custom_call_target="tpu_custom_call" | custom-call | flops 45298483200 | bytes 82116608 | tf_op jit(solution)/shard_map/pallas_call | solution.py:108
  352.7 3.3 fusion.2
  356.1 23.8 %fusion.3 = f32[3600,1280]{1,0:T(8,128)} fusion(bf16[3600,2048]{1,0:T(8,128)(2,1)} %get-tuple-element.62, bf16[2048,640]{1,0:T(8,128)(2,1)S(1)} %get-tuple-element.64, bf16[2048,640]{1,0:T(8,128)(2,1)S(1)} %get-tuple-element.63), kind=kOutput, calls=%fused_computation.7 | convolution fusion | flops 18884853760 | bytes 38420480 | tf_op jit(solution)/shard_map/dot_general | solution.py:210
  379.9 20.2 %fusion.1 = f32[3600,1920]{1,0:T(8,128)} fusion(f32[3600,1920]{1,0:T(8,128)} %get-tuple-element.54, f32[3600,1280]{1,0:T(8,128)} %fusion.3, bf16[3600,2048]{1,0:T(8,128)(2,1)} %get-tuple-element.60, bf16[2048,640]{1,0:T(8,128)(2,1)S(1)} %get-tuple-element.64), kind=kOutput, calls=%fused_computation.2 | convolution fusion | flops 9444096000 | bytes 45015040 | tf_op jit(solution)/shard_map/dot_general | solution.py:211
  400.1 2.1 fusion.10
  402.2 11.2 %fusion.11 = f32[3600,512]{1,0:T(8,128)S(1)} fusion(bf16[3600,2048]{1,0:T(8,128)(2,1)} %get-tuple-element.62, bf16[2048,256]{1,0:T(8,128)(2,1)S(1)} %get-tuple-element.66, bf16[2048,256]{1,0:T(8,128)(2,1)S(1)} %get-tuple-element.65), kind=kOutput, calls=%fused_computation.18 | convolution fusion | flops 7553941504 | bytes 24215552 | tf_op jit(solution)/shard_map/dot_general | solution.py:210
  413.4 6.2 %fusion.9 = f32[3600,1920]{1,0:T(8,128)} fusion(f32[3600,1920]{1,0:T(8,128)} %fusion.1, bf16[3600,2048]{1,0:T(8,128)(2,1)S(1)} %bitcast.33, bf16[2048,256]{1,0:T(8,128)(2,1)S(1)} %get-tuple-element.66, f32[3600,512]{1,0:T(8,128)S(1)} %fusion.11), kind=kOutput, calls=%fused_computation.14 | convolution fusion | flops 3777638400 | bytes 26853376 | tf_op jit(solution)/shard_map/dot_general | solution.py:211
  (60 shorter events, 19.7 us)
Async XLA Ops:
  6.5 282.5 %all-gather.4.cloned.1.call-start = ((), (), s32[]{:S(2)}) async-start(), calls=%async_computation.2 | async-start | bytes 10485760 | tf_op jit(solution)/shard_map/all_gather | solution.py:156
  12.8 100.1 %all-to-all-start = ((f32[4,32,3600]{2,1,0:T(8,128)}), f32[4,32,3600]{2,1,0:T(8,128)S(1)}, u32[]{:S(2)}, u32[]{:S(2)}) async-start(f32[4,32,3600]{2,1,0:T(8,128)} %shard_map.29), calls=%async_computation | async-start | bytes 3801088 | tf_op jit(solution)/shard_map/all_to_all | solution.py:168
  120.0 33.7 %collective-permute-start.1 = (f32[3600,128]{1,0:T(8,128)}, f32[3600,128]{1,0:T(8,128)}, u32[]{:S(2)}, u32[]{:S(2)}) collective-permute-start(f32[3600,128]{1,0:T(8,128)} %shard_map.30.refs_0_), channel_id=1, source_target_pairs={{0,4},{1,5},{2,6},{3,7},{4,0},{5,1},{6,2},{7,3},{8,12},{9,13},{10,... | collective-permute-start | bytes 5529608 | tf_op jit(solution)/shard_map/ppermute | solution.py:150
  121.6 93.1 %all-to-all-start.1 = ((f32[4,32,3600]{2,1,0:T(8,128)}), f32[4,32,3600]{2,1,0:T(8,128)S(1)}, u32[]{:S(2)}, u32[]{:S(2)}) async-start(f32[4,32,3600]{2,1,0:T(8,128)} %shard_map.28), calls=%async_computation.1 | async-start | bytes 3801088 | tf_op jit(solution)/shard_map/all_to_all | solution.py:168
  128.5 224.3 %all-gather.6.cloned.1.call-start = ((), (), s32[]{:S(2)}) async-start(), calls=%async_computation.3 | async-start | bytes 6553600 | tf_op jit(solution)/shard_map/all_gather | solution.py:156
  129.7 270.4 %all-gather.8.cloned.1.call-start = ((), (), s32[]{:S(2)}) async-start(), calls=%async_computation.4 | async-start | bytes 2621440 | tf_op jit(solution)/shard_map/all_gather | solution.py:156
  129.7 43.5 %collective-permute-start = (f32[3600,128]{1,0:T(8,128)}, f32[3600,128]{1,0:T(8,128)}, u32[]{:S(2)}, u32[]{:S(2)}) collective-permute-start(f32[3600,128]{1,0:T(8,128)} %shard_map.30.refs_0_), channel_id=1, source_target_pairs={{0,2},{1,3},{2,0},{3,1},{4,6},{5,7},{6,4},{7,5},{8,10},{9,11},{10,... | collective-permute-start | bytes 5529608 | tf_op jit(solution)/shard_map/ppermute | solution.py:150
  131.3 92.0 %collective-permute-start.5 = (f32[3600,128]{1,0:T(8,128)}, f32[3600,128]{1,0:T(8,128)}, u32[]{:S(2)}, u32[]{:S(2)}) collective-permute-start(f32[3600,128]{1,0:T(8,128)} %shard_map.30.refs_0_), channel_id=1, source_target_pairs={{0,1},{1,0},{2,3},{3,2},{4,5},{5,4},{6,7},{7,6},{8,9},{9,8},{10,11... | collective-permute-start | bytes 5529608 | tf_op jit(solution)/shard_map/ppermute | solution.py:150
  153.8 70.4 %collective-permute-start.2 = (f32[3600,128]{1,0:T(8,128)}, f32[3600,128]{1,0:T(8,128)}, u32[]{:S(2)}, u32[]{:S(2)}) collective-permute-start(f32[3600,128]{1,0:T(8,128)} %collective-permute-done.1.refs_8_), channel_id=1, source_target_pairs={{0,2},{1,3},{2,0},{3,1},{4,6},{5,7},{6,4},{7,5},{8,10},{9,11},{10,... | collective-permute-start | bytes 5529608 | tf_op jit(solution)/shard_map/ppermute | solution.py:150
  155.2 68.9 %collective-permute-start.7 = (f32[3600,128]{1,0:T(8,128)}, f32[3600,128]{1,0:T(8,128)}, u32[]{:S(2)}, u32[]{:S(2)}) collective-permute-start(f32[3600,128]{1,0:T(8,128)} %collective-permute-done.1.refs_8_), channel_id=1, source_target_pairs={{0,1},{1,0},{2,3},{3,2},{4,5},{5,4},{6,7},{7,6},{8,9},{9,8},{10,11... | collective-permute-start | bytes 5529608 | tf_op jit(solution)/shard_map/ppermute | solution.py:150
  173.3 51.4 %collective-permute-start.6 = (f32[3600,128]{1,0:T(8,128)}, f32[3600,128]{1,0:T(8,128)}, u32[]{:S(2)}, u32[]{:S(2)}) collective-permute-start(f32[3600,128]{1,0:T(8,128)} %collective-permute-done.refs_4_), channel_id=1, source_target_pairs={{0,1},{1,0},{2,3},{3,2},{4,5},{5,4},{6,7},{7,6},{8,9},{9,8},{10,11... | collective-permute-start | bytes 5529608 | tf_op jit(solution)/shard_map/ppermute | solution.py:150
  221.8 37.9 %collective-permute-start.3 = (f32[3600,128]{1,0:T(8,128)}, f32[3600,128]{1,0:T(8,128)S(1)}, u32[]{:S(2)}, u32[]{:S(2)}) collective-permute-start(f32[3600,128]{1,0:T(8,128)} %shard_map.31.refs_1_), channel_id=1, source_target_pairs={{0,2},{1,3},{2,0},{3,1},{4,6},{5,7},{6,4},{7,5},{8,10},{9,11},{10,... | collective-permute-start | bytes 5529608 | tf_op jit(solution)/shard_map/ppermute | solution.py:150
  223.3 38.3 %collective-permute-start.4 = (f32[3600,128]{1,0:T(8,128)}, f32[3600,128]{1,0:T(8,128)}, u32[]{:S(2)}, u32[]{:S(2)}) collective-permute-start(f32[3600,128]{1,0:T(8,128)} %shard_map.31.refs_1_), channel_id=1, source_target_pairs={{0,4},{1,5},{2,6},{3,7},{4,0},{5,1},{6,2},{7,3},{8,12},{9,13},{10,... | collective-permute-start | bytes 5529608 | tf_op jit(solution)/shard_map/ppermute | solution.py:150
  224.2 37.5 %collective-permute-start.9 = (f32[3600,128]{1,0:T(8,128)}, f32[3600,128]{1,0:T(8,128)S(1)}, u32[]{:S(2)}, u32[]{:S(2)}) collective-permute-start(f32[3600,128]{1,0:T(8,128)} %shard_map.31.refs_1_), channel_id=1, source_target_pairs={{0,1},{1,0},{2,3},{3,2},{4,5},{5,4},{6,7},{7,6},{8,9},{9,8},{10,11... | collective-permute-start | bytes 5529608 | tf_op jit(solution)/shard_map/ppermute | solution.py:150
  224.2 38.7 %collective-permute-start.8 = (f32[3600,128]{1,0:T(8,128)}, f32[3600,128]{1,0:T(8,128)}, u32[]{:S(2)}, u32[]{:S(2)}) collective-permute-start(f32[3600,128]{1,0:T(8,128)} %collective-permute-done.2.refs_12_), channel_id=1, source_target_pairs={{0,1},{1,0},{2,3},{3,2},{4,5},{5,4},{6,7},{7,6},{8,9},{9,8},{10,11... | collective-permute-start | bytes 5529608 | tf_op jit(solution)/shard_map/ppermute | solution.py:150
  259.7 25.3 %copy-start.2 = (f32[3600,128]{1,0:T(8,128)}, f32[3600,128]{1,0:T(8,128)S(1)}, u32[]{:S(2)}) copy-start(f32[3600,128]{1,0:T(8,128)S(1)} %collective-permute-done.3.refs_5_) | copy-start | bytes 5529604
  263.0 22.0 %slice-start.2 = ((f32[512,1920]{1,0:T(8,128)}), f32[512,256]{1,0:T(8,128)S(1)}, s32[]{:S(2)}) async-start(f32[512,1920]{1,0:T(8,128)} %param.3), calls=%async_computation.7 | async-start | bytes 1048576 | tf_op jit(solution)/shard_map/slice | solution.py:154
  263.0 18.3 %collective-permute-start.12 = (f32[1800,128]{1,0:T(8,128)S(1)}, f32[1800,128]{1,0:T(8,128)S(1)}, u32[]{:S(2)}, u32[]{:S(2)}) collective-permute-start(f32[1800,128]{1,0:T(8,128)S(1)} %slice.27), channel_id=1, source_target_pairs={{0,4},{1,5},{2,6},{3,7},{4,0},{5,1},{6,2},{7,3},{8,12},{9,13},{10,... | collective-permute-start | bytes 2764808 | tf_op jit(solution)/shard_map/ppermute | solution.py:150
  266.0 17.9 %collective-permute-start.13 = (f32[1800,128]{1,0:T(8,128)S(1)}, f32[1800,128]{1,0:T(8,128)S(1)}, u32[]{:S(2)}, u32[]{:S(2)}) collective-permute-start(f32[1800,128]{1,0:T(8,128)S(1)} %slice.28), channel_id=1, source_target_pairs={{0,2},{1,3},{2,0},{3,1},{4,6},{5,7},{6,4},{7,5},{8,10},{9,11},{10,... | collective-permute-start | bytes 2764808 | tf_op jit(solution)/shard_map/ppermute | solution.py:150
  266.8 19.0 %collective-permute-start.10 = (f32[3600,128]{1,0:T(8,128)S(1)}, f32[3600,128]{1,0:T(8,128)}, u32[]{:S(2)}, u32[]{:S(2)}) collective-permute-start(f32[3600,128]{1,0:T(8,128)S(1)} %collective-permute-done.3.refs_5_), channel_id=1, source_target_pairs={{0,1},{1,0},{2,3},{3,2},{4,5},{5,4},{6,7},{7,6},{8,9},{9,8},{10,11... | collective-permute-start | bytes 5529608 | tf_op jit(solution)/shard_map/ppermute | solution.py:150
  266.8 19.0 %collective-permute-start.11 = (f32[3600,128]{1,0:T(8,128)}, f32[3600,128]{1,0:T(8,128)}, u32[]{:S(2)}, u32[]{:S(2)}) collective-permute-start(f32[3600,128]{1,0:T(8,128)} %collective-permute-done.4.refs_9_), channel_id=1, source_target_pairs={{0,1},{1,0},{2,3},{3,2},{4,5},{5,4},{6,7},{7,6},{8,9},{9,8},{10,11... | collective-permute-start | bytes 5529608 | tf_op jit(solution)/shard_map/ppermute | solution.py:150
  284.9 4.1 collective-permute-start.14
  400.1 13.3 %slice-start.3 = ((s8[14745600]{0:T(1024)(128)(4,1)}), s8[4194304]{0:T(1024)(128)(4,1)S(1)}, s32[]{:S(2)}) async-start(s8[14745600]{0:T(1024)(128)(4,1)} %bitcast.32), calls=%async_computation.8 | async-start | bytes 8388608
  402.2 11.2 %slice-start.4 = ((s8[14745600]{0:T(1024)(128)(4,1)}), s8[4194304]{0:T(1024)(128)(4,1)S(1)}, s32[]{:S(2)}) async-start(s8[14745600]{0:T(1024)(128)(4,1)} %bitcast.32), calls=%async_computation.9 | async-start | bytes 8388608
  (7 other events, 36.4 us)
Sparse Core Ops, SparseCore 0:
  9.7 224.6 all-gather.3
  236.0 98.6 all-gather.5
  336.3 44.5 all-gather.7

commit v5 on v3

--- a/solution.py
+++ b/solution.py
@@ -22,13 +22,15 @@
     )
 
 
-def chunks_of(columns):
-    if columns == 1920:
-        order = [(0, 1024), (1280, 640), (1024, 256)]
-        return [(start, width, width) for start, width in order]
+def chunks_of(columns, line):
+    if columns == 1920 and line == 4:
+        order = [(0, 896), (896, 512), (1408, 256), (1664, 256)]
+        *gathered, ringed = [(start, width, width) for start, width in order]
+        return gathered, ringed
     wide = [(n, WIDE, WIDE) for n in range(0, columns - WIDE + 1, WIDE)]
     start = len(wide) * WIDE
-    return wide + ([(start, columns - start, WIDE)] if start < columns else [])
+    rest = [(start, columns - start, WIDE)] if start < columns else []
+    return wide + rest, None
 
 
 def cut_kernel(t_ref, out_ref):
@@ -146,29 +148,41 @@
 def per_device(line, devices, amplitudes, integrals):
     columns = integrals.shape[1]
     rows = amplitudes.shape[0] // line
-    chunks = chunks_of(columns)
+    chunks, ringed = chunks_of(columns, line)
 
     def swap(x, mask):
         return lax.ppermute(x, "ka", [(d, d ^ mask) for d in range(devices)])
 
-    def gather(n, source):
-        start, width, _ = chunks[n]
+    def piece(chunk, source):
+        start, width, _ = chunk
         x = lax.slice_in_dim(source, start, start + width, axis=1)
         x = x.reshape(devices // line, line, 2, -1, width).swapaxes(1, 2)
-        return lax.all_gather(x.reshape(-1, width), "ga", axis=0, tiled=True)
-
-    source, amplitudes = tie(integrals, amplitudes)
-    gathered = [gather(0, source)]
+        return x.reshape(-1, width)
+
+    def gather(n, source):
+        return lax.all_gather(piece(chunks[n], source), "ga", axis=0, tiled=True)
+
+    def forward(x):
+        return lax.ppermute(x, "ga", [(n, (n + 1) % line) for n in range(line)])
+
+    gathered = []
+    ring = []
+    if ringed:
+        own, amplitudes = tie(piece(ringed, integrals), amplitudes)
+        ring = [own, forward(own)]
 
     held = []
     for half in range(2):
         blocks = cut(amplitudes.T, line, half)
         if half:
-            blocks, first, source = tie(blocks, first, integrals)
-            gathered.append(gather(1, source))
+            blocks, first, ring, source = tie(blocks, first, ring, integrals)
+            gathered.append(gather(0, source))
+            if ringed:
+                ring.append(forward(ring[-1]))
             held.append({0: turn(first)})
         blocks = lax.all_to_all(blocks, "ga", split_axis=0, concat_axis=0, tiled=True)
         first = blocks.reshape(-1, rows)
+    first, ring = tie(first, ring)
     held.append({0: turn(first)})
 
     masks = [1 << bit for bit in range(1, devices.bit_length() - 1)]
@@ -180,8 +194,8 @@
             across[1] = {0: swap(blocks[0], 1)}
         for level in range(1, len(masks) + 1):
             if half and level == 2:
-                held, across, source = tie(held, across, integrals)
-                gathered += [gather(n, source) for n in range(2, len(chunks))]
+                held, across, ring, source = tie(held, across, ring, integrals)
+                gathered += [gather(n, source) for n in range(1, len(chunks))]
                 blocks = held[1]
             if half and level == 2 == len(masks):
                 some = rows // 16 * 8
@@ -202,15 +216,28 @@
     ]
 
     place = lax.axis_index("ka").astype(jnp.int32)
+    if ringed:
+        place, ring, parts = tie(place, ring, parts)
+        ring.append(forward(ring[-1]))
     out, whole = product(place.reshape(1), parts, gathered[0], chunks[0], columns)
-    for (start, _, _), w in zip(chunks[1:], gathered[1:]):
+
+    def rest(out, chunk, w):
         ladder = jnp.dot(
-            whole,
-            w,
-            precision=lax.Precision.HIGH,
-            preferred_element_type=jnp.float32,
+            whole, w, precision=lax.Precision.HIGH, preferred_element_type=jnp.float32
         )
-        out = lax.dynamic_update_slice_in_dim(out, 0.5 * ladder, start, axis=1)
+        return lax.dynamic_update_slice_in_dim(out, 0.5 * ladder, chunk[0], axis=1)
+
+    if ringed:
+        here = lax.axis_index("ga").astype(jnp.uint32)
+        size = own.shape[0]
+        w = jnp.zeros((line * size, ringed[1]), jnp.float32)
+        for n, shard in enumerate(ring):
+            row = lax.rem(here + jnp.uint32(line - n), jnp.uint32(line))
+            row = row * jnp.uint32(size)
+            w = lax.dynamic_update_slice(w, shard, (row, jnp.uint32(0)))
+        out = rest(out, ringed, w)
+    for chunk, w in zip(chunks[1:], gathered[1:]):
+        out = rest(out, chunk, w)
     return out
 
 

time: 429 us -> 470 us (1.096)
  waiting for transfers between devices: 228 us -> 265 us
    ppermute x0 -> x3, waiting for transfers between devices: none -> 172 us  [forward(): return lax.ppermute(x, 'ga', [(n, (n + 1) % line) for n in range(line)])]
    all_to_all x2, waiting for transfers between devices: 131 us -> 0.01 us  [per_device(): lax.all_to_all(blocks, 'ga', split_axis=0, concat_axis=0, tiled=True)]
    dot_general x2 -> x3, matrix products: 61.1 us -> 65.6 us  [rest(): jnp.dot(whole, w, precision=lax.Precision.HIGH, preferred_element_type=jn...]
  transfers between devices with their start and end apart: 20 -> 23, of which waited for: 9 -> 10; matrix products, arithmetic and copies ran while one was open for 11% -> 12% of each run, Pallas kernels for 20% -> 17%
where the time goes in v5:
time: 470 us; the launch traced here: 469 us
  waiting for transfers between devices  265 us (56%)
  Pallas kernels  84.9 us (18%)
  matrix products  65.6 us (14%)
  starting transfers between devices  23.8 us (5%)
  local copies, waits for them, and re-layouts  15.8 us (3%)
  between operations  13.2 us (3%)
    ppermute x3, waiting for transfers between devices, forward(): return lax.ppermute(x, 'ga', [(n, (n + 1) % line) for n in range(line)])  172 us
    ppermute x15, waiting for transfers between devices, swap(): return lax.ppermute(x, 'ka', [(d, d ^ mask) for d in range(devices)])  93.6 us
    pallas_call x1, Pallas kernels, product(): pl.pallas_call(functools.partial(product_kernel, len(parts) // 2), grid_s...  66.7 us
    dot_general x3, matrix products, rest(): jnp.dot(whole, w, precision=lax.Precision.HIGH, preferred_element_type=jn...  65.6 us
    pallas_call x2, Pallas kernels, turn(): pl.pallas_call(turn_kernel, grid=(pl.cdiv(rows, width),), in_specs=[pl.Bl...  11.7 us
    ppermute x15, starting transfers between devices, swap(): return lax.ppermute(x, 'ka', [(d, d ^ mask) for d in range(devices)])  11.4 us
    all_to_all x2, starting transfers between devices, per_device(): lax.all_to_all(blocks, 'ga', split_axis=0, concat_axis=0, tiled=True)  10.9 us
  transfers between devices with their start and end apart: 23, of which 10 were waited for; matrix products, arithmetic and copies ran while one was open for 12% of the time, Pallas kernels for 17%

profile of v5, /device:TPU:16, one launch (start us, length us, event | category | flops | bytes accessed | tf_op | source)
XLA Modules:
  0.0 468.6 jit_solution(8995220646954839031)
XLA Ops:
  7.7 3.2 shard_map.29
  10.8 5.2 %all-to-all-start = ((f32[4,32,3600]{2,1,0:T(8,128)}), f32[4,32,3600]{2,1,0:T(8,128)S(1)}, u32[]{:S(2)}, u32[]{:S(2)}) async-start(f32[4,32,3600]{2,1,0:T(8,128)} %shard_map.29), calls=%async_computation | async-start | bytes 3801088 | tf_op jit(solution)/shard_map/all_to_all | solution.py:183
  17.5 3.2 shard_map.28
  20.7 48.2 %collective-permute-done = f32[512,256]{1,0:T(8,128)S(1)} collective-permute-done((f32[512,256]{1,0:T(8,128)S(1)}, f32[512,256]{1,0:T(8,128)S(1)}, u32[]{:S(2)}, u32[]{:S(2)}) %collective-permute-start) | collective-permute-done | bytes 524320 | tf_op jit(solution)/shard_map/ppermute | solution.py:166
  69.0 2.4 slice-done
  72.7 5.8 %shard_map.30.refs_0_ = f32[3600,128]{1,0:T(8,128)} custom-call(f32[128,3600]{1,0:T(8,128)} %bitcast.29), custom_call_target="tpu_custom_call" | custom-call | bytes 3686400 | tf_op jit(solution)/shard_map/pallas_call | solution.py:63
  78.6 1.5 collective-permute-start.2
  80.1 1.5 collective-permute-start.1
  81.6 5.7 %all-to-all-start.1 = ((f32[4,32,3600]{2,1,0:T(8,128)}), f32[4,32,3600]{2,1,0:T(8,128)S(1)}, u32[]{:S(2)}, u32[]{:S(2)}) async-start(f32[4,32,3600]{2,1,0:T(8,128)} %shard_map.28), calls=%async_computation.1 | async-start | bytes 3801088 | tf_op jit(solution)/shard_map/all_to_all | solution.py:183
  87.3 32.3 %collective-permute-done.2.refs_8_ = f32[3600,128]{1,0:T(8,128)} collective-permute-done((f32[3600,128]{1,0:T(8,128)}, f32[3600,128]{1,0:T(8,128)}, u32[]{:S(2)}, u32[]{:S(2)}) %collective-permute-start.2) | collective-permute-done | bytes 1843232 | tf_op jit(solution)/shard_map/ppermute | solution.py:154
  119.6 1.5 collective-permute-start.3
  121.9 90.3 %collective-permute-done.4 = f32[512,256]{1,0:T(8,128)} collective-permute-done((f32[512,256]{1,0:T(8,128)S(1)}, f32[512,256]{1,0:T(8,128)}, u32[]{:S(2)}, u32[]{:S(2)}) %collective-permute-start.4) | collective-permute-done | bytes 524320 | tf_op jit(solution)/shard_map/ppermute | solution.py:166
  213.5 5.9 %shard_map.31.refs_1_ = f32[3600,128]{1,0:T(8,128)} custom-call(f32[128,3600]{1,0:T(8,128)} %bitcast.28), custom_call_target="tpu_custom_call" | custom-call | bytes 3686400 | tf_op jit(solution)/shard_map/pallas_call | solution.py:63
  219.4 1.6 collective-permute-start.5
  221.0 1.5 collective-permute-start.6
  223.0 37.8 %collective-permute-done.5.refs_5_ = f32[3600,128]{1,0:T(8,128)S(1)} collective-permute-done((f32[3600,128]{1,0:T(8,128)}, f32[3600,128]{1,0:T(8,128)S(1)}, u32[]{:S(2)}, u32[]{:S(2)}) %collective-permute-start.5) | collective-permute-done | bytes 1843232 | tf_op jit(solution)/shard_map/ppermute | solution.py:154
  263.5 1.5 collective-permute-start.14
  267.6 16.3 %collective-permute-done.14 = f32[1800,128]{1,0:T(8,128)S(1)} collective-permute-done((f32[1800,128]{1,0:T(8,128)S(1)}, f32[1800,128]{1,0:T(8,128)S(1)}, u32[]{:S(2)}, u32[]{:S(2)}) %collective-permute-start.14) | collective-permute-done | bytes 921632 | tf_op jit(solution)/shard_map/ppermute | solution.py:154
  287.4 4.0 collective-permute-done.16.refs_15_
  295.7 33.0 %collective-permute-done.17 = f32[512,256]{1,0:T(8,128)} collective-permute-done((f32[512,256]{1,0:T(8,128)}, f32[512,256]{1,0:T(8,128)}, u32[]{:S(2)}, u32[]{:S(2)}) %collective-permute-start.17) | collective-permute-done | bytes 524320 | tf_op jit(solution)/shard_map/ppermute | solution.py:166
  329.8 66.7 %shard_map.32 = (f32[3600,1920]{1,0:T(8,128)}, f32[3600,2048]{1,0:T(8,128)}) custom-call(s32[1]{0:T(128)} %bitcast.6.place_ref, f32[3600,128]{1,0:T(8,128)} %shard_map.30.refs_0_, f32[3600,128]{1,0:T(8,128)} %shard_map.31.refs_1_, f32[3600,128]{1,0:T(8,128)} %collective-permute-done.7.refs_2_, f32[3600,128]{1,0:T(8,128)} %collective-permute-done.11.refs_3_, ...), custom_call_target="tpu_custom_call" | custom-call | flops 39636172800 | bytes 79224832 | tf_op jit(solution)/shard_map/pallas_call | solution.py:112
  396.5 17.4 %fusion.1 = f32[3600,1920]{1,0:T(8,128)} fusion(f32[3600,1920]{1,0:T(8,128)} %get-tuple-element.97, f32[3600,2048]{1,0:T(8,128)} %get-tuple-element.98, f32[2048,256]{1,0:T(8,128)S(1)} %constant_dynamic-update-slice_fusion.2), kind=kOutput, calls=%fused_computation.4 | convolution fusion | flops 11325542400 | bytes 35274752 | tf_op jit(solution)/shard_map/dot_general | solution.py:225
  413.9 28.9 %multiply_dynamic-update-slice_fusion = f32[3600,1920]{1,0:T(8,128)} fusion(f32[3600,1920]{1,0:T(8,128)} %fusion.1, f32[3600,2048]{1,0:T(8,128)} %get-tuple-element.98, f32[2048,512]{1,0:T(8,128)} %all-gather.6.cloned.1.call-done), kind=kOutput, calls=%fused_computation | convolution fusion | flops 22651084800 | bytes 41058304 | tf_op jit(solution)/shard_map/dot_general | solution.py:225
  442.9 19.2 %fusion = f32[3600,1920]{1,0:T(8,128)} fusion(f32[3600,1920]{1,0:T(8,128)} %multiply_dynamic-update-slice_fusion, f32[3600,2048]{1,0:T(8,128)} %get-tuple-element.98, f32[2048,256]{1,0:T(8,128)} %all-gather.8.cloned.1.call-done), kind=kOutput, calls=%fused_computation.2 | convolution fusion | flops 11325542400 | bytes 35274752 | tf_op jit(solution)/shard_map/dot_general | solution.py:225
  (65 shorter events, 20.5 us)
Async XLA Ops:
  10.8 58.1 %all-to-all-start = ((f32[4,32,3600]{2,1,0:T(8,128)}), f32[4,32,3600]{2,1,0:T(8,128)S(1)}, u32[]{:S(2)}, u32[]{:S(2)}) async-start(f32[4,32,3600]{2,1,0:T(8,128)} %shard_map.29), calls=%async_computation | async-start | bytes 3801088 | tf_op jit(solution)/shard_map/all_to_all | solution.py:183
  16.1 313.7 %all-gather.4.cloned.1.call-start = ((), (), s32[]{:S(2)}) async-start(), calls=%async_computation.2 | async-start | bytes 9175040 | tf_op jit(solution)/shard_map/all_gather | solution.py:163
  16.1 52.9 %collective-permute-start = (f32[512,256]{1,0:T(8,128)S(1)}, f32[512,256]{1,0:T(8,128)S(1)}, u32[]{:S(2)}, u32[]{:S(2)}) collective-permute-start(f32[512,256]{1,0:T(8,128)S(1)} %bitcast.35), channel_id=1, source_target_pairs={{0,8},{8,16},{16,24},{24,0},{1,9},{9,17},{17,25},{25,1},{2,10},{10... | collective-permute-start | bytes 1572872 | tf_op jit(solution)/shard_map/ppermute | solution.py:166
  69.0 52.5 %copy-start.2 = (f32[512,256]{1,0:T(8,128)}, f32[512,256]{1,0:T(8,128)S(1)}, u32[]{:S(2)}) copy-start(f32[512,256]{1,0:T(8,128)S(1)} %collective-permute-done) | copy-start | bytes 1572868
  78.6 41.1 %collective-permute-start.2 = (f32[3600,128]{1,0:T(8,128)}, f32[3600,128]{1,0:T(8,128)}, u32[]{:S(2)}, u32[]{:S(2)}) collective-permute-start(f32[3600,128]{1,0:T(8,128)} %shard_map.30.refs_0_), channel_id=1, source_target_pairs={{0,4},{1,5},{2,6},{3,7},{4,0},{5,1},{6,2},{7,3},{8,12},{9,13},{10,... | collective-permute-start | bytes 5529608 | tf_op jit(solution)/shard_map/ppermute | solution.py:154
  80.1 41.3 %collective-permute-start.1 = (f32[3600,128]{1,0:T(8,128)}, f32[3600,128]{1,0:T(8,128)}, u32[]{:S(2)}, u32[]{:S(2)}) collective-permute-start(f32[3600,128]{1,0:T(8,128)} %shard_map.30.refs_0_), channel_id=1, source_target_pairs={{0,2},{1,3},{2,0},{3,1},{4,6},{5,7},{6,4},{7,5},{8,10},{9,11},{10,... | collective-permute-start | bytes 5529608 | tf_op jit(solution)/shard_map/ppermute | solution.py:154
  81.6 130.7 %all-to-all-start.1 = ((f32[4,32,3600]{2,1,0:T(8,128)}), f32[4,32,3600]{2,1,0:T(8,128)S(1)}, u32[]{:S(2)}, u32[]{:S(2)}) async-start(f32[4,32,3600]{2,1,0:T(8,128)} %shard_map.28), calls=%async_computation.1 | async-start | bytes 3801088 | tf_op jit(solution)/shard_map/all_to_all | solution.py:183
  87.3 326.6 %all-gather.6.cloned.1.call-start = ((), (), s32[]{:S(2)}) async-start(), calls=%async_computation.3 | async-start | bytes 5242880 | tf_op jit(solution)/shard_map/all_gather | solution.py:163
  87.3 133.7 %collective-permute-start.7 = (f32[3600,128]{1,0:T(8,128)}, f32[3600,128]{1,0:T(8,128)}, u32[]{:S(2)}, u32[]{:S(2)}) collective-permute-start(f32[3600,128]{1,0:T(8,128)} %shard_map.30.refs_0_), channel_id=1, source_target_pairs={{0,1},{1,0},{2,3},{3,2},{4,5},{5,4},{6,7},{7,6},{8,9},{9,8},{10,11... | collective-permute-start | bytes 5529608 | tf_op jit(solution)/shard_map/ppermute | solution.py:154
  119.6 102.9 %collective-permute-start.3 = (f32[3600,128]{1,0:T(8,128)}, f32[3600,128]{1,0:T(8,128)}, u32[]{:S(2)}, u32[]{:S(2)}) collective-permute-start(f32[3600,128]{1,0:T(8,128)} %collective-permute-done.2.refs_8_), channel_id=1, source_target_pairs={{0,2},{1,3},{2,0},{3,1},{4,6},{5,7},{6,4},{7,5},{8,10},{9,11},{10,... | collective-permute-start | bytes 5529608 | tf_op jit(solution)/shard_map/ppermute | solution.py:154
  121.4 101.1 %collective-permute-start.8 = (f32[3600,128]{1,0:T(8,128)}, f32[3600,128]{1,0:T(8,128)}, u32[]{:S(2)}, u32[]{:S(2)}) collective-permute-start(f32[3600,128]{1,0:T(8,128)} %collective-permute-done.1.refs_4_), channel_id=1, source_target_pairs={{0,1},{1,0},{2,3},{3,2},{4,5},{5,4},{6,7},{7,6},{8,9},{9,8},{10,11... | collective-permute-start | bytes 5529608 | tf_op jit(solution)/shard_map/ppermute | solution.py:154
  121.4 90.8 %collective-permute-start.4 = (f32[512,256]{1,0:T(8,128)S(1)}, f32[512,256]{1,0:T(8,128)}, u32[]{:S(2)}, u32[]{:S(2)}) collective-permute-start(f32[512,256]{1,0:T(8,128)S(1)} %collective-permute-done), channel_id=1, source_target_pairs={{0,8},{8,16},{16,24},{24,0},{1,9},{9,17},{17,25},{25,1},{2,10},{10... | collective-permute-start | bytes 1572872 | tf_op jit(solution)/shard_map/ppermute | solution.py:166
  121.4 101.6 %collective-permute-start.9 = (f32[3600,128]{1,0:T(8,128)}, f32[3600,128]{1,0:T(8,128)}, u32[]{:S(2)}, u32[]{:S(2)}) collective-permute-start(f32[3600,128]{1,0:T(8,128)} %collective-permute-done.2.refs_8_), channel_id=1, source_target_pairs={{0,1},{1,0},{2,3},{3,2},{4,5},{5,4},{6,7},{7,6},{8,9},{9,8},{10,11... | collective-permute-start | bytes 5529608 | tf_op jit(solution)/shard_map/ppermute | solution.py:154
  219.4 41.5 %collective-permute-start.5 = (f32[3600,128]{1,0:T(8,128)}, f32[3600,128]{1,0:T(8,128)S(1)}, u32[]{:S(2)}, u32[]{:S(2)}) collective-permute-start(f32[3600,128]{1,0:T(8,128)} %shard_map.31.refs_1_), channel_id=1, source_target_pairs={{0,2},{1,3},{2,0},{3,1},{4,6},{5,7},{6,4},{7,5},{8,10},{9,11},{10,... | collective-permute-start | bytes 5529608 | tf_op jit(solution)/shard_map/ppermute | solution.py:154
  221.0 41.3 %collective-permute-start.6 = (f32[3600,128]{1,0:T(8,128)}, f32[3600,128]{1,0:T(8,128)}, u32[]{:S(2)}, u32[]{:S(2)}) collective-permute-start(f32[3600,128]{1,0:T(8,128)} %shard_map.31.refs_1_), channel_id=1, source_target_pairs={{0,4},{1,5},{2,6},{3,7},{4,0},{5,1},{6,2},{7,3},{8,12},{9,13},{10,... | collective-permute-start | bytes 5529608 | tf_op jit(solution)/shard_map/ppermute | solution.py:154
  222.5 39.8 %collective-permute-start.11 = (f32[3600,128]{1,0:T(8,128)}, f32[3600,128]{1,0:T(8,128)}, u32[]{:S(2)}, u32[]{:S(2)}) collective-permute-start(f32[3600,128]{1,0:T(8,128)} %shard_map.31.refs_1_), channel_id=1, source_target_pairs={{0,1},{1,0},{2,3},{3,2},{4,5},{5,4},{6,7},{7,6},{8,9},{9,8},{10,11... | collective-permute-start | bytes 5529608 | tf_op jit(solution)/shard_map/ppermute | solution.py:154
  222.5 39.8 %collective-permute-start.10 = (f32[3600,128]{1,0:T(8,128)}, f32[3600,128]{1,0:T(8,128)}, u32[]{:S(2)}, u32[]{:S(2)}) collective-permute-start(f32[3600,128]{1,0:T(8,128)} %collective-permute-done.3.refs_12_), channel_id=1, source_target_pairs={{0,1},{1,0},{2,3},{3,2},{4,5},{5,4},{6,7},{7,6},{8,9},{9,8},{10,11... | collective-permute-start | bytes 5529608 | tf_op jit(solution)/shard_map/ppermute | solution.py:154
  263.4 179.5 %all-gather.8.cloned.1.call-start = ((), (), s32[]{:S(2)}) async-start(), calls=%async_computation.4 | async-start | bytes 2621440 | tf_op jit(solution)/shard_map/all_gather | solution.py:163
  263.5 20.3 %collective-permute-start.14 = (f32[1800,128]{1,0:T(8,128)S(1)}, f32[1800,128]{1,0:T(8,128)S(1)}, u32[]{:S(2)}, u32[]{:S(2)}) collective-permute-start(f32[1800,128]{1,0:T(8,128)S(1)} %slice.19), channel_id=1, source_target_pairs={{0,4},{1,5},{2,6},{3,7},{4,0},{5,1},{6,2},{7,3},{8,12},{9,13},{10,... | collective-permute-start | bytes 2764808 | tf_op jit(solution)/shard_map/ppermute | solution.py:154
  266.3 20.0 %collective-permute-start.15 = (f32[1800,128]{1,0:T(8,128)S(1)}, f32[1800,128]{1,0:T(8,128)S(1)}, u32[]{:S(2)}, u32[]{:S(2)}) collective-permute-start(f32[1800,128]{1,0:T(8,128)S(1)} %slice.20), channel_id=1, source_target_pairs={{0,2},{1,3},{2,0},{3,1},{4,6},{5,7},{6,4},{7,5},{8,10},{9,11},{10,... | collective-permute-start | bytes 2764808 | tf_op jit(solution)/shard_map/ppermute | solution.py:154
  267.0 20.3 %collective-permute-start.12 = (f32[3600,128]{1,0:T(8,128)}, f32[3600,128]{1,0:T(8,128)}, u32[]{:S(2)}, u32[]{:S(2)}) collective-permute-start(f32[3600,128]{1,0:T(8,128)} %copy-done.4), channel_id=1, source_target_pairs={{0,1},{1,0},{2,3},{3,2},{4,5},{5,4},{6,7},{7,6},{8,9},{9,8},{10,11... | collective-permute-start | bytes 5529608 | tf_op jit(solution)/shard_map/ppermute | solution.py:154
  267.0 20.3 %collective-permute-start.13 = (f32[3600,128]{1,0:T(8,128)}, f32[3600,128]{1,0:T(8,128)}, u32[]{:S(2)}, u32[]{:S(2)}) collective-permute-start(f32[3600,128]{1,0:T(8,128)} %collective-permute-done.6.refs_9_), channel_id=1, source_target_pairs={{0,1},{1,0},{2,3},{3,2},{4,5},{5,4},{6,7},{7,6},{8,9},{9,8},{10,11... | collective-permute-start | bytes 5529608 | tf_op jit(solution)/shard_map/ppermute | solution.py:154
  287.4 4.0 collective-permute-start.16
  291.4 37.3 %collective-permute-start.17 = (f32[512,256]{1,0:T(8,128)}, f32[512,256]{1,0:T(8,128)}, u32[]{:S(2)}, u32[]{:S(2)}) collective-permute-start(f32[512,256]{1,0:T(8,128)} %collective-permute-done.4), channel_id=1, source_target_pairs={{0,8},{8,16},{16,24},{24,0},{1,9},{9,17},{17,25},{25,1},{2,10},{10... | collective-permute-start | bytes 1572872 | tf_op jit(solution)/shard_map/ppermute | solution.py:166
  (8 other events, 87.4 us)
Sparse Core Ops, SparseCore 0:
  72.8 181.1 all-gather.3
  263.5 89.5 all-gather.5
  354.8 44.5 all-gather.7

commit v6 on v3

--- a/solution.py
+++ b/solution.py
@@ -151,21 +151,21 @@
     def swap(x, mask):
         return lax.ppermute(x, "ka", [(d, d ^ mask) for d in range(devices)])
 
-    def gather(n, source):
-        start, width, _ = chunks[n]
-        x = lax.slice_in_dim(source, start, start + width, axis=1)
+    pieces = []
+    for start, width, _ in chunks:
+        x = lax.slice_in_dim(integrals, start, start + width, axis=1)
         x = x.reshape(devices // line, line, 2, -1, width).swapaxes(1, 2)
-        return lax.all_gather(x.reshape(-1, width), "ga", axis=0, tiled=True)
-
-    source, amplitudes = tie(integrals, amplitudes)
-    gathered = [gather(0, source)]
+        pieces.append(x.reshape(-1, width))
+
+    def gather(x):
+        return lax.all_gather(x, "ga", axis=0, tiled=True)
 
     held = []
     for half in range(2):
         blocks = cut(amplitudes.T, line, half)
         if half:
-            blocks, first, source = tie(blocks, first, integrals)
-            gathered.append(gather(1, source))
+            blocks, first, *pieces[:2] = tie(blocks, first, *pieces[:2])
+            gathered = [gather(x) for x in pieces[:2]]
             held.append({0: turn(first)})
         blocks = lax.all_to_all(blocks, "ga", split_axis=0, concat_axis=0, tiled=True)
         first = blocks.reshape(-1, rows)
@@ -180,8 +180,8 @@
             across[1] = {0: swap(blocks[0], 1)}
         for level in range(1, len(masks) + 1):
             if half and level == 2:
-                held, across, source = tie(held, across, integrals)
-                gathered += [gather(n, source) for n in range(2, len(chunks))]
+                held, across, pieces = tie(held, across, pieces)
+                gathered += [gather(x) for x in pieces[2:]]
                 blocks = held[1]
             if half and level == 2 == len(masks):
                 some = rows // 16 * 8

time: 429 us -> 420 us (0.979)
    all_to_all x2, waiting for transfers between devices: 131 us -> 82.4 us  [per_device(): lax.all_to_all(blocks, 'ga', split_axis=0, concat_axis=0, tiled=True)]
    all_gather x3, waiting for transfers between devices: 0.02 us -> 39.4 us  [gather(): return lax.all_gather(x, 'ga', axis=0, tiled=True)]
    ppermute x15, waiting for transfers between devices: 96.3 us -> 104 us  [swap(): return lax.ppermute(x, 'ka', [(d, d ^ mask) for d in range(devices)])]
  transfers between devices with their start and end apart: 20 -> 20, of which waited for: 9 -> 12; matrix products, arithmetic and copies ran while one was open for 11% -> 12% of each run, Pallas kernels for 20% -> 20%
where the time goes in v6:
time: 420 us; the launch traced here: 416 us
  waiting for transfers between devices  226 us (54%)
  Pallas kernels  84.7 us (20%)
  matrix products  61.1 us (15%)
  starting transfers between devices  21 us (5%)
  between operations  13.2 us (3%)
  local copies, waits for them, and re-layouts  10.2 us (2%)
    ppermute x15, waiting for transfers between devices, swap(): return lax.ppermute(x, 'ka', [(d, d ^ mask) for d in range(devices)])  104 us
    all_to_all x2, waiting for transfers between devices, per_device(): lax.all_to_all(blocks, 'ga', split_axis=0, concat_axis=0, tiled=True)  82.4 us
    pallas_call x1, Pallas kernels, product(): pl.pallas_call(functools.partial(product_kernel, len(parts) // 2), grid_s...  66.6 us
    dot_general x2, matrix products, per_device(): jnp.dot(whole, w, precision=lax.Precision.HIGH, preferred_element_type=jn...  61.1 us
    all_gather x3, waiting for transfers between devices, gather(): return lax.all_gather(x, 'ga', axis=0, tiled=True)  39.4 us
    all_to_all x2, starting transfers between devices, per_device(): lax.all_to_all(blocks, 'ga', split_axis=0, concat_axis=0, tiled=True)  12.2 us
    pallas_call x2, Pallas kernels, turn(): pl.pallas_call(turn_kernel, grid=(pl.cdiv(rows, width),), in_specs=[pl.Bl...  11.7 us
    ppermute x15, starting transfers between devices, swap(): return lax.ppermute(x, 'ka', [(d, d ^ mask) for d in range(devices)])  8.77 us
  transfers between devices with their start and end apart: 20, of which 12 were waited for; matrix products, arithmetic and copies ran while one was open for 12% of the time, Pallas kernels for 20%

profile of v6, /device:TPU:16, one launch (start us, length us, event | category | flops | bytes accessed | tf_op | source)
XLA Modules:
  0.0 416.2 jit_solution(4395687730634752625)
XLA Ops:
  6.5 3.2 shard_map.29
  9.7 5.2 %all-to-all-start = ((f32[4,32,3600]{2,1,0:T(8,128)}), f32[4,32,3600]{2,1,0:T(8,128)}, u32[]{:S(2)}, u32[]{:S(2)}) async-start(f32[4,32,3600]{2,1,0:T(8,128)} %shard_map.29), calls=%async_computation | async-start | bytes 3801088 | tf_op jit(solution)/shard_map/all_to_all | solution.py:170
  14.9 3.2 shard_map.28
  18.2 1.6 slice-done
  23.0 32.7 %all-to-all-done = f32[4,32,3600]{2,1,0:T(8,128)} async-done(((f32[4,32,3600]{2,1,0:T(8,128)}), f32[4,32,3600]{2,1,0:T(8,128)}, u32[]{:S(2)}, u32[]{:S(2)}) %all-to-all-start) | async-done | bytes 1843232 | tf_op jit(solution)/shard_map/all_to_all | solution.py:170
  55.7 5.8 %shard_map.30.refs_0_ = f32[3600,128]{1,0:T(8,128)} custom-call(f32[128,3600]{1,0:T(8,128)} %bitcast.2.t_ref), custom_call_target="tpu_custom_call" | custom-call | bytes 3686400 | tf_op jit(solution)/shard_map/pallas_call | solution.py:61
  61.5 1.5 collective-permute-start.1
  63.0 7.0 %all-to-all-start.1 = ((f32[4,32,3600]{2,1,0:T(8,128)}), f32[4,32,3600]{2,1,0:T(8,128)S(1)}, u32[]{:S(2)}, u32[]{:S(2)}) async-start(f32[4,32,3600]{2,1,0:T(8,128)} %shard_map.28), calls=%async_computation.1 | async-start | bytes 3801088 | tf_op jit(solution)/shard_map/all_to_all | solution.py:170
  70.8 1.6 collective-permute-start
  72.4 30.6 %collective-permute-done.1.refs_8_ = f32[3600,128]{1,0:T(8,128)} collective-permute-done((f32[3600,128]{1,0:T(8,128)}, f32[3600,128]{1,0:T(8,128)}, u32[]{:S(2)}, u32[]{:S(2)}) %collective-permute-start.1) | collective-permute-done | bytes 1843232 | tf_op jit(solution)/shard_map/ppermute | solution.py:152
  103.0 1.5 collective-permute-start.2
  104.5 9.8 %collective-permute-done.refs_4_ = f32[3600,128]{1,0:T(8,128)} collective-permute-done((f32[3600,128]{1,0:T(8,128)}, f32[3600,128]{1,0:T(8,128)}, u32[]{:S(2)}, u32[]{:S(2)}) %collective-permute-start) | collective-permute-done | bytes 1843232 | tf_op jit(solution)/shard_map/ppermute | solution.py:152
  114.3 49.7 %all-to-all-done.1 = f32[4,32,3600]{2,1,0:T(8,128)S(1)} async-done(((f32[4,32,3600]{2,1,0:T(8,128)}), f32[4,32,3600]{2,1,0:T(8,128)S(1)}, u32[]{:S(2)}, u32[]{:S(2)}) %all-to-all-start.1) | async-done | bytes 1843232 | tf_op jit(solution)/shard_map/all_to_all | solution.py:170
  165.3 5.9 %shard_map.31.refs_1_ = f32[3600,128]{1,0:T(8,128)} custom-call(f32[128,3600]{1,0:T(8,128)} %bitcast.26), custom_call_target="tpu_custom_call" | custom-call | bytes 3686400 | tf_op jit(solution)/shard_map/pallas_call | solution.py:61
  171.1 1.5 collective-permute-start.3
  174.7 38.8 %collective-permute-done.3.refs_5_ = f32[3600,128]{1,0:T(8,128)S(1)} collective-permute-done((f32[3600,128]{1,0:T(8,128)}, f32[3600,128]{1,0:T(8,128)S(1)}, u32[]{:S(2)}, u32[]{:S(2)}) %collective-permute-start.3) | collective-permute-done | bytes 1843232 | tf_op jit(solution)/shard_map/ppermute | solution.py:152
  217.6 18.6 %collective-permute-done.12 = f32[1800,128]{1,0:T(8,128)S(1)} collective-permute-done((f32[1800,128]{1,0:T(8,128)S(1)}, f32[1800,128]{1,0:T(8,128)S(1)}, u32[]{:S(2)}, u32[]{:S(2)}) %collective-permute-start.12) | collective-permute-done | bytes 921632 | tf_op jit(solution)/shard_map/ppermute | solution.py:152
  238.6 4.1 collective-permute-done.14.refs_15_
  242.7 2.2 all-gather.4.cloned.1.call-done.refs_16_
  244.9 66.6 %shard_map.32 = (f32[3600,1920]{1,0:T(8,128)}, f32[3600,2048]{1,0:T(8,128)}) custom-call(s32[1]{0:T(128)} %bitcast.place_ref, f32[3600,128]{1,0:T(8,128)} %shard_map.30.refs_0_, f32[3600,128]{1,0:T(8,128)} %shard_map.31.refs_1_, f32[3600,128]{1,0:T(8,128)} %collective-permute-done.5.refs_2_, f32[3600,128]{1,0:T(8,128)} %collective-permute-done.9.refs_3_, ...), custom_call_target="tpu_custom_call" | custom-call | flops 45298483200 | bytes 82116608 | tf_op jit(solution)/shard_map/pallas_call | solution.py:110
  311.5 32.8 %all-gather.6.cloned.1.call-done = f32[2048,640]{1,0:T(8,128)} async-done(((f32[512,640]{1,0:T(8,128)}), f32[2048,640]{1,0:T(8,128)}) %all-gather.6.cloned.1.call-update) | async-done | bytes 5242896 | tf_op jit(solution)/shard_map/all_gather | solution.py:161
  344.3 41.8 %multiply_dynamic-update-slice_fusion = f32[3600,1920]{1,0:T(8,128)} fusion(f32[3600,1920]{1,0:T(8,128)} %get-tuple-element.40, f32[3600,2048]{1,0:T(8,128)} %get-tuple-element.41, f32[2048,640]{1,0:T(8,128)} %all-gather.6.cloned.1.call-done), kind=kOutput, calls=%fused_computation | convolution fusion | flops 28313856000 | bytes 43950080 | tf_op jit(solution)/shard_map/dot_general | solution.py:207
  386.1 4.4 %all-gather.8.cloned.1.call-done = f32[2048,256]{1,0:T(8,128)} async-done(((f32[512,256]{1,0:T(8,128)}), f32[2048,256]{1,0:T(8,128)}) %all-gather.8.cloned.1.call-update) | async-done | bytes 2097168 | tf_op jit(solution)/shard_map/all_gather | solution.py:161
  390.5 19.3 %fusion = f32[3600,1920]{1,0:T(8,128)} fusion(f32[3600,1920]{1,0:T(8,128)} %multiply_dynamic-update-slice_fusion, f32[3600,2048]{1,0:T(8,128)} %get-tuple-element.41, f32[2048,256]{1,0:T(8,128)} %all-gather.8.cloned.1.call-done), kind=kOutput, calls=%fused_computation.2 | convolution fusion | flops 11325542400 | bytes 35274752 | tf_op jit(solution)/shard_map/dot_general | solution.py:207
  (43 shorter events, 13.8 us)
Async XLA Ops:
  9.7 45.9 %all-to-all-start = ((f32[4,32,3600]{2,1,0:T(8,128)}), f32[4,32,3600]{2,1,0:T(8,128)}, u32[]{:S(2)}, u32[]{:S(2)}) async-start(f32[4,32,3600]{2,1,0:T(8,128)} %shard_map.29), calls=%async_computation | async-start | bytes 3801088 | tf_op jit(solution)/shard_map/all_to_all | solution.py:170
  14.9 229.9 %all-gather.4.cloned.1.call-start = ((), (), s32[]{:S(2)}) async-start(), calls=%async_computation.2 | async-start | bytes 10485760 | tf_op jit(solution)/shard_map/all_gather | solution.py:161
  18.2 1.6 slice-start
  19.8 1.9 slice-start.1
  61.5 41.5 %collective-permute-start.1 = (f32[3600,128]{1,0:T(8,128)}, f32[3600,128]{1,0:T(8,128)}, u32[]{:S(2)}, u32[]{:S(2)}) collective-permute-start(f32[3600,128]{1,0:T(8,128)} %shard_map.30.refs_0_), channel_id=1, source_target_pairs={{0,4},{1,5},{2,6},{3,7},{4,0},{5,1},{6,2},{7,3},{8,12},{9,13},{10,... | collective-permute-start | bytes 5529608 | tf_op jit(solution)/shard_map/ppermute | solution.py:152
  63.0 101.0 %all-to-all-start.1 = ((f32[4,32,3600]{2,1,0:T(8,128)}), f32[4,32,3600]{2,1,0:T(8,128)S(1)}, u32[]{:S(2)}, u32[]{:S(2)}) async-start(f32[4,32,3600]{2,1,0:T(8,128)} %shard_map.28), calls=%async_computation.1 | async-start | bytes 3801088 | tf_op jit(solution)/shard_map/all_to_all | solution.py:170
  70.0 274.2 %all-gather.6.cloned.1.call-start = ((), (), s32[]{:S(2)}) async-start(), calls=%async_computation.3 | async-start | bytes 6553600 | tf_op jit(solution)/shard_map/all_gather | solution.py:161
  70.8 319.7 %all-gather.8.cloned.1.call-start = ((), (), s32[]{:S(2)}) async-start(), calls=%async_computation.4 | async-start | bytes 2621440 | tf_op jit(solution)/shard_map/all_gather | solution.py:161
  70.8 43.5 %collective-permute-start = (f32[3600,128]{1,0:T(8,128)}, f32[3600,128]{1,0:T(8,128)}, u32[]{:S(2)}, u32[]{:S(2)}) collective-permute-start(f32[3600,128]{1,0:T(8,128)} %shard_map.30.refs_0_), channel_id=1, source_target_pairs={{0,2},{1,3},{2,0},{3,1},{4,6},{5,7},{6,4},{7,5},{8,10},{9,11},{10,... | collective-permute-start | bytes 5529608 | tf_op jit(solution)/shard_map/ppermute | solution.py:152
  72.4 100.3 %collective-permute-start.5 = (f32[3600,128]{1,0:T(8,128)}, f32[3600,128]{1,0:T(8,128)}, u32[]{:S(2)}, u32[]{:S(2)}) collective-permute-start(f32[3600,128]{1,0:T(8,128)} %shard_map.30.refs_0_), channel_id=1, source_target_pairs={{0,1},{1,0},{2,3},{3,2},{4,5},{5,4},{6,7},{7,6},{8,9},{9,8},{10,11... | collective-permute-start | bytes 5529608 | tf_op jit(solution)/shard_map/ppermute | solution.py:152
  103.0 70.3 %collective-permute-start.2 = (f32[3600,128]{1,0:T(8,128)}, f32[3600,128]{1,0:T(8,128)}, u32[]{:S(2)}, u32[]{:S(2)}) collective-permute-start(f32[3600,128]{1,0:T(8,128)} %collective-permute-done.1.refs_8_), channel_id=1, source_target_pairs={{0,2},{1,3},{2,0},{3,1},{4,6},{5,7},{6,4},{7,5},{8,10},{9,11},{10,... | collective-permute-start | bytes 5529608 | tf_op jit(solution)/shard_map/ppermute | solution.py:152
  104.5 68.9 %collective-permute-start.7 = (f32[3600,128]{1,0:T(8,128)}, f32[3600,128]{1,0:T(8,128)}, u32[]{:S(2)}, u32[]{:S(2)}) collective-permute-start(f32[3600,128]{1,0:T(8,128)} %collective-permute-done.1.refs_8_), channel_id=1, source_target_pairs={{0,1},{1,0},{2,3},{3,2},{4,5},{5,4},{6,7},{7,6},{8,9},{9,8},{10,11... | collective-permute-start | bytes 5529608 | tf_op jit(solution)/shard_map/ppermute | solution.py:152
  114.3 60.4 %collective-permute-start.6 = (f32[3600,128]{1,0:T(8,128)}, f32[3600,128]{1,0:T(8,128)}, u32[]{:S(2)}, u32[]{:S(2)}) collective-permute-start(f32[3600,128]{1,0:T(8,128)} %collective-permute-done.refs_4_), channel_id=1, source_target_pairs={{0,1},{1,0},{2,3},{3,2},{4,5},{5,4},{6,7},{7,6},{8,9},{9,8},{10,11... | collective-permute-start | bytes 5529608 | tf_op jit(solution)/shard_map/ppermute | solution.py:152
  165.3 8.6 %slice-start.2 = ((f32[512,1920]{1,0:T(8,128)}), f32[512,256]{1,0:T(8,128)S(1)}, s32[]{:S(2)}) async-start(f32[512,1920]{1,0:T(8,128)} %param.3), calls=%async_computation.7 | async-start | bytes 1048576 | tf_op jit(solution)/shard_map/slice | solution.py:156
  171.1 42.4 %collective-permute-start.3 = (f32[3600,128]{1,0:T(8,128)}, f32[3600,128]{1,0:T(8,128)S(1)}, u32[]{:S(2)}, u32[]{:S(2)}) collective-permute-start(f32[3600,128]{1,0:T(8,128)} %shard_map.31.refs_1_), channel_id=1, source_target_pairs={{0,2},{1,3},{2,0},{3,1},{4,6},{5,7},{6,4},{7,5},{8,10},{9,11},{10,... | collective-permute-start | bytes 5529608 | tf_op jit(solution)/shard_map/ppermute | solution.py:152
  172.6 42.2 %collective-permute-start.4 = (f32[3600,128]{1,0:T(8,128)}, f32[3600,128]{1,0:T(8,128)}, u32[]{:S(2)}, u32[]{:S(2)}) collective-permute-start(f32[3600,128]{1,0:T(8,128)} %shard_map.31.refs_1_), channel_id=1, source_target_pairs={{0,4},{1,5},{2,6},{3,7},{4,0},{5,1},{6,2},{7,3},{8,12},{9,13},{10,... | collective-permute-start | bytes 5529608 | tf_op jit(solution)/shard_map/ppermute | solution.py:152
  173.3 41.5 %collective-permute-start.9 = (f32[3600,128]{1,0:T(8,128)}, f32[3600,128]{1,0:T(8,128)}, u32[]{:S(2)}, u32[]{:S(2)}) collective-permute-start(f32[3600,128]{1,0:T(8,128)} %shard_map.31.refs_1_), channel_id=1, source_target_pairs={{0,1},{1,0},{2,3},{3,2},{4,5},{5,4},{6,7},{7,6},{8,9},{9,8},{10,11... | collective-permute-start | bytes 5529608 | tf_op jit(solution)/shard_map/ppermute | solution.py:152
  173.3 41.5 %collective-permute-start.8 = (f32[3600,128]{1,0:T(8,128)}, f32[3600,128]{1,0:T(8,128)}, u32[]{:S(2)}, u32[]{:S(2)}) collective-permute-start(f32[3600,128]{1,0:T(8,128)} %collective-permute-done.2.refs_12_), channel_id=1, source_target_pairs={{0,1},{1,0},{2,3},{3,2},{4,5},{5,4},{6,7},{7,6},{8,9},{9,8},{10,11... | collective-permute-start | bytes 5529608 | tf_op jit(solution)/shard_map/ppermute | solution.py:152
  213.5 23.7 %copy-start.1 = (f32[3600,128]{1,0:T(8,128)}, f32[3600,128]{1,0:T(8,128)S(1)}, u32[]{:S(2)}) copy-start(f32[3600,128]{1,0:T(8,128)S(1)} %collective-permute-done.3.refs_5_) | copy-start | bytes 5529604
  214.9 21.3 %collective-permute-start.12 = (f32[1800,128]{1,0:T(8,128)S(1)}, f32[1800,128]{1,0:T(8,128)S(1)}, u32[]{:S(2)}, u32[]{:S(2)}) collective-permute-start(f32[1800,128]{1,0:T(8,128)S(1)} %slice.18), channel_id=1, source_target_pairs={{0,4},{1,5},{2,6},{3,7},{4,0},{5,1},{6,2},{7,3},{8,12},{9,13},{10,... | collective-permute-start | bytes 2764808 | tf_op jit(solution)/shard_map/ppermute | solution.py:152
  216.5 21.0 %collective-permute-start.13 = (f32[1800,128]{1,0:T(8,128)S(1)}, f32[1800,128]{1,0:T(8,128)S(1)}, u32[]{:S(2)}, u32[]{:S(2)}) collective-permute-start(f32[1800,128]{1,0:T(8,128)S(1)} %slice.19), channel_id=1, source_target_pairs={{0,2},{1,3},{2,0},{3,1},{4,6},{5,7},{6,4},{7,5},{8,10},{9,11},{10,... | collective-permute-start | bytes 2764808 | tf_op jit(solution)/shard_map/ppermute | solution.py:152
  217.1 21.4 %collective-permute-start.10 = (f32[3600,128]{1,0:T(8,128)S(1)}, f32[3600,128]{1,0:T(8,128)}, u32[]{:S(2)}, u32[]{:S(2)}) collective-permute-start(f32[3600,128]{1,0:T(8,128)S(1)} %collective-permute-done.3.refs_5_), channel_id=1, source_target_pairs={{0,1},{1,0},{2,3},{3,2},{4,5},{5,4},{6,7},{7,6},{8,9},{9,8},{10,11... | collective-permute-start | bytes 5529608 | tf_op jit(solution)/shard_map/ppermute | solution.py:152
  217.1 21.4 %collective-permute-start.11 = (f32[3600,128]{1,0:T(8,128)}, f32[3600,128]{1,0:T(8,128)}, u32[]{:S(2)}, u32[]{:S(2)}) collective-permute-start(f32[3600,128]{1,0:T(8,128)} %collective-permute-done.4.refs_9_), channel_id=1, source_target_pairs={{0,1},{1,0},{2,3},{3,2},{4,5},{5,4},{6,7},{7,6},{8,9},{9,8},{10,11... | collective-permute-start | bytes 5529608 | tf_op jit(solution)/shard_map/ppermute | solution.py:152
  238.5 4.1 collective-permute-start.14
  (1 other events, 1.3 us)
Sparse Core Ops, SparseCore 0:
  55.8 189.0 all-gather.3
  246.4 97.7 all-gather.5
  345.8 44.5 all-gather.7

commit v7 on v3

--- a/solution.py
+++ b/solution.py
@@ -24,7 +24,7 @@
 
 def chunks_of(columns):
     if columns == 1920:
-        order = [(0, 1024), (1280, 640), (1024, 256)]
+        order = [(0, 1280), (1280, 512), (1792, 128)]
         return [(start, width, width) for start, width in order]
     wide = [(n, WIDE, WIDE) for n in range(0, columns - WIDE + 1, WIDE)]
     start = len(wide) * WIDE
@@ -151,21 +151,24 @@
     def swap(x, mask):
         return lax.ppermute(x, "ka", [(d, d ^ mask) for d in range(devices)])
 
-    def gather(n, source):
+    def piece(n, source):
         start, width, _ = chunks[n]
         x = lax.slice_in_dim(source, start, start + width, axis=1)
         x = x.reshape(devices // line, line, 2, -1, width).swapaxes(1, 2)
-        return lax.all_gather(x.reshape(-1, width), "ga", axis=0, tiled=True)
-
-    source, amplitudes = tie(integrals, amplitudes)
-    gathered = [gather(0, source)]
+        return x.reshape(-1, width)
+
+    def gather(x):
+        return lax.all_gather(x, "ga", axis=0, tiled=True)
 
     held = []
     for half in range(2):
         blocks = cut(amplitudes.T, line, half)
         if half:
-            blocks, first, source = tie(blocks, first, integrals)
-            gathered.append(gather(1, source))
+            now = piece(0, integrals)
+            blocks, first, now, source = tie(blocks, first, now, integrals)
+            gathered = [gather(now)]
+            first, then = tie(first, piece(1, source))
+            gathered.append(gather(then))
             held.append({0: turn(first)})
         blocks = lax.all_to_all(blocks, "ga", split_axis=0, concat_axis=0, tiled=True)
         first = blocks.reshape(-1, rows)
@@ -181,7 +184,7 @@
         for level in range(1, len(masks) + 1):
             if half and level == 2:
                 held, across, source = tie(held, across, integrals)
-                gathered += [gather(n, source) for n in range(2, len(chunks))]
+                gathered += [gather(piece(n, source)) for n in range(2, len(chunks))]
                 blocks = held[1]
             if half and level == 2 == len(masks):
                 some = rows // 16 * 8

time: 429 us -> 419 us (0.977)
  matrix products: 61.1 us -> 47.1 us
  Pallas kernels: 84.9 us -> 97.2 us
  waiting for transfers between devices: 228 us -> 222 us
    all_to_all x2, waiting for transfers between devices: 131 us -> 84.2 us  [per_device(): lax.all_to_all(blocks, 'ga', split_axis=0, concat_axis=0, tiled=True)]
    all_gather x3, waiting for transfers between devices: 0.02 us -> 35.3 us  [gather(): return lax.all_gather(x, 'ga', axis=0, tiled=True)]
    dot_general x2, matrix products: 61.1 us -> 47.1 us  [per_device(): jnp.dot(whole, w, precision=lax.Precision.HIGH, preferred_element_type=jn...]
    pallas_call x1, Pallas kernels: 66.6 us -> 79.2 us  [product(): pl.pallas_call(functools.partial(product_kernel, len(parts) // 2), grid_s...]
    ppermute x15, waiting for transfers between devices: 96.3 us -> 103 us  [swap(): return lax.ppermute(x, 'ka', [(d, d ^ mask) for d in range(devices)])]
  transfers between devices with their start and end apart: 20 -> 20, of which waited for: 9 -> 12; matrix products, arithmetic and copies ran while one was open for 11% -> 9% of each run, Pallas kernels for 20% -> 23%
where the time goes in v7:
time: 419 us; the launch traced here: 415 us
  waiting for transfers between devices  222 us (53%)
  Pallas kernels  97.2 us (23%)
  matrix products  47.1 us (11%)
  starting transfers between devices  23.1 us (6%)
  between operations  13.2 us (3%)
  local copies, waits for them, and re-layouts  12.4 us (3%)
    ppermute x15, waiting for transfers between devices, swap(): return lax.ppermute(x, 'ka', [(d, d ^ mask) for d in range(devices)])  103 us
    all_to_all x2, waiting for transfers between devices, per_device(): lax.all_to_all(blocks, 'ga', split_axis=0, concat_axis=0, tiled=True)  84.2 us
    pallas_call x1, Pallas kernels, product(): pl.pallas_call(functools.partial(product_kernel, len(parts) // 2), grid_s...  79.2 us
    dot_general x2, matrix products, per_device(): jnp.dot(whole, w, precision=lax.Precision.HIGH, preferred_element_type=jn...  47.1 us
    all_gather x3, waiting for transfers between devices, gather(): return lax.all_gather(x, 'ga', axis=0, tiled=True)  35.3 us
    all_to_all x2, starting transfers between devices, per_device(): lax.all_to_all(blocks, 'ga', split_axis=0, concat_axis=0, tiled=True)  12.3 us
    pallas_call x2, Pallas kernels, turn(): pl.pallas_call(turn_kernel, grid=(pl.cdiv(rows, width),), in_specs=[pl.Bl...  11.7 us
    ppermute x15, starting transfers between devices, swap(): return lax.ppermute(x, 'ka', [(d, d ^ mask) for d in range(devices)])  10.8 us
  transfers between devices with their start and end apart: 20, of which 12 were waited for; matrix products, arithmetic and copies ran while one was open for 9% of the time, Pallas kernels for 23%

profile of v7, /device:TPU:16, one launch (start us, length us, event | category | flops | bytes accessed | tf_op | source)
XLA Modules:
  0.0 415.1 jit_solution(13058940675913057589)
XLA Ops:
  6.5 3.2 shard_map.29
  9.7 5.2 %all-to-all-start = ((f32[4,32,3600]{2,1,0:T(8,128)}), f32[4,32,3600]{2,1,0:T(8,128)}, u32[]{:S(2)}, u32[]{:S(2)}) async-start(f32[4,32,3600]{2,1,0:T(8,128)} %shard_map.29), calls=%async_computation | async-start | bytes 3801088 | tf_op jit(solution)/shard_map/all_to_all | solution.py:173
  14.9 3.2 shard_map.28
  18.2 1.7 slice-done
  19.9 1.7 copy.5
  21.6 34.0 %all-to-all-done = f32[4,32,3600]{2,1,0:T(8,128)} async-done(((f32[4,32,3600]{2,1,0:T(8,128)}), f32[4,32,3600]{2,1,0:T(8,128)}, u32[]{:S(2)}, u32[]{:S(2)}) %all-to-all-start) | async-done | bytes 1843232 | tf_op jit(solution)/shard_map/all_to_all | solution.py:173
  58.0 5.8 %shard_map.30.refs_0_ = f32[3600,128]{1,0:T(8,128)} custom-call(f32[128,3600]{1,0:T(8,128)} %bitcast.2.t_ref), custom_call_target="tpu_custom_call" | custom-call | bytes 3686400 | tf_op jit(solution)/shard_map/pallas_call | solution.py:61
  63.8 1.5 collective-permute-start.1
  65.3 7.1 %all-to-all-start.1 = ((f32[4,32,3600]{2,1,0:T(8,128)}), f32[4,32,3600]{2,1,0:T(8,128)S(1)}, u32[]{:S(2)}, u32[]{:S(2)}) async-start(f32[4,32,3600]{2,1,0:T(8,128)} %shard_map.28), calls=%async_computation.1 | async-start | bytes 3801088 | tf_op jit(solution)/shard_map/all_to_all | solution.py:173
  73.9 31.4 %collective-permute-done.1.refs_8_ = f32[3600,128]{1,0:T(8,128)} collective-permute-done((f32[3600,128]{1,0:T(8,128)}, f32[3600,128]{1,0:T(8,128)}, u32[]{:S(2)}, u32[]{:S(2)}) %collective-permute-start.1) | collective-permute-done | bytes 1843232 | tf_op jit(solution)/shard_map/ppermute | solution.py:152
  105.3 1.5 collective-permute-start.2
  106.8 9.0 %collective-permute-done.refs_4_ = f32[3600,128]{1,0:T(8,128)} collective-permute-done((f32[3600,128]{1,0:T(8,128)}, f32[3600,128]{1,0:T(8,128)}, u32[]{:S(2)}, u32[]{:S(2)}) %collective-permute-start) | collective-permute-done | bytes 1843232 | tf_op jit(solution)/shard_map/ppermute | solution.py:152
  115.8 50.1 %all-to-all-done.1 = f32[4,32,3600]{2,1,0:T(8,128)S(1)} async-done(((f32[4,32,3600]{2,1,0:T(8,128)}), f32[4,32,3600]{2,1,0:T(8,128)S(1)}, u32[]{:S(2)}, u32[]{:S(2)}) %all-to-all-start.1) | async-done | bytes 1843232 | tf_op jit(solution)/shard_map/all_to_all | solution.py:173
  167.2 5.8 %shard_map.31.refs_1_ = f32[3600,128]{1,0:T(8,128)} custom-call(f32[128,3600]{1,0:T(8,128)} %bitcast.26), custom_call_target="tpu_custom_call" | custom-call | bytes 3686400 | tf_op jit(solution)/shard_map/pallas_call | solution.py:61
  174.5 1.5 collective-permute-start.4
  176.6 38.9 %collective-permute-done.3.refs_5_ = f32[3600,128]{1,0:T(8,128)S(1)} collective-permute-done((f32[3600,128]{1,0:T(8,128)}, f32[3600,128]{1,0:T(8,128)S(1)}, u32[]{:S(2)}, u32[]{:S(2)}) %collective-permute-start.3) | collective-permute-done | bytes 1843232 | tf_op jit(solution)/shard_map/ppermute | solution.py:152
  218.1 1.5 collective-permute-start.12
  222.2 17.3 %collective-permute-done.12 = f32[1800,128]{1,0:T(8,128)S(1)} collective-permute-done((f32[1800,128]{1,0:T(8,128)S(1)}, f32[1800,128]{1,0:T(8,128)S(1)}, u32[]{:S(2)}, u32[]{:S(2)}) %collective-permute-start.12) | collective-permute-done | bytes 921632 | tf_op jit(solution)/shard_map/ppermute | solution.py:152
  243.7 3.4 collective-permute-done.14.refs_15_
  247.1 32.2 %all-gather.4.cloned.1.call-done.refs_16_ = f32[2048,1280]{1,0:T(8,128)} async-done(((f32[512,1280]{1,0:T(8,128)}), f32[2048,1280]{1,0:T(8,128)}) %all-gather.4.cloned.1.call-update) | async-done | bytes 10485776 | tf_op jit(solution)/shard_map/all_gather | solution.py:161
  279.2 79.2 %shard_map.32 = (f32[3600,1920]{1,0:T(8,128)}, f32[3600,2048]{1,0:T(8,128)}) custom-call(s32[1]{0:T(128)} %bitcast.place_ref, f32[3600,128]{1,0:T(8,128)} %shard_map.30.refs_0_, f32[3600,128]{1,0:T(8,128)} %shard_map.31.refs_1_, f32[3600,128]{1,0:T(8,128)} %collective-permute-done.5.refs_2_, f32[3600,128]{1,0:T(8,128)} %copy-done.2, ...), custom_call_target="tpu_custom_call" | custom-call | flops 56623104000 | bytes 87900160 | tf_op jit(solution)/shard_map/pallas_call | solution.py:110
  358.4 3.0 all-gather.6.cloned.1.call-done
  361.4 28.9 %multiply_dynamic-update-slice_fusion = f32[3600,1920]{1,0:T(8,128)} fusion(f32[3600,1920]{1,0:T(8,128)} %get-tuple-element.43, f32[3600,2048]{1,0:T(8,128)} %get-tuple-element.44, f32[2048,512]{1,0:T(8,128)} %all-gather.6.cloned.1.call-done), kind=kOutput, calls=%fused_computation | convolution fusion | flops 22651084800 | bytes 41058304 | tf_op jit(solution)/shard_map/dot_general | solution.py:210
  390.4 18.1 %fusion = f32[3600,1920]{1,0:T(8,128)} fusion(f32[3600,1920]{1,0:T(8,128)} %multiply_dynamic-update-slice_fusion, f32[3600,2048]{1,0:T(8,128)} %get-tuple-element.44, f32[2048,128]{1,0:T(8,128)} %all-gather.8.cloned.1.call-done), kind=kOutput, calls=%fused_computation.2 | convolution fusion | flops 5662771200 | bytes 32382976 | tf_op jit(solution)/shard_map/dot_general | solution.py:210
  (45 shorter events, 16.6 us)
Async XLA Ops:
  9.7 45.9 %all-to-all-start = ((f32[4,32,3600]{2,1,0:T(8,128)}), f32[4,32,3600]{2,1,0:T(8,128)}, u32[]{:S(2)}, u32[]{:S(2)}) async-start(f32[4,32,3600]{2,1,0:T(8,128)} %shard_map.29), calls=%async_computation | async-start | bytes 3801088 | tf_op jit(solution)/shard_map/all_to_all | solution.py:173
  14.9 264.3 %all-gather.4.cloned.1.call-start = ((), (), s32[]{:S(2)}) async-start(), calls=%async_computation.2 | async-start | bytes 13107200 | tf_op jit(solution)/shard_map/all_gather | solution.py:161
  18.2 1.7 slice-start
  63.8 41.5 %collective-permute-start.1 = (f32[3600,128]{1,0:T(8,128)}, f32[3600,128]{1,0:T(8,128)}, u32[]{:S(2)}, u32[]{:S(2)}) collective-permute-start(f32[3600,128]{1,0:T(8,128)} %shard_map.30.refs_0_), channel_id=1, source_target_pairs={{0,4},{1,5},{2,6},{3,7},{4,0},{5,1},{6,2},{7,3},{8,12},{9,13},{10,... | collective-permute-start | bytes 5529608 | tf_op jit(solution)/shard_map/ppermute | solution.py:152
  65.3 100.6 %all-to-all-start.1 = ((f32[4,32,3600]{2,1,0:T(8,128)}), f32[4,32,3600]{2,1,0:T(8,128)S(1)}, u32[]{:S(2)}, u32[]{:S(2)}) async-start(f32[4,32,3600]{2,1,0:T(8,128)} %shard_map.28), calls=%async_computation.1 | async-start | bytes 3801088 | tf_op jit(solution)/shard_map/all_to_all | solution.py:173
  72.4 289.0 %all-gather.6.cloned.1.call-start = ((), (), s32[]{:S(2)}) async-start(), calls=%async_computation.3 | async-start | bytes 5242880 | tf_op jit(solution)/shard_map/all_gather | solution.py:161
  72.4 43.4 %collective-permute-start = (f32[3600,128]{1,0:T(8,128)}, f32[3600,128]{1,0:T(8,128)}, u32[]{:S(2)}, u32[]{:S(2)}) collective-permute-start(f32[3600,128]{1,0:T(8,128)} %shard_map.30.refs_0_), channel_id=1, source_target_pairs={{0,2},{1,3},{2,0},{3,1},{4,6},{5,7},{6,4},{7,5},{8,10},{9,11},{10,... | collective-permute-start | bytes 5529608 | tf_op jit(solution)/shard_map/ppermute | solution.py:152
  73.9 100.7 %collective-permute-start.5 = (f32[3600,128]{1,0:T(8,128)}, f32[3600,128]{1,0:T(8,128)}, u32[]{:S(2)}, u32[]{:S(2)}) collective-permute-start(f32[3600,128]{1,0:T(8,128)} %shard_map.30.refs_0_), channel_id=1, source_target_pairs={{0,1},{1,0},{2,3},{3,2},{4,5},{5,4},{6,7},{7,6},{8,9},{9,8},{10,11... | collective-permute-start | bytes 5529608 | tf_op jit(solution)/shard_map/ppermute | solution.py:152
  105.3 70.8 %collective-permute-start.2 = (f32[3600,128]{1,0:T(8,128)}, f32[3600,128]{1,0:T(8,128)}, u32[]{:S(2)}, u32[]{:S(2)}) collective-permute-start(f32[3600,128]{1,0:T(8,128)} %collective-permute-done.1.refs_8_), channel_id=1, source_target_pairs={{0,2},{1,3},{2,0},{3,1},{4,6},{5,7},{6,4},{7,5},{8,10},{9,11},{10,... | collective-permute-start | bytes 5529608 | tf_op jit(solution)/shard_map/ppermute | solution.py:152
  106.7 69.3 %collective-permute-start.7 = (f32[3600,128]{1,0:T(8,128)}, f32[3600,128]{1,0:T(8,128)}, u32[]{:S(2)}, u32[]{:S(2)}) collective-permute-start(f32[3600,128]{1,0:T(8,128)} %collective-permute-done.1.refs_8_), channel_id=1, source_target_pairs={{0,1},{1,0},{2,3},{3,2},{4,5},{5,4},{6,7},{7,6},{8,9},{9,8},{10,11... | collective-permute-start | bytes 5529608 | tf_op jit(solution)/shard_map/ppermute | solution.py:152
  106.8 283.6 %all-gather.8.cloned.1.call-start = ((), (), s32[]{:S(2)}) async-start(), calls=%async_computation.4 | async-start | bytes 1310720 | tf_op jit(solution)/shard_map/all_gather | solution.py:161
  115.8 60.8 %collective-permute-start.6 = (f32[3600,128]{1,0:T(8,128)}, f32[3600,128]{1,0:T(8,128)}, u32[]{:S(2)}, u32[]{:S(2)}) collective-permute-start(f32[3600,128]{1,0:T(8,128)} %collective-permute-done.refs_4_), channel_id=1, source_target_pairs={{0,1},{1,0},{2,3},{3,2},{4,5},{5,4},{6,7},{7,6},{8,9},{9,8},{10,11... | collective-permute-start | bytes 5529608 | tf_op jit(solution)/shard_map/ppermute | solution.py:152
  173.0 42.4 %collective-permute-start.3 = (f32[3600,128]{1,0:T(8,128)}, f32[3600,128]{1,0:T(8,128)S(1)}, u32[]{:S(2)}, u32[]{:S(2)}) collective-permute-start(f32[3600,128]{1,0:T(8,128)} %shard_map.31.refs_1_), channel_id=1, source_target_pairs={{0,2},{1,3},{2,0},{3,1},{4,6},{5,7},{6,4},{7,5},{8,10},{9,11},{10,... | collective-permute-start | bytes 5529608 | tf_op jit(solution)/shard_map/ppermute | solution.py:152
  174.5 42.2 %collective-permute-start.4 = (f32[3600,128]{1,0:T(8,128)}, f32[3600,128]{1,0:T(8,128)}, u32[]{:S(2)}, u32[]{:S(2)}) collective-permute-start(f32[3600,128]{1,0:T(8,128)} %shard_map.31.refs_1_), channel_id=1, source_target_pairs={{0,4},{1,5},{2,6},{3,7},{4,0},{5,1},{6,2},{7,3},{8,12},{9,13},{10,... | collective-permute-start | bytes 5529608 | tf_op jit(solution)/shard_map/ppermute | solution.py:152
  176.0 40.7 %collective-permute-start.9 = (f32[3600,128]{1,0:T(8,128)}, f32[3600,128]{1,0:T(8,128)S(1)}, u32[]{:S(2)}, u32[]{:S(2)}) collective-permute-start(f32[3600,128]{1,0:T(8,128)} %shard_map.31.refs_1_), channel_id=1, source_target_pairs={{0,1},{1,0},{2,3},{3,2},{4,5},{5,4},{6,7},{7,6},{8,9},{9,8},{10,11... | collective-permute-start | bytes 5529608 | tf_op jit(solution)/shard_map/ppermute | solution.py:152
  176.0 42.0 %collective-permute-start.8 = (f32[3600,128]{1,0:T(8,128)}, f32[3600,128]{1,0:T(8,128)}, u32[]{:S(2)}, u32[]{:S(2)}) collective-permute-start(f32[3600,128]{1,0:T(8,128)} %collective-permute-done.2.refs_12_), channel_id=1, source_target_pairs={{0,1},{1,0},{2,3},{3,2},{4,5},{5,4},{6,7},{7,6},{8,9},{9,8},{10,11... | collective-permute-start | bytes 5529608 | tf_op jit(solution)/shard_map/ppermute | solution.py:152
  215.5 25.0 %copy-start.1 = (f32[3600,128]{1,0:T(8,128)}, f32[3600,128]{1,0:T(8,128)S(1)}, u32[]{:S(2)}) copy-start(f32[3600,128]{1,0:T(8,128)S(1)} %collective-permute-done.3.refs_5_) | copy-start | bytes 5529604
  216.8 1.3 copy-start.2
  218.1 21.4 %collective-permute-start.12 = (f32[1800,128]{1,0:T(8,128)S(1)}, f32[1800,128]{1,0:T(8,128)S(1)}, u32[]{:S(2)}, u32[]{:S(2)}) collective-permute-start(f32[1800,128]{1,0:T(8,128)S(1)} %slice.17), channel_id=1, source_target_pairs={{0,4},{1,5},{2,6},{3,7},{4,0},{5,1},{6,2},{7,3},{8,12},{9,13},{10,... | collective-permute-start | bytes 2764808 | tf_op jit(solution)/shard_map/ppermute | solution.py:152
  220.9 22.0 %slice-start.2 = ((f32[512,1920]{1,0:T(8,128)}), f32[512,128]{1,0:T(8,128)S(1)}, s32[]{:S(2)}) async-start(f32[512,1920]{1,0:T(8,128)} %param.3), calls=%async_computation.7 | async-start | bytes 524288 | tf_op jit(solution)/shard_map/slice | solution.py:156
  220.9 21.0 %collective-permute-start.13 = (f32[1800,128]{1,0:T(8,128)S(1)}, f32[1800,128]{1,0:T(8,128)S(1)}, u32[]{:S(2)}, u32[]{:S(2)}) collective-permute-start(f32[1800,128]{1,0:T(8,128)S(1)} %slice.18), channel_id=1, source_target_pairs={{0,2},{1,3},{2,0},{3,1},{4,6},{5,7},{6,4},{7,5},{8,10},{9,11},{10,... | collective-permute-start | bytes 2764808 | tf_op jit(solution)/shard_map/ppermute | solution.py:152
  221.7 22.0 %collective-permute-start.10 = (f32[3600,128]{1,0:T(8,128)S(1)}, f32[3600,128]{1,0:T(8,128)}, u32[]{:S(2)}, u32[]{:S(2)}) collective-permute-start(f32[3600,128]{1,0:T(8,128)S(1)} %collective-permute-done.3.refs_5_), channel_id=1, source_target_pairs={{0,1},{1,0},{2,3},{3,2},{4,5},{5,4},{6,7},{7,6},{8,9},{9,8},{10,11... | collective-permute-start | bytes 5529608 | tf_op jit(solution)/shard_map/ppermute | solution.py:152
  221.7 22.0 %collective-permute-start.11 = (f32[3600,128]{1,0:T(8,128)}, f32[3600,128]{1,0:T(8,128)}, u32[]{:S(2)}, u32[]{:S(2)}) collective-permute-start(f32[3600,128]{1,0:T(8,128)} %collective-permute-done.4.refs_9_), channel_id=1, source_target_pairs={{0,1},{1,0},{2,3},{3,2},{4,5},{5,4},{6,7},{7,6},{8,9},{9,8},{10,11... | collective-permute-start | bytes 5529608 | tf_op jit(solution)/shard_map/ppermute | solution.py:152
  242.9 4.1 collective-permute-start.14
  (2 other events, 2.5 us)
Sparse Core Ops, SparseCore 0:
  55.8 223.4 all-gather.3
  280.8 80.5 all-gather.5
  362.9 27.4 all-gather.7

commit v8 on v7

--- a/solution.py
+++ b/solution.py
@@ -24,7 +24,7 @@
 
 def chunks_of(columns):
     if columns == 1920:
-        order = [(0, 1280), (1280, 512), (1792, 128)]
+        order = [(0, 1024), (1024, 128), (1152, 512), (1664, 256)]
         return [(start, width, width) for start, width in order]
     wide = [(n, WIDE, WIDE) for n in range(0, columns - WIDE + 1, WIDE)]
     start = len(wide) * WIDE
@@ -160,14 +160,21 @@
     def gather(x):
         return lax.all_gather(x, "ga", axis=0, tiled=True)
 
+    narrow = []
+    if len(chunks) > 2:
+        now, amplitudes = tie(piece(1, integrals), amplitudes)
+        narrow = [gather(now)]
+
     held = []
     for half in range(2):
         blocks = cut(amplitudes.T, line, half)
         if half:
             now = piece(0, integrals)
-            blocks, first, now, source = tie(blocks, first, now, integrals)
-            gathered = [gather(now)]
-            first, then = tie(first, piece(1, source))
+            blocks, first, now, source, narrow = tie(
+                blocks, first, now, integrals, narrow
+            )
+            gathered = [gather(now), *narrow]
+            first, then = tie(first, piece(len(gathered), source))
             gathered.append(gather(then))
             held.append({0: turn(first)})
         blocks = lax.all_to_all(blocks, "ga", split_axis=0, concat_axis=0, tiled=True)
@@ -184,7 +191,7 @@
         for level in range(1, len(masks) + 1):
             if half and level == 2:
                 held, across, source = tie(held, across, integrals)
-                gathered += [gather(piece(n, source)) for n in range(2, len(chunks))]
+                gathered += [gather(piece(n, source)) for n in range(len(gathered), len(chunks))]
                 blocks = held[1]
             if half and level == 2 == len(masks):
                 some = rows // 16 * 8

time: 419 us -> 421 us (level)
  matrix products: 47.1 us -> 64.9 us
  Pallas kernels: 97.2 us -> 84.7 us
    all_to_all x2, waiting for transfers between devices: 84.2 us -> 50.7 us  [per_device(): lax.all_to_all(blocks, 'ga', split_axis=0, concat_axis=0, tiled=True)]
    all_gather x3 -> x4, waiting for transfers between devices: 35.3 us -> 63.6 us  [gather(): return lax.all_gather(x, 'ga', axis=0, tiled=True)]
    dot_general x2 -> x3, matrix products: 47.1 us -> 64.9 us  [per_device(): jnp.dot(whole, w, precision=lax.Precision.HIGH, preferred_element_type=jn...]
    pallas_call x1, Pallas kernels: 79.2 us -> 66.7 us  [product(): pl.pallas_call(functools.partial(product_kernel, len(parts) // 2), grid_s...]
  transfers between devices with their start and end apart: 20 -> 21, of which waited for: 12 -> 11; matrix products, arithmetic and copies ran while one was open for 9% -> 13% of each run, Pallas kernels for 23% -> 20%
where the time goes in v8:
time: 421 us; the launch traced here: 417 us
  waiting for transfers between devices  218 us (52%)
  Pallas kernels  84.7 us (20%)
  matrix products  64.9 us (15%)
  starting transfers between devices  23 us (5%)
  local copies, waits for them, and re-layouts  13.8 us (3%)
  between operations  13.2 us (3%)
    ppermute x15, waiting for transfers between devices, swap(): return lax.ppermute(x, 'ka', [(d, d ^ mask) for d in range(devices)])  103 us
    pallas_call x1, Pallas kernels, product(): pl.pallas_call(functools.partial(product_kernel, len(parts) // 2), grid_s...  66.7 us
    dot_general x3, matrix products, per_device(): jnp.dot(whole, w, precision=lax.Precision.HIGH, preferred_element_type=jn...  64.9 us
    all_gather x4, waiting for transfers between devices, gather(): return lax.all_gather(x, 'ga', axis=0, tiled=True)  63.6 us
    all_to_all x2, waiting for transfers between devices, per_device(): lax.all_to_all(blocks, 'ga', split_axis=0, concat_axis=0, tiled=True)  50.7 us
    all_to_all x2, starting transfers between devices, per_device(): lax.all_to_all(blocks, 'ga', split_axis=0, concat_axis=0, tiled=True)  12.3 us
    pallas_call x2, Pallas kernels, turn(): pl.pallas_call(turn_kernel, grid=(pl.cdiv(rows, width),), in_specs=[pl.Bl...  11.6 us
    ppermute x15, starting transfers between devices, swap(): return lax.ppermute(x, 'ka', [(d, d ^ mask) for d in range(devices)])  10.7 us
  transfers between devices with their start and end apart: 21, of which 11 were waited for; matrix products, arithmetic and copies ran while one was open for 13% of the time, Pallas kernels for 20%

profile of v8, /device:TPU:16, one launch (start us, length us, event | category | flops | bytes accessed | tf_op | source)
XLA Modules:
  0.0 417.4 jit_solution(11002154501696365578)
XLA Ops:
  8.2 3.2 shard_map.29
  11.4 5.2 %all-to-all-start = ((f32[4,32,3600]{2,1,0:T(8,128)}), f32[4,32,3600]{2,1,0:T(8,128)}, u32[]{:S(2)}, u32[]{:S(2)}) async-start(f32[4,32,3600]{2,1,0:T(8,128)} %shard_map.29), calls=%async_computation | async-start | bytes 3801088 | tf_op jit(solution)/shard_map/all_to_all | solution.py:180
  17.4 3.2 shard_map.28
  20.6 1.6 slice-done
  23.7 48.1 %all-gather.5.cloned.1.call-done = f32[2048,128]{1,0:T(8,128)} async-done(((f32[512,128]{1,0:T(8,128)}), f32[2048,128]{1,0:T(8,128)}) %all-gather.5.cloned.1.call-update) | async-done | bytes 1048592 | tf_op jit(solution)/shard_map/all_gather | solution.py:161
  71.7 2.5 all-to-all-done
  76.5 5.8 %shard_map.30.refs_0_ = f32[3600,128]{1,0:T(8,128)} custom-call(f32[128,3600]{1,0:T(8,128)} %bitcast.5.t_ref), custom_call_target="tpu_custom_call" | custom-call | bytes 3686400 | tf_op jit(solution)/shard_map/pallas_call | solution.py:61
  82.3 1.5 collective-permute-start.1
  83.9 7.1 %all-to-all-start.1 = ((f32[4,32,3600]{2,1,0:T(8,128)}), f32[4,32,3600]{2,1,0:T(8,128)S(1)}, u32[]{:S(2)}, u32[]{:S(2)}) async-start(f32[4,32,3600]{2,1,0:T(8,128)} %shard_map.28), calls=%async_computation.1 | async-start | bytes 3801088 | tf_op jit(solution)/shard_map/all_to_all | solution.py:180
  90.9 1.5 collective-permute-start
  92.4 31.4 %collective-permute-done.1.refs_8_ = f32[3600,128]{1,0:T(8,128)} collective-permute-done((f32[3600,128]{1,0:T(8,128)}, f32[3600,128]{1,0:T(8,128)}, u32[]{:S(2)}, u32[]{:S(2)}) %collective-permute-start.1) | collective-permute-done | bytes 1843232 | tf_op jit(solution)/shard_map/ppermute | solution.py:152
  123.8 1.5 collective-permute-start.2
  125.4 9.0 %collective-permute-done.refs_4_ = f32[3600,128]{1,0:T(8,128)} collective-permute-done((f32[3600,128]{1,0:T(8,128)}, f32[3600,128]{1,0:T(8,128)}, u32[]{:S(2)}, u32[]{:S(2)}) %collective-permute-start) | collective-permute-done | bytes 1843232 | tf_op jit(solution)/shard_map/ppermute | solution.py:152
  134.4 48.2 %all-to-all-done.1 = f32[4,32,3600]{2,1,0:T(8,128)S(1)} async-done(((f32[4,32,3600]{2,1,0:T(8,128)}), f32[4,32,3600]{2,1,0:T(8,128)S(1)}, u32[]{:S(2)}, u32[]{:S(2)}) %all-to-all-start.1) | async-done | bytes 1843232 | tf_op jit(solution)/shard_map/all_to_all | solution.py:180
  183.8 5.8 %shard_map.31.refs_1_ = f32[3600,128]{1,0:T(8,128)} custom-call(f32[128,3600]{1,0:T(8,128)} %bitcast.32), custom_call_target="tpu_custom_call" | custom-call | bytes 3686400 | tf_op jit(solution)/shard_map/pallas_call | solution.py:61
  193.1 39.0 %collective-permute-done.3.refs_5_ = f32[3600,128]{1,0:T(8,128)S(1)} collective-permute-done((f32[3600,128]{1,0:T(8,128)}, f32[3600,128]{1,0:T(8,128)S(1)}, u32[]{:S(2)}, u32[]{:S(2)}) %collective-permute-start.3) | collective-permute-done | bytes 1843232 | tf_op jit(solution)/shard_map/ppermute | solution.py:152
  234.7 1.5 collective-permute-start.12
  238.8 17.3 %collective-permute-done.12 = f32[1800,128]{1,0:T(8,128)S(1)} collective-permute-done((f32[1800,128]{1,0:T(8,128)S(1)}, f32[1800,128]{1,0:T(8,128)S(1)}, u32[]{:S(2)}, u32[]{:S(2)}) %collective-permute-start.12) | collective-permute-done | bytes 921632 | tf_op jit(solution)/shard_map/ppermute | solution.py:152
  260.4 3.3 collective-permute-done.14.refs_15_
  263.7 66.7 %shard_map.32 = (f32[3600,1920]{1,0:T(8,128)}, f32[3600,2048]{1,0:T(8,128)}) custom-call(s32[1]{0:T(128)} %bitcast.place_ref, f32[3600,128]{1,0:T(8,128)} %shard_map.30.refs_0_, f32[3600,128]{1,0:T(8,128)} %shard_map.31.refs_1_, f32[3600,128]{1,0:T(8,128)} %collective-permute-done.5.refs_2_, f32[3600,128]{1,0:T(8,128)} %copy-done.3, ...), custom_call_target="tpu_custom_call" | custom-call | flops 45298483200 | bytes 82116608 | tf_op jit(solution)/shard_map/pallas_call | solution.py:110
  330.4 16.7 %fusion.1 = f32[3600,1920]{1,0:T(8,128)} fusion(f32[3600,1920]{1,0:T(8,128)} %get-tuple-element.48, f32[3600,2048]{1,0:T(8,128)} %get-tuple-element.49, f32[2048,128]{1,0:T(8,128)S(1)} %copy-done.1), kind=kOutput, calls=%fused_computation.4 | convolution fusion | flops 5662771200 | bytes 32382976 | tf_op jit(solution)/shard_map/dot_general | solution.py:217
  347.1 28.9 %multiply_dynamic-update-slice_fusion = f32[3600,1920]{1,0:T(8,128)} fusion(f32[3600,1920]{1,0:T(8,128)} %fusion.1, f32[3600,2048]{1,0:T(8,128)} %get-tuple-element.49, f32[2048,512]{1,0:T(8,128)} %all-gather.9.cloned.1.call-done), kind=kOutput, calls=%fused_computation | convolution fusion | flops 22651084800 | bytes 41058304 | tf_op jit(solution)/shard_map/dot_general | solution.py:217
  376.0 15.6 %all-gather.11.cloned.1.call-done = f32[2048,256]{1,0:T(8,128)} async-done(((f32[512,256]{1,0:T(8,128)}), f32[2048,256]{1,0:T(8,128)}) %all-gather.11.cloned.1.call-update) | async-done | bytes 2097168 | tf_op jit(solution)/shard_map/all_gather | solution.py:161
  391.6 19.3 %fusion = f32[3600,1920]{1,0:T(8,128)} fusion(f32[3600,1920]{1,0:T(8,128)} %multiply_dynamic-update-slice_fusion, f32[3600,2048]{1,0:T(8,128)} %get-tuple-element.49, f32[2048,256]{1,0:T(8,128)} %all-gather.11.cloned.1.call-done), kind=kOutput, calls=%fused_computation.2 | convolution fusion | flops 11325542400 | bytes 35274752 | tf_op jit(solution)/shard_map/dot_general | solution.py:217
  (53 shorter events, 20.5 us)
Async XLA Ops:
  11.4 62.8 %all-to-all-start = ((f32[4,32,3600]{2,1,0:T(8,128)}), f32[4,32,3600]{2,1,0:T(8,128)}, u32[]{:S(2)}, u32[]{:S(2)}) async-start(f32[4,32,3600]{2,1,0:T(8,128)} %shard_map.29), calls=%async_computation | async-start | bytes 3801088 | tf_op jit(solution)/shard_map/all_to_all | solution.py:180
  16.6 55.1 %all-gather.5.cloned.1.call-start = ((), (), s32[]{:S(2)}) async-start(), calls=%async_computation.2 | async-start | bytes 1310720 | tf_op jit(solution)/shard_map/all_gather | solution.py:161
  17.3 246.4 %all-gather.7.cloned.1.call-start = ((), (), s32[]{:S(2)}) async-start(), calls=%async_computation.3 | async-start | bytes 10485760 | tf_op jit(solution)/shard_map/all_gather | solution.py:161
  82.3 41.5 %collective-permute-start.1 = (f32[3600,128]{1,0:T(8,128)}, f32[3600,128]{1,0:T(8,128)}, u32[]{:S(2)}, u32[]{:S(2)}) collective-permute-start(f32[3600,128]{1,0:T(8,128)} %shard_map.30.refs_0_), channel_id=1, source_target_pairs={{0,4},{1,5},{2,6},{3,7},{4,0},{5,1},{6,2},{7,3},{8,12},{9,13},{10,... | collective-permute-start | bytes 5529608 | tf_op jit(solution)/shard_map/ppermute | solution.py:152
  83.9 98.7 %all-to-all-start.1 = ((f32[4,32,3600]{2,1,0:T(8,128)}), f32[4,32,3600]{2,1,0:T(8,128)S(1)}, u32[]{:S(2)}, u32[]{:S(2)}) async-start(f32[4,32,3600]{2,1,0:T(8,128)} %shard_map.28), calls=%async_computation.1 | async-start | bytes 3801088 | tf_op jit(solution)/shard_map/all_to_all | solution.py:180
  90.9 256.2 %all-gather.9.cloned.1.call-start = ((), (), s32[]{:S(2)}) async-start(), calls=%async_computation.4 | async-start | bytes 5242880 | tf_op jit(solution)/shard_map/all_gather | solution.py:161
  90.9 43.4 %collective-permute-start = (f32[3600,128]{1,0:T(8,128)}, f32[3600,128]{1,0:T(8,128)}, u32[]{:S(2)}, u32[]{:S(2)}) collective-permute-start(f32[3600,128]{1,0:T(8,128)} %shard_map.30.refs_0_), channel_id=1, source_target_pairs={{0,2},{1,3},{2,0},{3,1},{4,6},{5,7},{6,4},{7,5},{8,10},{9,11},{10,... | collective-permute-start | bytes 5529608 | tf_op jit(solution)/shard_map/ppermute | solution.py:152
  92.4 98.7 %collective-permute-start.5 = (f32[3600,128]{1,0:T(8,128)}, f32[3600,128]{1,0:T(8,128)}, u32[]{:S(2)}, u32[]{:S(2)}) collective-permute-start(f32[3600,128]{1,0:T(8,128)} %shard_map.30.refs_0_), channel_id=1, source_target_pairs={{0,1},{1,0},{2,3},{3,2},{4,5},{5,4},{6,7},{7,6},{8,9},{9,8},{10,11... | collective-permute-start | bytes 5529608 | tf_op jit(solution)/shard_map/ppermute | solution.py:152
  123.8 68.7 %collective-permute-start.2 = (f32[3600,128]{1,0:T(8,128)}, f32[3600,128]{1,0:T(8,128)}, u32[]{:S(2)}, u32[]{:S(2)}) collective-permute-start(f32[3600,128]{1,0:T(8,128)} %collective-permute-done.1.refs_8_), channel_id=1, source_target_pairs={{0,2},{1,3},{2,0},{3,1},{4,6},{5,7},{6,4},{7,5},{8,10},{9,11},{10,... | collective-permute-start | bytes 5529608 | tf_op jit(solution)/shard_map/ppermute | solution.py:152
  125.3 67.2 %collective-permute-start.7 = (f32[3600,128]{1,0:T(8,128)}, f32[3600,128]{1,0:T(8,128)}, u32[]{:S(2)}, u32[]{:S(2)}) collective-permute-start(f32[3600,128]{1,0:T(8,128)} %collective-permute-done.1.refs_8_), channel_id=1, source_target_pairs={{0,1},{1,0},{2,3},{3,2},{4,5},{5,4},{6,7},{7,6},{8,9},{9,8},{10,11... | collective-permute-start | bytes 5529608 | tf_op jit(solution)/shard_map/ppermute | solution.py:152
  125.3 266.2 %all-gather.11.cloned.1.call-start = ((), (), s32[]{:S(2)}) async-start(), calls=%async_computation.5 | async-start | bytes 2621440 | tf_op jit(solution)/shard_map/all_gather | solution.py:161
  134.4 58.7 %collective-permute-start.6 = (f32[3600,128]{1,0:T(8,128)}, f32[3600,128]{1,0:T(8,128)}, u32[]{:S(2)}, u32[]{:S(2)}) collective-permute-start(f32[3600,128]{1,0:T(8,128)} %collective-permute-done.refs_4_), channel_id=1, source_target_pairs={{0,1},{1,0},{2,3},{3,2},{4,5},{5,4},{6,7},{7,6},{8,9},{9,8},{10,11... | collective-permute-start | bytes 5529608 | tf_op jit(solution)/shard_map/ppermute | solution.py:152
  189.7 42.4 %collective-permute-start.3 = (f32[3600,128]{1,0:T(8,128)}, f32[3600,128]{1,0:T(8,128)S(1)}, u32[]{:S(2)}, u32[]{:S(2)}) collective-permute-start(f32[3600,128]{1,0:T(8,128)} %shard_map.31.refs_1_), channel_id=1, source_target_pairs={{0,2},{1,3},{2,0},{3,1},{4,6},{5,7},{6,4},{7,5},{8,10},{9,11},{10,... | collective-permute-start | bytes 5529608 | tf_op jit(solution)/shard_map/ppermute | solution.py:152
  191.1 42.3 %collective-permute-start.4 = (f32[3600,128]{1,0:T(8,128)}, f32[3600,128]{1,0:T(8,128)}, u32[]{:S(2)}, u32[]{:S(2)}) collective-permute-start(f32[3600,128]{1,0:T(8,128)} %shard_map.31.refs_1_), channel_id=1, source_target_pairs={{0,4},{1,5},{2,6},{3,7},{4,0},{5,1},{6,2},{7,3},{8,12},{9,13},{10,... | collective-permute-start | bytes 5529608 | tf_op jit(solution)/shard_map/ppermute | solution.py:152
  192.5 40.8 %collective-permute-start.9 = (f32[3600,128]{1,0:T(8,128)}, f32[3600,128]{1,0:T(8,128)S(1)}, u32[]{:S(2)}, u32[]{:S(2)}) collective-permute-start(f32[3600,128]{1,0:T(8,128)} %shard_map.31.refs_1_), channel_id=1, source_target_pairs={{0,1},{1,0},{2,3},{3,2},{4,5},{5,4},{6,7},{7,6},{8,9},{9,8},{10,11... | collective-permute-start | bytes 5529608 | tf_op jit(solution)/shard_map/ppermute | solution.py:152
  192.6 42.1 %collective-permute-start.8 = (f32[3600,128]{1,0:T(8,128)}, f32[3600,128]{1,0:T(8,128)}, u32[]{:S(2)}, u32[]{:S(2)}) collective-permute-start(f32[3600,128]{1,0:T(8,128)} %collective-permute-done.2.refs_12_), channel_id=1, source_target_pairs={{0,1},{1,0},{2,3},{3,2},{4,5},{5,4},{6,7},{7,6},{8,9},{9,8},{10,11... | collective-permute-start | bytes 5529608 | tf_op jit(solution)/shard_map/ppermute | solution.py:152
  232.1 25.1 %copy-start.2 = (f32[3600,128]{1,0:T(8,128)}, f32[3600,128]{1,0:T(8,128)S(1)}, u32[]{:S(2)}) copy-start(f32[3600,128]{1,0:T(8,128)S(1)} %collective-permute-done.3.refs_5_) | copy-start | bytes 5529604
  234.7 21.4 %collective-permute-start.12 = (f32[1800,128]{1,0:T(8,128)S(1)}, f32[1800,128]{1,0:T(8,128)S(1)}, u32[]{:S(2)}, u32[]{:S(2)}) collective-permute-start(f32[1800,128]{1,0:T(8,128)S(1)} %slice.21), channel_id=1, source_target_pairs={{0,4},{1,5},{2,6},{3,7},{4,0},{5,1},{6,2},{7,3},{8,12},{9,13},{10,... | collective-permute-start | bytes 2764808 | tf_op jit(solution)/shard_map/ppermute | solution.py:152
  237.5 22.1 %slice-start.2 = ((f32[512,1920]{1,0:T(8,128)}), f32[512,256]{1,0:T(8,128)S(1)}, s32[]{:S(2)}) async-start(f32[512,1920]{1,0:T(8,128)} %param.3), calls=%async_computation.8 | async-start | bytes 1048576 | tf_op jit(solution)/shard_map/slice | solution.py:156
  237.5 21.1 %collective-permute-start.13 = (f32[1800,128]{1,0:T(8,128)S(1)}, f32[1800,128]{1,0:T(8,128)S(1)}, u32[]{:S(2)}, u32[]{:S(2)}) collective-permute-start(f32[1800,128]{1,0:T(8,128)S(1)} %slice.22), channel_id=1, source_target_pairs={{0,2},{1,3},{2,0},{3,1},{4,6},{5,7},{6,4},{7,5},{8,10},{9,11},{10,... | collective-permute-start | bytes 2764808 | tf_op jit(solution)/shard_map/ppermute | solution.py:152
  238.3 22.2 %collective-permute-start.10 = (f32[3600,128]{1,0:T(8,128)S(1)}, f32[3600,128]{1,0:T(8,128)}, u32[]{:S(2)}, u32[]{:S(2)}) collective-permute-start(f32[3600,128]{1,0:T(8,128)S(1)} %collective-permute-done.3.refs_5_), channel_id=1, source_target_pairs={{0,1},{1,0},{2,3},{3,2},{4,5},{5,4},{6,7},{7,6},{8,9},{9,8},{10,11... | collective-permute-start | bytes 5529608 | tf_op jit(solution)/shard_map/ppermute | solution.py:152
  238.3 22.2 %collective-permute-start.11 = (f32[3600,128]{1,0:T(8,128)}, f32[3600,128]{1,0:T(8,128)}, u32[]{:S(2)}, u32[]{:S(2)}) collective-permute-start(f32[3600,128]{1,0:T(8,128)} %collective-permute-done.4.refs_9_), channel_id=1, source_target_pairs={{0,1},{1,0},{2,3},{3,2},{4,5},{5,4},{6,7},{7,6},{8,9},{9,8},{10,11... | collective-permute-start | bytes 5529608 | tf_op jit(solution)/shard_map/ppermute | solution.py:152
  259.6 4.1 collective-permute-start.14
  263.7 66.7 %copy-start.1 = (f32[2048,128]{1,0:T(8,128)S(1)}, f32[2048,128]{1,0:T(8,128)}, u32[]{:S(2)}) copy-start(f32[2048,128]{1,0:T(8,128)} %all-gather.5.cloned.1.call-done) | copy-start | bytes 3145732
  (4 other events, 5.4 us)
Sparse Core Ops, SparseCore 0:
  19.0 52.6 all-gather.4
  74.3 189.0 all-gather.6
  265.0 80.5 all-gather.8
  347.0 44.5 all-gather.10

commit v9 on v3

--- a/solution.py
+++ b/solution.py
@@ -74,69 +74,82 @@
     return high, (x - high.astype(jnp.float32)).astype(jnp.bfloat16)
 
 
-def product_kernel(devices, place_ref, *refs):
-    parts, w_hbm = refs[: 2 * devices], refs[2 * devices]
-    out_ref, t_ref, w, w_high, w_low, t_high, t_low, arrived = refs[-8:]
-    depth, width = w.shape
-    block = depth // devices
+def product_kernel(halves, added, place_ref, *refs):
+    out_ref, w, w_high, w_low, t_high, t_low, arrived = refs[-7:]
+    count = arrived.shape[0]
+    parts, w_hbm = refs[:count], refs[count]
+    size = w.shape[0] // count
 
     @pl.when(pl.program_id(0) == 0)
     def _():
-        whole = pltpu.make_async_copy(w_hbm, w, arrived)
-        whole.start()
-        whole.wait()
-        for n in range(devices):
-            rows = slice(n * block, (n + 1) * block)
+        copies = []
+        for n in range(count):
+            block = place_ref[0] ^ (n // len(halves))
+            start = (2 * block + halves[n % len(halves)]) * size
+            rows = pl.ds(pl.multiple_of(start, size), size)
+            to = w.at[pl.ds(n * size, size)]
+            copies.append(pltpu.make_async_copy(w_hbm.at[rows], to, arrived.at[n]))
+            copies[-1].start()
+        for n, copy in enumerate(copies):
+            copy.wait()
+        for n in range(count):
+            rows = slice(n * size, (n + 1) * size)
             w_high[rows, :], w_low[rows, :] = split(w[rows, :])
 
-    for n in range(devices):
-        value = jnp.concatenate([parts[2 * n][...], parts[2 * n + 1][...]], axis=1)
-        to = pl.ds(pl.multiple_of((place_ref[0] ^ n) * block, block), block)
-        t_ref[:, to] = value
-        t_high[:, to], t_low[:, to] = split(value)
+    for n, part in enumerate(parts):
+        to = slice(n * size, (n + 1) * size)
+        t_high[:, to], t_low[:, to] = split(part[...])
     dot = functools.partial(jnp.dot, preferred_element_type=jnp.float32)
     total = dot(t_low[...], w_high[...])
     total += dot(t_high[...], w_low[...])
     total += dot(t_high[...], w_high[...])
-    out_ref[:, :width] = 0.5 * total
-
-
-def product(place, parts, w, chunk, full):
+    width = w.shape[1]
+    if added:
+        out_ref[:, :width] = refs[count + 1][:, :width] + 0.5 * total
+    else:
+        out_ref[:, :width] = 0.5 * total
+
+
+def product(place, parts, halves, w, out, added, chunk, full):
     start, width, block = chunk
     rows, size = parts[0].shape
-    depth = w.shape[0]
+    count = len(parts)
+    depth = size * count
+    anywhere = pl.BlockSpec(memory_space=pl.ANY)
+    out_spec = pl.BlockSpec((ROWS, block), lambda i, p: (i, start // block))
+    operands = [place, *parts, w]
+    in_specs = [pl.BlockSpec((ROWS, size), lambda i, p: (i, 0))] * count + [anywhere]
+    aliases = {}
+    if out is not None:
+        aliases = {len(operands): 0}
+        operands.append(out)
+        in_specs.append(out_spec if added else anywhere)
     t_half = pltpu.VMEM((ROWS, depth), jnp.bfloat16)
     w_half = pltpu.VMEM((depth, width), jnp.bfloat16)
     return pl.pallas_call(
-        functools.partial(product_kernel, len(parts) // 2),
+        functools.partial(product_kernel, halves, added),
         grid_spec=pltpu.PrefetchScalarGridSpec(
             num_scalar_prefetch=1,
             grid=(pl.cdiv(rows, ROWS),),
-            in_specs=[pl.BlockSpec((ROWS, size), lambda i, p: (i, 0))] * len(parts)
-            + [pl.BlockSpec(memory_space=pl.ANY)],
-            out_specs=[
-                pl.BlockSpec((ROWS, block), lambda i, p: (i, start // block)),
-                pl.BlockSpec((ROWS, depth), lambda i, p: (i, 0)),
-            ],
+            in_specs=in_specs,
+            out_specs=out_spec,
             scratch_shapes=[
                 pltpu.VMEM((depth, width), jnp.float32),
                 w_half,
                 w_half,
                 t_half,
                 t_half,
-                pltpu.SemaphoreType.DMA(()),
+                pltpu.SemaphoreType.DMA((count,)),
             ],
         ),
-        out_shape=[
-            jax.ShapeDtypeStruct((rows, full), jnp.float32),
-            jax.ShapeDtypeStruct((rows, depth), jnp.float32),
-        ],
+        out_shape=jax.ShapeDtypeStruct((rows, full), jnp.float32),
+        input_output_aliases=aliases,
         compiler_params=params(),
         cost_estimate=moved(
-            4 * (2 * rows * depth + depth * width + rows * width),
+            4 * (rows * depth + depth * width + rows * width),
             6 * rows * depth * width,
         ),
-    )(place, *parts, w)
+    )(*operands)
 
 
 def tie(*values):
@@ -174,13 +187,22 @@
     masks = [1 << bit for bit in range(1, devices.bit_length() - 1)]
     orders = (masks[::-1], masks)
     across = [{}, {}]
+    place = lax.axis_index("ka").astype(jnp.int32).reshape(1)
+
+    def parts_of(half):
+        both = held[half], across[half]
+        return [both[n % 2][n - n % 2] for n in range(devices)]
+
     for half, order in enumerate(orders):
         blocks = held[half]
         if half:
             across[1] = {0: swap(blocks[0], 1)}
         for level in range(1, len(masks) + 1):
             if half and level == 2:
-                held, across, source = tie(held, across, integrals)
+                out = product(
+                    place, parts_of(0), (0,), gathered[0], None, False, chunks[0], columns
+                )
+                held, across, source, out = tie(held, across, integrals, out)
                 gathered += [gather(n, source) for n in range(2, len(chunks))]
                 blocks = held[1]
             if half and level == 2 == len(masks):
@@ -195,22 +217,12 @@
                     blocks[n] = swap(blocks[n ^ last], last)
         for n in sorted(blocks.keys() - across[half].keys()):
             across[half][n] = swap(blocks[n], 1)
-    parts = [
-        (across if n % 2 else held)[half][n - n % 2]
-        for n in range(devices)
-        for half in range(2)
-    ]
-
-    place = lax.axis_index("ka").astype(jnp.int32)
-    out, whole = product(place.reshape(1), parts, gathered[0], chunks[0], columns)
-    for (start, _, _), w in zip(chunks[1:], gathered[1:]):
-        ladder = jnp.dot(
-            whole,
-            w,
-            precision=lax.Precision.HIGH,
-            preferred_element_type=jnp.float32,
-        )
-        out = lax.dynamic_update_slice_in_dim(out, 0.5 * ladder, start, axis=1)
+    out = product(
+        place, parts_of(1), (1,), gathered[0], out, True, chunks[0], columns
+    )
+    parts = [x for pair in zip(parts_of(0), parts_of(1)) for x in pair]
+    for chunk, w in zip(chunks[1:], gathered[1:]):
+        out = product(place, parts, (0, 1), w, out, False, chunk, columns)
     return out
 
 

time: 429 us -> 419 us (0.977)
  Pallas kernels: 84.9 us -> 150 us
  matrix products: 61.1 us -> 0 us
  waiting for transfers between devices: 228 us -> 215 us
    pallas_call x1 -> x4, Pallas kernels: 66.6 us -> 132 us  [product(): pl.pallas_call(functools.partial(product_kernel, halves, added), grid_spe...]
    dot_general x2 -> x0, matrix products: 61.1 us -> none  [per_device(): jnp.dot(whole, w, precision=lax.Precision.HIGH, preferred_element_type=jn...]
    ppermute x15, waiting for transfers between devices: 96.3 us -> 86.4 us  [swap(): return lax.ppermute(x, 'ka', [(d, d ^ mask) for d in range(devices)])]
  transfers between devices with their start and end apart: 20 -> 20, of which waited for: 9 -> 9; matrix products, arithmetic and copies ran while one was open for 11% -> 1% of each run, Pallas kernels for 20% -> 31%
where the time goes in v9:
time: 419 us; the launch traced here: 413 us
  waiting for transfers between devices  215 us (51%)
  Pallas kernels  150 us (36%)
  starting transfers between devices  22 us (5%)
  between operations  13.2 us (3%)
  local copies, waits for them, and re-layouts  12.3 us (3%)
    pallas_call x4, Pallas kernels, product(): pl.pallas_call(functools.partial(product_kernel, halves, added), grid_spe...  132 us
    all_to_all x2, waiting for transfers between devices, per_device(): lax.all_to_all(blocks, 'ga', split_axis=0, concat_axis=0, tiled=True)  128 us
    ppermute x15, waiting for transfers between devices, swap(): return lax.ppermute(x, 'ka', [(d, d ^ mask) for d in range(devices)])  86.4 us
    all_to_all x2, starting transfers between devices, per_device(): lax.all_to_all(blocks, 'ga', split_axis=0, concat_axis=0, tiled=True)  12.1 us
    pallas_call x2, Pallas kernels, turn(): pl.pallas_call(turn_kernel, grid=(pl.cdiv(rows, width),), in_specs=[pl.Bl...  11.6 us
    ppermute x15, starting transfers between devices, swap(): return lax.ppermute(x, 'ka', [(d, d ^ mask) for d in range(devices)])  9.81 us
  transfers between devices with their start and end apart: 20, of which 9 were waited for; matrix products, arithmetic and copies ran while one was open for 1% of the time, Pallas kernels for 31%

profile of v9, /device:TPU:16, one launch (start us, length us, event | category | flops | bytes accessed | tf_op | source)
XLA Modules:
  0.0 412.6 jit_solution(5963891590633755770)
XLA Ops:
  6.5 1.6 slice-done
  9.6 3.2 shard_map.29
  12.9 5.2 %all-to-all-start = ((f32[4,32,3600]{2,1,0:T(8,128)}), f32[4,32,3600]{2,1,0:T(8,128)S(1)}, u32[]{:S(2)}, u32[]{:S(2)}) async-start(f32[4,32,3600]{2,1,0:T(8,128)} %shard_map.29), calls=%async_computation | async-start | bytes 3801088 | tf_op jit(solution)/shard_map/all_to_all | solution.py:183
  18.1 3.4 shard_map.28
  21.5 91.5 %all-to-all-done = f32[4,32,3600]{2,1,0:T(8,128)S(1)} async-done(((f32[4,32,3600]{2,1,0:T(8,128)}), f32[4,32,3600]{2,1,0:T(8,128)S(1)}, u32[]{:S(2)}, u32[]{:S(2)}) %all-to-all-start) | async-done | bytes 1843232 | tf_op jit(solution)/shard_map/all_to_all | solution.py:183
  114.3 5.8 %shard_map.30.refs_0_ = f32[3600,128]{1,0:T(8,128)} custom-call(f32[128,3600]{1,0:T(8,128)} %bitcast.23), custom_call_target="tpu_custom_call" | custom-call | bytes 3686400 | tf_op jit(solution)/shard_map/pallas_call | solution.py:61
  120.1 1.5 collective-permute-start.1
  121.6 1.5 collective-permute-start
  123.1 30.7 %collective-permute-done.1.refs_4_.refs_8_ = f32[3600,128]{1,0:T(8,128)} collective-permute-done((f32[3600,128]{1,0:T(8,128)}, f32[3600,128]{1,0:T(8,128)}, u32[]{:S(2)}, u32[]{:S(2)}) %collective-permute-start.1) | collective-permute-done | bytes 1843232 | tf_op jit(solution)/shard_map/ppermute | solution.py:165
  153.8 1.5 collective-permute-start.2
  155.3 6.9 %all-to-all-start.1 = ((f32[4,32,3600]{2,1,0:T(8,128)}), f32[4,32,3600]{2,1,0:T(8,128)S(1)}, u32[]{:S(2)}, u32[]{:S(2)}) async-start(f32[4,32,3600]{2,1,0:T(8,128)} %shard_map.28), calls=%async_computation.1 | async-start | bytes 3801088 | tf_op jit(solution)/shard_map/all_to_all | solution.py:183
  165.4 29.1 %collective-permute-done.2.refs_6_.refs_12_ = f32[3600,128]{1,0:T(8,128)} collective-permute-done((f32[3600,128]{1,0:T(8,128)}, f32[3600,128]{1,0:T(8,128)}, u32[]{:S(2)}, u32[]{:S(2)}) %collective-permute-start.2) | collective-permute-done | bytes 1843232 | tf_op jit(solution)/shard_map/ppermute | solution.py:165
  194.5 36.8 %all-to-all-done.1 = f32[4,32,3600]{2,1,0:T(8,128)S(1)} async-done(((f32[4,32,3600]{2,1,0:T(8,128)}), f32[4,32,3600]{2,1,0:T(8,128)S(1)}, u32[]{:S(2)}, u32[]{:S(2)}) %all-to-all-start.1) | async-done | bytes 1843232 | tf_op jit(solution)/shard_map/all_to_all | solution.py:183
  232.6 5.8 %shard_map.31.refs_0_.refs_1_ = f32[3600,128]{1,0:T(8,128)} custom-call(f32[128,3600]{1,0:T(8,128)} %bitcast.22), custom_call_target="tpu_custom_call" | custom-call | bytes 3686400 | tf_op jit(solution)/shard_map/pallas_call | solution.py:61
  239.3 1.5 collective-permute-start.4
  240.9 31.2 %shard_map.32.refs_9_ = f32[3600,1920]{1,0:T(8,128)} custom-call(s32[1]{0:T(128)} %bitcast.place_ref, f32[3600,128]{1,0:T(8,128)} %shard_map.30.refs_0_, f32[3600,128]{1,0:T(8,128)} %collective-permute-done.5.refs_1_.refs_2_, f32[3600,128]{1,0:T(8,128)} %collective-permute-done.refs_2_.refs_4_, f32[3600,128]{1,0:T(8,128)} %collective-permute-done.6.refs_3_.refs_6_, ...), custom_call_target="tpu_custom_call" | custom-call | flops 22649241600 | bytes 33685504 | tf_op jit(solution)/shard_map/pallas_call | solution.py:129
  272.1 5.2 %collective-permute-done.3.refs_2_.refs_5_ = f32[3600,128]{1,0:T(8,128)S(1)} collective-permute-done((f32[3600,128]{1,0:T(8,128)}, f32[3600,128]{1,0:T(8,128)S(1)}, u32[]{:S(2)}, u32[]{:S(2)}) %collective-permute-start.3) | collective-permute-done | bytes 1843232 | tf_op jit(solution)/shard_map/ppermute | solution.py:165
  277.3 2.5 collective-permute-done.4.refs_4_.refs_9_
  279.8 1.6 collective-permute-start.12
  283.3 15.2 %collective-permute-done.12 = f32[1800,128]{1,0:T(8,128)S(1)} collective-permute-done((f32[1800,128]{1,0:T(8,128)S(1)}, f32[1800,128]{1,0:T(8,128)S(1)}, u32[]{:S(2)}, u32[]{:S(2)}) %collective-permute-start.12) | collective-permute-done | bytes 921632 | tf_op jit(solution)/shard_map/ppermute | solution.py:165
  302.0 3.2 collective-permute-done.14.refs_7_.refs_15_
  305.2 32.9 %shard_map.33.refs_17_ = f32[3600,1920]{1,0:T(8,128)} custom-call(s32[1]{0:T(128)} %bitcast.place_ref, f32[3600,128]{1,0:T(8,128)} %shard_map.31.refs_0_.refs_1_, f32[3600,128]{1,0:T(8,128)} %collective-permute-done.9.refs_1_.refs_3_, f32[3600,128]{1,0:T(8,128)} %copy-done.2, ...), custom_call_target="tpu_custom_call", output_to_operand_aliasing={{}: (10, {})} | custom-call | flops 22649241600 | bytes 33685504 | tf_op jit(solution)/shard_map/pallas_call | solution.py:129
  338.2 44.3 %shard_map.34.refs_17_ = f32[3600,1920]{1,0:T(8,128)} custom-call(s32[1]{0:T(128)} %bitcast.place_ref, f32[3600,128]{1,0:T(8,128)} %shard_map.30.refs_0_, f32[3600,128]{1,0:T(8,128)} %shard_map.31.refs_0_.refs_1_, f32[3600,128]{1,0:T(8,128)} %collective-permute-done.5.refs_1_.refs_2_, ...), custom_call_target="tpu_custom_call", output_to_operand_aliasing={{}: (18, {})} | custom-call | flops 28311552000 | bytes 43950080 | tf_op jit(solution)/shard_map/pallas_call | solution.py:129
  382.5 23.5 %shard_map.35 = f32[3600,1920]{1,0:T(8,128)} custom-call(s32[1]{0:T(128)} %bitcast.place_ref, f32[3600,128]{1,0:T(8,128)} %shard_map.30.refs_0_, f32[3600,128]{1,0:T(8,128)} %shard_map.31.refs_0_.refs_1_, f32[3600,128]{1,0:T(8,128)} %collective-permute-done.5.refs_1_.refs_2_, ...), custom_call_target="tpu_custom_call", output_to_operand_aliasing={{}: (18, {})} | custom-call | flops 11324620800 | bytes 35274752 | tf_op jit(solution)/shard_map/pallas_call | solution.py:129
  (46 shorter events, 13.7 us)
Async XLA Ops:
  6.5 1.6 slice-start
  6.5 234.3 %all-gather.4.cloned.1.call-start = ((), (), s32[]{:S(2)}) async-start(), calls=%async_computation.2 | async-start | bytes 10485760 | tf_op jit(solution)/shard_map/all_gather | solution.py:171
  12.9 100.1 %all-to-all-start = ((f32[4,32,3600]{2,1,0:T(8,128)}), f32[4,32,3600]{2,1,0:T(8,128)S(1)}, u32[]{:S(2)}, u32[]{:S(2)}) async-start(f32[4,32,3600]{2,1,0:T(8,128)} %shard_map.29), calls=%async_computation | async-start | bytes 3801088 | tf_op jit(solution)/shard_map/all_to_all | solution.py:183
  120.1 33.7 %collective-permute-start.1 = (f32[3600,128]{1,0:T(8,128)}, f32[3600,128]{1,0:T(8,128)}, u32[]{:S(2)}, u32[]{:S(2)}) collective-permute-start(f32[3600,128]{1,0:T(8,128)} %shard_map.30.refs_0_), channel_id=1, source_target_pairs={{0,4},{1,5},{2,6},{3,7},{4,0},{5,1},{6,2},{7,3},{8,12},{9,13},{10,... | collective-permute-start | bytes 5529608 | tf_op jit(solution)/shard_map/ppermute | solution.py:165
  121.6 43.8 %collective-permute-start = (f32[3600,128]{1,0:T(8,128)}, f32[3600,128]{1,0:T(8,128)}, u32[]{:S(2)}, u32[]{:S(2)}) collective-permute-start(f32[3600,128]{1,0:T(8,128)} %shard_map.30.refs_0_), channel_id=1, source_target_pairs={{0,2},{1,3},{2,0},{3,1},{4,6},{5,7},{6,4},{7,5},{8,10},{9,11},{10,... | collective-permute-start | bytes 5529608 | tf_op jit(solution)/shard_map/ppermute | solution.py:165
  153.8 40.7 %collective-permute-start.2 = (f32[3600,128]{1,0:T(8,128)}, f32[3600,128]{1,0:T(8,128)}, u32[]{:S(2)}, u32[]{:S(2)}) collective-permute-start(f32[3600,128]{1,0:T(8,128)} %collective-permute-done.1.refs_4_.refs_8_), channel_id=1, source_target_pairs={{0,2},{1,3},{2,0},{3,1},{4,6},{5,7},{6,4},{7,5},{8,10},{9,11},{10,... | collective-permute-start | bytes 5529608 | tf_op jit(solution)/shard_map/ppermute | solution.py:165
  155.3 76.1 %all-to-all-start.1 = ((f32[4,32,3600]{2,1,0:T(8,128)}), f32[4,32,3600]{2,1,0:T(8,128)S(1)}, u32[]{:S(2)}, u32[]{:S(2)}) async-start(f32[4,32,3600]{2,1,0:T(8,128)} %shard_map.28), calls=%async_computation.1 | async-start | bytes 3801088 | tf_op jit(solution)/shard_map/all_to_all | solution.py:183
  162.2 1.3 slice-start.1
  162.2 176.0 %all-gather.8.cloned.1.call-start = ((), (), s32[]{:S(2)}) async-start(), calls=%async_computation.4 | async-start | bytes 6553600 | tf_op jit(solution)/shard_map/all_gather | solution.py:171
  164.7 217.8 %all-gather.6.cloned.1.call-start = ((), (), s32[]{:S(2)}) async-start(), calls=%async_computation.3 | async-start | bytes 2621440 | tf_op jit(solution)/shard_map/all_gather | solution.py:171
  164.8 74.5 %collective-permute-start.5 = (f32[3600,128]{1,0:T(8,128)}, f32[3600,128]{1,0:T(8,128)}, u32[]{:S(2)}, u32[]{:S(2)}) collective-permute-start(f32[3600,128]{1,0:T(8,128)} %shard_map.30.refs_0_), channel_id=1, source_target_pairs={{0,1},{1,0},{2,3},{3,2},{4,5},{5,4},{6,7},{7,6},{8,9},{9,8},{10,11... | collective-permute-start | bytes 5529608 | tf_op jit(solution)/shard_map/ppermute | solution.py:165
  164.9 76.0 %collective-permute-start.7 = (f32[3600,128]{1,0:T(8,128)}, f32[3600,128]{1,0:T(8,128)}, u32[]{:S(2)}, u32[]{:S(2)}) collective-permute-start(f32[3600,128]{1,0:T(8,128)} %collective-permute-done.1.refs_4_.refs_8_), channel_id=1, source_target_pairs={{0,1},{1,0},{2,3},{3,2},{4,5},{5,4},{6,7},{7,6},{8,9},{9,8},{10,11... | collective-permute-start | bytes 5529608 | tf_op jit(solution)/shard_map/ppermute | solution.py:165
  165.4 75.5 %collective-permute-start.6 = (f32[3600,128]{1,0:T(8,128)}, f32[3600,128]{1,0:T(8,128)}, u32[]{:S(2)}, u32[]{:S(2)}) collective-permute-start(f32[3600,128]{1,0:T(8,128)} %collective-permute-done.refs_2_.refs_4_), channel_id=1, source_target_pairs={{0,1},{1,0},{2,3},{3,2},{4,5},{5,4},{6,7},{7,6},{8,9},{9,8},{10,11... | collective-permute-start | bytes 5529608 | tf_op jit(solution)/shard_map/ppermute | solution.py:165
  194.5 46.3 %collective-permute-start.8 = (f32[3600,128]{1,0:T(8,128)}, f32[3600,128]{1,0:T(8,128)}, u32[]{:S(2)}, u32[]{:S(2)}) collective-permute-start(f32[3600,128]{1,0:T(8,128)} %collective-permute-done.2.refs_6_.refs_12_), channel_id=1, source_target_pairs={{0,1},{1,0},{2,3},{3,2},{4,5},{5,4},{6,7},{7,6},{8,9},{9,8},{10,11... | collective-permute-start | bytes 5529608 | tf_op jit(solution)/shard_map/ppermute | solution.py:165
  238.4 38.8 %collective-permute-start.3 = (f32[3600,128]{1,0:T(8,128)}, f32[3600,128]{1,0:T(8,128)S(1)}, u32[]{:S(2)}, u32[]{:S(2)}) collective-permute-start(f32[3600,128]{1,0:T(8,128)} %shard_map.31.refs_0_.refs_1_), channel_id=1, source_target_pairs={{0,2},{1,3},{2,0},{3,1},{4,6},{5,7},{6,4},{7,5},{8,10},{9,11},{10,... | collective-permute-start | bytes 5529608 | tf_op jit(solution)/shard_map/ppermute | solution.py:165
  239.3 40.4 %collective-permute-start.4 = (f32[3600,128]{1,0:T(8,128)}, f32[3600,128]{1,0:T(8,128)}, u32[]{:S(2)}, u32[]{:S(2)}) collective-permute-start(f32[3600,128]{1,0:T(8,128)} %shard_map.31.refs_0_.refs_1_), channel_id=1, source_target_pairs={{0,4},{1,5},{2,6},{3,7},{4,0},{5,1},{6,2},{7,3},{8,12},{9,13},{10,... | collective-permute-start | bytes 5529608 | tf_op jit(solution)/shard_map/ppermute | solution.py:165
  240.8 38.9 %collective-permute-start.9 = (f32[3600,128]{1,0:T(8,128)}, f32[3600,128]{1,0:T(8,128)}, u32[]{:S(2)}, u32[]{:S(2)}) collective-permute-start(f32[3600,128]{1,0:T(8,128)} %shard_map.31.refs_0_.refs_1_), channel_id=1, source_target_pairs={{0,1},{1,0},{2,3},{3,2},{4,5},{5,4},{6,7},{7,6},{8,9},{9,8},{10,11... | collective-permute-start | bytes 5529608 | tf_op jit(solution)/shard_map/ppermute | solution.py:165
  277.3 5.6 %copy-start.2 = (f32[3600,128]{1,0:T(8,128)}, f32[3600,128]{1,0:T(8,128)S(1)}, u32[]{:S(2)}) copy-start(f32[3600,128]{1,0:T(8,128)S(1)} %collective-permute-done.3.refs_2_.refs_5_) | copy-start | bytes 5529604
  279.8 18.7 %collective-permute-start.12 = (f32[1800,128]{1,0:T(8,128)S(1)}, f32[1800,128]{1,0:T(8,128)S(1)}, u32[]{:S(2)}, u32[]{:S(2)}) collective-permute-start(f32[1800,128]{1,0:T(8,128)S(1)} %slice.16), channel_id=1, source_target_pairs={{0,4},{1,5},{2,6},{3,7},{4,0},{5,1},{6,2},{7,3},{8,12},{9,13},{10,... | collective-permute-start | bytes 2764808 | tf_op jit(solution)/shard_map/ppermute | solution.py:165
  282.6 17.4 %collective-permute-start.13 = (f32[1800,128]{1,0:T(8,128)S(1)}, f32[1800,128]{1,0:T(8,128)S(1)}, u32[]{:S(2)}, u32[]{:S(2)}) collective-permute-start(f32[1800,128]{1,0:T(8,128)S(1)} %slice.17), channel_id=1, source_target_pairs={{0,2},{1,3},{2,0},{3,1},{4,6},{5,7},{6,4},{7,5},{8,10},{9,11},{10,... | collective-permute-start | bytes 2764808 | tf_op jit(solution)/shard_map/ppermute | solution.py:165
  282.8 19.2 %collective-permute-start.10 = (f32[3600,128]{1,0:T(8,128)S(1)}, f32[3600,128]{1,0:T(8,128)}, u32[]{:S(2)}, u32[]{:S(2)}) collective-permute-start(f32[3600,128]{1,0:T(8,128)S(1)} %collective-permute-done.3.refs_2_.refs_5_), channel_id=1, source_target_pairs={{0,1},{1,0},{2,3},{3,2},{4,5},{5,4},{6,7},{7,6},{8,9},{9,8},{10,11... | collective-permute-start | bytes 5529608 | tf_op jit(solution)/shard_map/ppermute | solution.py:165
  282.8 19.2 %collective-permute-start.11 = (f32[3600,128]{1,0:T(8,128)}, f32[3600,128]{1,0:T(8,128)}, u32[]{:S(2)}, u32[]{:S(2)}) collective-permute-start(f32[3600,128]{1,0:T(8,128)} %collective-permute-done.4.refs_4_.refs_9_), channel_id=1, source_target_pairs={{0,1},{1,0},{2,3},{3,2},{4,5},{5,4},{6,7},{7,6},{8,9},{9,8},{10,11... | collective-permute-start | bytes 5529608 | tf_op jit(solution)/shard_map/ppermute | solution.py:165
  299.5 1.6 slice-start.2
  301.1 4.1 %collective-permute-start.14 = (f32[3600,128]{1,0:T(8,128)}, f32[3600,128]{1,0:T(8,128)}, u32[]{:S(2)}, u32[]{:S(2)}) collective-permute-start(f32[3600,128]{1,0:T(8,128)} %constant_dynamic-update-slice_fusion.refs_6_.refs_13_), channel_id=1, source_target_pairs={{0,1},{1,0},{2,3},{3,2},{4,5},{5,4},{6,7},{7,6},{8,9},{9,8},{10,11... | collective-permute-start | bytes 5529608 | tf_op jit(solution)/shard_map/ppermute | solution.py:165
  (2 other events, 2.6 us)
Sparse Core Ops, SparseCore 0:
  9.7 224.8 all-gather.3
  236.2 98.6 all-gather.7
  336.5 44.5 all-gather.5

commit v10 on v9

--- a/solution.py
+++ b/solution.py
@@ -114,23 +114,24 @@
     start, width, block = chunk
     rows, size = parts[0].shape
     count = len(parts)
+    tile = ROWS if width > 256 else 3 * ROWS
     depth = size * count
     anywhere = pl.BlockSpec(memory_space=pl.ANY)
-    out_spec = pl.BlockSpec((ROWS, block), lambda i, p: (i, start // block))
+    out_spec = pl.BlockSpec((tile, block), lambda i, p: (i, start // block))
     operands = [place, *parts, w]
-    in_specs = [pl.BlockSpec((ROWS, size), lambda i, p: (i, 0))] * count + [anywhere]
+    in_specs = [pl.BlockSpec((tile, size), lambda i, p: (i, 0))] * count + [anywhere]
     aliases = {}
     if out is not None:
         aliases = {len(operands): 0}
         operands.append(out)
         in_specs.append(out_spec if added else anywhere)
-    t_half = pltpu.VMEM((ROWS, depth), jnp.bfloat16)
+    t_half = pltpu.VMEM((tile, depth), jnp.bfloat16)
     w_half = pltpu.VMEM((depth, width), jnp.bfloat16)
     return pl.pallas_call(
         functools.partial(product_kernel, halves, added),
         grid_spec=pltpu.PrefetchScalarGridSpec(
             num_scalar_prefetch=1,
-            grid=(pl.cdiv(rows, ROWS),),
+            grid=(pl.cdiv(rows, tile),),
             in_specs=in_specs,
             out_specs=out_spec,
             scratch_shapes=[

time: 419 us -> 415 us (level)
  no operation moved by 1% of the time
where the time goes in v10:
time: 415 us; the launch traced here: 409 us
  waiting for transfers between devices  215 us (52%)
  Pallas kernels  146 us (35%)
  starting transfers between devices  22 us (5%)
  between operations  13.2 us (3%)
  local copies, waits for them, and re-layouts  12.3 us (3%)
    all_to_all x2, waiting for transfers between devices, per_device(): lax.all_to_all(blocks, 'ga', split_axis=0, concat_axis=0, tiled=True)  128 us
    pallas_call x4, Pallas kernels, product(): pl.pallas_call(functools.partial(product_kernel, halves, added), grid_spe...  128 us
    ppermute x15, waiting for transfers between devices, swap(): return lax.ppermute(x, 'ka', [(d, d ^ mask) for d in range(devices)])  86.4 us
    all_to_all x2, starting transfers between devices, per_device(): lax.all_to_all(blocks, 'ga', split_axis=0, concat_axis=0, tiled=True)  12.1 us
    pallas_call x2, Pallas kernels, turn(): pl.pallas_call(turn_kernel, grid=(pl.cdiv(rows, width),), in_specs=[pl.Bl...  11.6 us
    ppermute x15, starting transfers between devices, swap(): return lax.ppermute(x, 'ka', [(d, d ^ mask) for d in range(devices)])  9.81 us
  transfers between devices with their start and end apart: 20, of which 9 were waited for; matrix products, arithmetic and copies ran while one was open for 1% of the time, Pallas kernels for 31%

profile of v10, /device:TPU:16, one launch (start us, length us, event | category | flops | bytes accessed | tf_op | source)
XLA Modules:
  0.0 408.8 jit_solution(2231146273208563890)
XLA Ops:
  6.5 1.6 slice-done
  9.6 3.2 shard_map.29
  12.9 5.2 %all-to-all-start = ((f32[4,32,3600]{2,1,0:T(8,128)}), f32[4,32,3600]{2,1,0:T(8,128)S(1)}, u32[]{:S(2)}, u32[]{:S(2)}) async-start(f32[4,32,3600]{2,1,0:T(8,128)} %shard_map.29), calls=%async_computation | async-start | bytes 3801088 | tf_op jit(solution)/shard_map/all_to_all | solution.py:184
  18.1 3.4 shard_map.28
  21.5 91.5 %all-to-all-done = f32[4,32,3600]{2,1,0:T(8,128)S(1)} async-done(((f32[4,32,3600]{2,1,0:T(8,128)}), f32[4,32,3600]{2,1,0:T(8,128)S(1)}, u32[]{:S(2)}, u32[]{:S(2)}) %all-to-all-start) | async-done | bytes 1843232 | tf_op jit(solution)/shard_map/all_to_all | solution.py:184
  114.3 5.8 %shard_map.30.refs_0_ = f32[3600,128]{1,0:T(8,128)} custom-call(f32[128,3600]{1,0:T(8,128)} %bitcast.23), custom_call_target="tpu_custom_call" | custom-call | bytes 3686400 | tf_op jit(solution)/shard_map/pallas_call | solution.py:61
  120.1 1.5 collective-permute-start.1
  121.6 1.5 collective-permute-start
  123.1 30.7 %collective-permute-done.1.refs_4_.refs_8_ = f32[3600,128]{1,0:T(8,128)} collective-permute-done((f32[3600,128]{1,0:T(8,128)}, f32[3600,128]{1,0:T(8,128)}, u32[]{:S(2)}, u32[]{:S(2)}) %collective-permute-start.1) | collective-permute-done | bytes 1843232 | tf_op jit(solution)/shard_map/ppermute | solution.py:166
  153.8 1.5 collective-permute-start.2
  155.3 6.9 %all-to-all-start.1 = ((f32[4,32,3600]{2,1,0:T(8,128)}), f32[4,32,3600]{2,1,0:T(8,128)S(1)}, u32[]{:S(2)}, u32[]{:S(2)}) async-start(f32[4,32,3600]{2,1,0:T(8,128)} %shard_map.28), calls=%async_computation.1 | async-start | bytes 3801088 | tf_op jit(solution)/shard_map/all_to_all | solution.py:184
  165.4 29.1 %collective-permute-done.2.refs_6_.refs_12_ = f32[3600,128]{1,0:T(8,128)} collective-permute-done((f32[3600,128]{1,0:T(8,128)}, f32[3600,128]{1,0:T(8,128)}, u32[]{:S(2)}, u32[]{:S(2)}) %collective-permute-start.2) | collective-permute-done | bytes 1843232 | tf_op jit(solution)/shard_map/ppermute | solution.py:166
  194.5 36.8 %all-to-all-done.1 = f32[4,32,3600]{2,1,0:T(8,128)S(1)} async-done(((f32[4,32,3600]{2,1,0:T(8,128)}), f32[4,32,3600]{2,1,0:T(8,128)S(1)}, u32[]{:S(2)}, u32[]{:S(2)}) %all-to-all-start.1) | async-done | bytes 1843232 | tf_op jit(solution)/shard_map/all_to_all | solution.py:184
  232.6 5.8 %shard_map.31.refs_0_.refs_1_ = f32[3600,128]{1,0:T(8,128)} custom-call(f32[128,3600]{1,0:T(8,128)} %bitcast.22), custom_call_target="tpu_custom_call" | custom-call | bytes 3686400 | tf_op jit(solution)/shard_map/pallas_call | solution.py:61
  239.3 1.5 collective-permute-start.4
  240.9 31.2 %shard_map.32.refs_9_ = f32[3600,1920]{1,0:T(8,128)} custom-call(s32[1]{0:T(128)} %bitcast.place_ref, f32[3600,128]{1,0:T(8,128)} %shard_map.30.refs_0_, f32[3600,128]{1,0:T(8,128)} %collective-permute-done.5.refs_1_.refs_2_, f32[3600,128]{1,0:T(8,128)} %collective-permute-done.refs_2_.refs_4_, f32[3600,128]{1,0:T(8,128)} %collective-permute-done.6.refs_3_.refs_6_, ...), custom_call_target="tpu_custom_call" | custom-call | flops 22649241600 | bytes 33685504 | tf_op jit(solution)/shard_map/pallas_call | solution.py:130
  272.1 5.2 %collective-permute-done.3.refs_2_.refs_5_ = f32[3600,128]{1,0:T(8,128)S(1)} collective-permute-done((f32[3600,128]{1,0:T(8,128)}, f32[3600,128]{1,0:T(8,128)S(1)}, u32[]{:S(2)}, u32[]{:S(2)}) %collective-permute-start.3) | collective-permute-done | bytes 1843232 | tf_op jit(solution)/shard_map/ppermute | solution.py:166
  277.3 2.5 collective-permute-done.4.refs_4_.refs_9_
  279.8 1.6 collective-permute-start.12
  283.3 15.2 %collective-permute-done.12 = f32[1800,128]{1,0:T(8,128)S(1)} collective-permute-done((f32[1800,128]{1,0:T(8,128)S(1)}, f32[1800,128]{1,0:T(8,128)S(1)}, u32[]{:S(2)}, u32[]{:S(2)}) %collective-permute-start.12) | collective-permute-done | bytes 921632 | tf_op jit(solution)/shard_map/ppermute | solution.py:166
  302.0 3.2 collective-permute-done.14.refs_7_.refs_15_
  305.2 32.9 %shard_map.33.refs_17_ = f32[3600,1920]{1,0:T(8,128)} custom-call(s32[1]{0:T(128)} %bitcast.place_ref, f32[3600,128]{1,0:T(8,128)} %shard_map.31.refs_0_.refs_1_, f32[3600,128]{1,0:T(8,128)} %collective-permute-done.9.refs_1_.refs_3_, f32[3600,128]{1,0:T(8,128)} %copy-done.2, ...), custom_call_target="tpu_custom_call", output_to_operand_aliasing={{}: (10, {})} | custom-call | flops 22649241600 | bytes 33685504 | tf_op jit(solution)/shard_map/pallas_call | solution.py:130
  338.2 44.3 %shard_map.34.refs_17_ = f32[3600,1920]{1,0:T(8,128)} custom-call(s32[1]{0:T(128)} %bitcast.place_ref, f32[3600,128]{1,0:T(8,128)} %shard_map.30.refs_0_, f32[3600,128]{1,0:T(8,128)} %shard_map.31.refs_0_.refs_1_, f32[3600,128]{1,0:T(8,128)} %collective-permute-done.5.refs_1_.refs_2_, ...), custom_call_target="tpu_custom_call", output_to_operand_aliasing={{}: (18, {})} | custom-call | flops 28311552000 | bytes 43950080 | tf_op jit(solution)/shard_map/pallas_call | solution.py:130
  382.5 19.8 %shard_map.35 = f32[3600,1920]{1,0:T(8,128)} custom-call(s32[1]{0:T(128)} %bitcast.place_ref, f32[3600,128]{1,0:T(8,128)} %shard_map.30.refs_0_, f32[3600,128]{1,0:T(8,128)} %shard_map.31.refs_0_.refs_1_, f32[3600,128]{1,0:T(8,128)} %collective-permute-done.5.refs_1_.refs_2_, ...), custom_call_target="tpu_custom_call", output_to_operand_aliasing={{}: (18, {})} | custom-call | flops 11324620800 | bytes 35274752 | tf_op jit(solution)/shard_map/pallas_call | solution.py:130
  (46 shorter events, 13.7 us)
Async XLA Ops:
  6.5 1.6 slice-start
  6.5 234.3 %all-gather.4.cloned.1.call-start = ((), (), s32[]{:S(2)}) async-start(), calls=%async_computation.2 | async-start | bytes 10485760 | tf_op jit(solution)/shard_map/all_gather | solution.py:172
  12.9 100.1 %all-to-all-start = ((f32[4,32,3600]{2,1,0:T(8,128)}), f32[4,32,3600]{2,1,0:T(8,128)S(1)}, u32[]{:S(2)}, u32[]{:S(2)}) async-start(f32[4,32,3600]{2,1,0:T(8,128)} %shard_map.29), calls=%async_computation | async-start | bytes 3801088 | tf_op jit(solution)/shard_map/all_to_all | solution.py:184
  120.1 33.7 %collective-permute-start.1 = (f32[3600,128]{1,0:T(8,128)}, f32[3600,128]{1,0:T(8,128)}, u32[]{:S(2)}, u32[]{:S(2)}) collective-permute-start(f32[3600,128]{1,0:T(8,128)} %shard_map.30.refs_0_), channel_id=1, source_target_pairs={{0,4},{1,5},{2,6},{3,7},{4,0},{5,1},{6,2},{7,3},{8,12},{9,13},{10,... | collective-permute-start | bytes 5529608 | tf_op jit(solution)/shard_map/ppermute | solution.py:166
  121.6 43.8 %collective-permute-start = (f32[3600,128]{1,0:T(8,128)}, f32[3600,128]{1,0:T(8,128)}, u32[]{:S(2)}, u32[]{:S(2)}) collective-permute-start(f32[3600,128]{1,0:T(8,128)} %shard_map.30.refs_0_), channel_id=1, source_target_pairs={{0,2},{1,3},{2,0},{3,1},{4,6},{5,7},{6,4},{7,5},{8,10},{9,11},{10,... | collective-permute-start | bytes 5529608 | tf_op jit(solution)/shard_map/ppermute | solution.py:166
  153.8 40.7 %collective-permute-start.2 = (f32[3600,128]{1,0:T(8,128)}, f32[3600,128]{1,0:T(8,128)}, u32[]{:S(2)}, u32[]{:S(2)}) collective-permute-start(f32[3600,128]{1,0:T(8,128)} %collective-permute-done.1.refs_4_.refs_8_), channel_id=1, source_target_pairs={{0,2},{1,3},{2,0},{3,1},{4,6},{5,7},{6,4},{7,5},{8,10},{9,11},{10,... | collective-permute-start | bytes 5529608 | tf_op jit(solution)/shard_map/ppermute | solution.py:166
  155.3 76.1 %all-to-all-start.1 = ((f32[4,32,3600]{2,1,0:T(8,128)}), f32[4,32,3600]{2,1,0:T(8,128)S(1)}, u32[]{:S(2)}, u32[]{:S(2)}) async-start(f32[4,32,3600]{2,1,0:T(8,128)} %shard_map.28), calls=%async_computation.1 | async-start | bytes 3801088 | tf_op jit(solution)/shard_map/all_to_all | solution.py:184
  162.2 1.3 slice-start.1
  162.2 176.0 %all-gather.8.cloned.1.call-start = ((), (), s32[]{:S(2)}) async-start(), calls=%async_computation.4 | async-start | bytes 6553600 | tf_op jit(solution)/shard_map/all_gather | solution.py:172
  164.7 217.8 %all-gather.6.cloned.1.call-start = ((), (), s32[]{:S(2)}) async-start(), calls=%async_computation.3 | async-start | bytes 2621440 | tf_op jit(solution)/shard_map/all_gather | solution.py:172
  164.8 74.5 %collective-permute-start.5 = (f32[3600,128]{1,0:T(8,128)}, f32[3600,128]{1,0:T(8,128)}, u32[]{:S(2)}, u32[]{:S(2)}) collective-permute-start(f32[3600,128]{1,0:T(8,128)} %shard_map.30.refs_0_), channel_id=1, source_target_pairs={{0,1},{1,0},{2,3},{3,2},{4,5},{5,4},{6,7},{7,6},{8,9},{9,8},{10,11... | collective-permute-start | bytes 5529608 | tf_op jit(solution)/shard_map/ppermute | solution.py:166
  164.9 76.0 %collective-permute-start.7 = (f32[3600,128]{1,0:T(8,128)}, f32[3600,128]{1,0:T(8,128)}, u32[]{:S(2)}, u32[]{:S(2)}) collective-permute-start(f32[3600,128]{1,0:T(8,128)} %collective-permute-done.1.refs_4_.refs_8_), channel_id=1, source_target_pairs={{0,1},{1,0},{2,3},{3,2},{4,5},{5,4},{6,7},{7,6},{8,9},{9,8},{10,11... | collective-permute-start | bytes 5529608 | tf_op jit(solution)/shard_map/ppermute | solution.py:166
  165.4 75.5 %collective-permute-start.6 = (f32[3600,128]{1,0:T(8,128)}, f32[3600,128]{1,0:T(8,128)}, u32[]{:S(2)}, u32[]{:S(2)}) collective-permute-start(f32[3600,128]{1,0:T(8,128)} %collective-permute-done.refs_2_.refs_4_), channel_id=1, source_target_pairs={{0,1},{1,0},{2,3},{3,2},{4,5},{5,4},{6,7},{7,6},{8,9},{9,8},{10,11... | collective-permute-start | bytes 5529608 | tf_op jit(solution)/shard_map/ppermute | solution.py:166
  194.5 46.3 %collective-permute-start.8 = (f32[3600,128]{1,0:T(8,128)}, f32[3600,128]{1,0:T(8,128)}, u32[]{:S(2)}, u32[]{:S(2)}) collective-permute-start(f32[3600,128]{1,0:T(8,128)} %collective-permute-done.2.refs_6_.refs_12_), channel_id=1, source_target_pairs={{0,1},{1,0},{2,3},{3,2},{4,5},{5,4},{6,7},{7,6},{8,9},{9,8},{10,11... | collective-permute-start | bytes 5529608 | tf_op jit(solution)/shard_map/ppermute | solution.py:166
  238.4 38.8 %collective-permute-start.3 = (f32[3600,128]{1,0:T(8,128)}, f32[3600,128]{1,0:T(8,128)S(1)}, u32[]{:S(2)}, u32[]{:S(2)}) collective-permute-start(f32[3600,128]{1,0:T(8,128)} %shard_map.31.refs_0_.refs_1_), channel_id=1, source_target_pairs={{0,2},{1,3},{2,0},{3,1},{4,6},{5,7},{6,4},{7,5},{8,10},{9,11},{10,... | collective-permute-start | bytes 5529608 | tf_op jit(solution)/shard_map/ppermute | solution.py:166
  239.3 40.4 %collective-permute-start.4 = (f32[3600,128]{1,0:T(8,128)}, f32[3600,128]{1,0:T(8,128)}, u32[]{:S(2)}, u32[]{:S(2)}) collective-permute-start(f32[3600,128]{1,0:T(8,128)} %shard_map.31.refs_0_.refs_1_), channel_id=1, source_target_pairs={{0,4},{1,5},{2,6},{3,7},{4,0},{5,1},{6,2},{7,3},{8,12},{9,13},{10,... | collective-permute-start | bytes 5529608 | tf_op jit(solution)/shard_map/ppermute | solution.py:166
  240.8 38.9 %collective-permute-start.9 = (f32[3600,128]{1,0:T(8,128)}, f32[3600,128]{1,0:T(8,128)}, u32[]{:S(2)}, u32[]{:S(2)}) collective-permute-start(f32[3600,128]{1,0:T(8,128)} %shard_map.31.refs_0_.refs_1_), channel_id=1, source_target_pairs={{0,1},{1,0},{2,3},{3,2},{4,5},{5,4},{6,7},{7,6},{8,9},{9,8},{10,11... | collective-permute-start | bytes 5529608 | tf_op jit(solution)/shard_map/ppermute | solution.py:166
  277.3 5.6 %copy-start.2 = (f32[3600,128]{1,0:T(8,128)}, f32[3600,128]{1,0:T(8,128)S(1)}, u32[]{:S(2)}) copy-start(f32[3600,128]{1,0:T(8,128)S(1)} %collective-permute-done.3.refs_2_.refs_5_) | copy-start | bytes 5529604
  279.8 18.7 %collective-permute-start.12 = (f32[1800,128]{1,0:T(8,128)S(1)}, f32[1800,128]{1,0:T(8,128)S(1)}, u32[]{:S(2)}, u32[]{:S(2)}) collective-permute-start(f32[1800,128]{1,0:T(8,128)S(1)} %slice.16), channel_id=1, source_target_pairs={{0,4},{1,5},{2,6},{3,7},{4,0},{5,1},{6,2},{7,3},{8,12},{9,13},{10,... | collective-permute-start | bytes 2764808 | tf_op jit(solution)/shard_map/ppermute | solution.py:166
  282.6 17.4 %collective-permute-start.13 = (f32[1800,128]{1,0:T(8,128)S(1)}, f32[1800,128]{1,0:T(8,128)S(1)}, u32[]{:S(2)}, u32[]{:S(2)}) collective-permute-start(f32[1800,128]{1,0:T(8,128)S(1)} %slice.17), channel_id=1, source_target_pairs={{0,2},{1,3},{2,0},{3,1},{4,6},{5,7},{6,4},{7,5},{8,10},{9,11},{10,... | collective-permute-start | bytes 2764808 | tf_op jit(solution)/shard_map/ppermute | solution.py:166
  282.8 19.2 %collective-permute-start.10 = (f32[3600,128]{1,0:T(8,128)S(1)}, f32[3600,128]{1,0:T(8,128)}, u32[]{:S(2)}, u32[]{:S(2)}) collective-permute-start(f32[3600,128]{1,0:T(8,128)S(1)} %collective-permute-done.3.refs_2_.refs_5_), channel_id=1, source_target_pairs={{0,1},{1,0},{2,3},{3,2},{4,5},{5,4},{6,7},{7,6},{8,9},{9,8},{10,11... | collective-permute-start | bytes 5529608 | tf_op jit(solution)/shard_map/ppermute | solution.py:166
  282.8 19.2 %collective-permute-start.11 = (f32[3600,128]{1,0:T(8,128)}, f32[3600,128]{1,0:T(8,128)}, u32[]{:S(2)}, u32[]{:S(2)}) collective-permute-start(f32[3600,128]{1,0:T(8,128)} %collective-permute-done.4.refs_4_.refs_9_), channel_id=1, source_target_pairs={{0,1},{1,0},{2,3},{3,2},{4,5},{5,4},{6,7},{7,6},{8,9},{9,8},{10,11... | collective-permute-start | bytes 5529608 | tf_op jit(solution)/shard_map/ppermute | solution.py:166
  299.5 1.6 slice-start.2
  301.1 4.1 %collective-permute-start.14 = (f32[3600,128]{1,0:T(8,128)}, f32[3600,128]{1,0:T(8,128)}, u32[]{:S(2)}, u32[]{:S(2)}) collective-permute-start(f32[3600,128]{1,0:T(8,128)} %constant_dynamic-update-slice_fusion.refs_6_.refs_13_), channel_id=1, source_target_pairs={{0,1},{1,0},{2,3},{3,2},{4,5},{5,4},{6,7},{7,6},{8,9},{9,8},{10,11... | collective-permute-start | bytes 5529608 | tf_op jit(solution)/shard_map/ppermute | solution.py:166
  (2 other events, 2.6 us)
Sparse Core Ops, SparseCore 0:
  9.7 224.8 all-gather.3
  236.2 98.6 all-gather.7
  336.5 44.5 all-gather.5
